TPU v7x, 32 devices: a whole 2x2x4 slice. The times are simulated.
32 devices in a mesh: dp: 8 (over z, y), tensor: 4 (over x, core).
Axes of the slice: x: 2, y: 2, z: 4, core: 2. Of those that a mesh axis runs over, the one named last changes fastest.
Arguments:
- tokens: bfloat16 [16384, 768], P(('dp', 'tensor')), may hold values from -6 to 6
- doc_lengths: int32 [32, 8], P('dp'), may hold values from 0 to 512, as said below
- qkv_weight: bfloat16 [768, 2304], P(None, 'tensor'), may hold values from -0.21875 to 0.21875
- attn_out_weight: bfloat16 [768, 768], P('tensor'), may hold values from -1.25 to 1.25
- norm1_gain: float32 [768], replicated, may hold values from 0.5 to 1.5
- norm1_bias: float32 [768], replicated, may hold values from -0.8 to 0.8
- ffn_in_weight: bfloat16 [768, 3072], P(None, 'tensor'), may hold values from -0.21875 to 0.21875
- ffn_out_weight: bfloat16 [3072, 768], P('tensor'), may hold values from -0.109375 to 0.109375
- norm2_gain: float32 [768], replicated, may hold values from 0.5 to 1.5
- norm2_bias: float32 [768], replicated, may hold values from -0.8 to 0.8
- adapter_down: bfloat16 [16, 768, 48], P(None, ('dp', 'tensor')), may hold values from -0.21875 to 0.21875
- adapter_up: bfloat16 [16, 48, 768], P(None, None, ('dp', 'tensor')), may hold values from -1.75 to 1.75
- merging_query: bfloat16 [768, 768], P(('dp', 'tensor')), may hold values from -0.4375 to 0.4375
- merging_key: bfloat16 [768, 768], P(('dp', 'tensor')), may hold values from -0.21875 to 0.21875
- merging_value: bfloat16 [768, 768], P(('dp', 'tensor')), may hold values from -0.21875 to 0.21875
- merging_gain: float32 [768], replicated, may hold values from 0.5 to 1.5
- merging_bias: float32 [768], replicated, may hold values from -0.8 to 0.8
- out_grad: bfloat16 [16384, 768], P(('dp', 'tensor')), may hold values from -6 to 6
Outputs:
- layer_out: float32 [16384, 768], P(('dp', 'tensor'))
- input_grad: float32 [16384, 768], P(('dp', 'tensor'))
- grad_query: float32 [768, 768], P(('dp', 'tensor'))
- grad_key: float32 [768, 768], P(('dp', 'tensor'))
- grad_value: float32 [768, 768], P(('dp', 'tensor'))
- grad_gain: float32 [768], replicated
- grad_bias: float32 [768], replicated
- adapter_mass: float32 [16], replicated
Inputs may be any that keep to these rules, and one draw needn't show every extreme that they name: `doc_lengths`: A row's 8 lengths, some of which may be 0, sum to at most 512; the slots past the sum are padding. Some row holds one document of 512 tokens.
All inputs are finite; a program needn't handle non-finite values.
Results may differ from a plain program's by a relative error of at most 0.04.
Values may be sent and summed in bfloat16 or wider, within the bound.
No kernel may reach another device: no remote copies, remote signals or barrier semaphores. Data moves between devices by JAX's collectives and lax.ppermute only.
A program may use at most 192 MiB of HBM per device.

v0:
```python
import functools

import jax
import jax.numpy as jnp
from jax import lax
from jax.experimental import pallas as pl
from jax.experimental.pallas import tpu as pltpu
from jax.sharding import PartitionSpec as P

HEAD_DIM = 64
AXES = ("dp", "tensor")
ATTEND_MIB, FFN_MIB, MERGE_MIB = 16, 16, 22
LANES = 128
COST = 0.0
CHUNK = 256
EPS = 1e-12
BIG_NEGATIVE = -1e30
ROOT_HALF = 0.7071067811865476
ROOT_TAU = 0.3989422804014327
F32, BF16 = jnp.float32, jnp.bfloat16

CORE, ACROSS, PAIR_Y, PAIR_Z, DEPTH, ROW = range(6)
GAIN1, SHIFT1, GAIN2, SHIFT2, GAIN3, SHIFT3 = range(6)

SMEM = pl.BlockSpec(memory_space=pltpu.SMEM)
VMEM = pl.BlockSpec(memory_space=pltpu.VMEM)
ANY = pl.BlockSpec(memory_space=pl.ANY)
HBM = pl.BlockSpec(memory_space=pltpu.HBM)


def by_chunks(count, body):
    @pl.loop(0, count // CHUNK)
    def _(i):
        body(pl.ds(pl.multiple_of(i * CHUNK, CHUNK), CHUNK))


def line_of(lines, i):
    return lines[i : i + 1]


def dot(a, b):
    return lax.dot_general(a, b, (((1,), (0,)), ((), ())), preferred_element_type=F32)


def dot_last(a, b):
    return lax.dot_general(a, b, (((1,), (1,)), ((), ())), preferred_element_type=F32)


def dot_first(a, b):
    return lax.dot_general(a, b, (((0,), (0,)), ((), ())), preferred_element_type=F32)


def normalize(u):
    centered = u - jnp.mean(u, axis=-1, keepdims=True)
    inv_std = lax.rsqrt(jnp.mean(centered * centered, axis=-1, keepdims=True) + EPS)
    return centered * inv_std, inv_std


def norm_back(grad, normed, inv_std):
    return inv_std * (
        grad
        - jnp.mean(grad, axis=-1, keepdims=True)
        - normed * jnp.mean(grad * normed, axis=-1, keepdims=True)
    )


def gelu_both(u):
    half = 0.5 * (1.0 + lax.erf(u * ROOT_HALF))
    return u * half, half + u * jnp.exp(-0.5 * u * u) * ROOT_TAU


def segment_bias(meta_ref, lengths_ref, bias_ref):
    seq = bias_ref.shape[0]
    row = meta_ref[ROW]
    by_row = lax.broadcasted_iota(jnp.int32, (seq, 1), 0)
    by_lane = lax.broadcasted_iota(jnp.int32, (1, seq), 1)
    seg_row = jnp.zeros((seq, 1), jnp.int32)
    seg_lane = jnp.zeros((1, seq), jnp.int32)
    end = jnp.int32(0)
    for i in range(lengths_ref.shape[1]):
        end = end + lengths_ref[row, i]
        seg_row = seg_row + jnp.where(by_row >= end, 1, 0)
        seg_lane = seg_lane + jnp.where(by_lane >= end, 1, 0)
    bias_ref[...] = jnp.where(seg_row == seg_lane, 0.0, BIG_NEGATIVE).astype(F32)


def attend_forward(columns, last, meta, lengths, tokens, before, lines, weight0, weight1, *refs):
    saved, first_out, bias = refs[:6], refs[6], refs[-1]
    segment_bias(meta, lengths, bias)
    total = before[...].astype(F32)
    width = 3 * HEAD_DIM
    for quarter, weight in enumerate((weight0, weight1)):
        turned = dot_last(weight[:columns], tokens[...]).astype(BF16)
        turned_out, att_out, prob_out = saved[3 * quarter : 3 * quarter + 3]
        turned_out[...] = turned

        @pl.loop(0, columns // width)
        def _(head, turned_out=turned_out, att_out=att_out, prob_out=prob_out):
            base = pl.multiple_of(head * width, width)
            queries, keys, values = (
                turned_out[pl.ds(base + i * HEAD_DIM, HEAD_DIM)] for i in range(3)
            )
            scores = dot(keys.T, queries * BF16(HEAD_DIM**-0.5)) + bias[...]
            exponent = jnp.exp(scores - jnp.max(scores, axis=0, keepdims=True))
            prob = (exponent * (1.0 / jnp.sum(exponent, axis=0, keepdims=True))).astype(BF16)
            prob_out[head] = prob
            part = pl.ds(pl.multiple_of(head * HEAD_DIM, HEAD_DIM), HEAD_DIM)
            att_out[part] = dot(values, prob).astype(BF16)

        total = total + dot(att_out[...].T, weight[columns:])
    if not last:
        first_out[...] = total
        return
    normed_out, inv_out = refs[7:9]
    normed, inv_std = normalize(total)
    normed_out[...] = normed
    inv_out[...] = inv_std
    first_out[...] = normed * line_of(lines, GAIN1) + line_of(lines, SHIFT1)


def sds(shape, dtype):
    return jax.ShapeDtypeStruct(shape, dtype)


def params(mib):
    return pltpu.CompilerParams(vmem_limit_bytes=mib << 20)


def kernel(body, deps, mib, *, in_specs, **kw):
    n = len(deps)
    call = pl.pallas_call(
        lambda *refs: body(*refs[n:]),
        in_specs=[ANY] * n + in_specs,
        compiler_params=params(mib),
        **kw,
    )
    return functools.partial(call, *deps)


def sync(name, meta, joins, carries, deps):
    sides = [j[0] if isinstance(j[0], int) else None for j in joins]
    parts = [j[1:] if isinstance(j[0], int) else j for j in joins]
    flat = [p for j in parts for p in j]

    def body(meta_ref, *refs):
        refs = refs[len(carries) :]
        sources, outs = list(refs[: len(flat)]), refs[len(flat) : len(flat) + len(parts)]
        for side, join, out in zip(sides, parts, outs):
            row = 0
            for i, part in enumerate(join):
                size = part.shape[0]
                if side is not None:
                    n = len(join) // 2
                    row = pl.multiple_of(((meta_ref[side] ^ (i // n)) * n + i % n) * size, 16)
                out[pl.ds(row, size)] = sources.pop(0)[...]
                row = row + size

    joined = [sds((sum(p.shape[0] for p in j), *j[0].shape[1:]), j[0].dtype) for j in parts]
    n_deps = len(deps)
    out = kernel(
        body,
        deps,
        16,
        in_specs=[SMEM] + [ANY] * len(carries) + [VMEM] * len(flat),
        out_specs=[VMEM] * len(joined) + [ANY] * len(carries),
        out_shape=joined + [sds(c.shape, c.dtype) for c in carries],
        input_output_aliases={n_deps + 1 + i: len(joined) + i for i in range(len(carries))},
        cost_estimate=cost(0),
        name=name,
    )(meta, *carries, *flat)
    return out


def in_hbm(array):
    return pltpu.with_memory_space_constraint(array, pltpu.HBM)


def cost(us):
    return pl.CostEstimate(flops=int(us * 1.1e9 * COST), bytes_accessed=1024, transcendentals=0)


def call_attend_forward(deps, columns, last, meta, lengths, tokens, before, lines, quarters):
    seq, width = tokens.shape
    heads = columns // (3 * HEAD_DIM)
    inner = heads * HEAD_DIM
    square, narrow = sds((seq, width), F32), sds((seq, 1), F32)
    out_shape = [
        pltpu.HBM((columns, seq), BF16),
        pltpu.HBM((inner, seq), BF16),
        pltpu.HBM((heads, seq, seq), BF16),
    ] * 2 + [square] + [square, narrow] * last
    return kernel(
        functools.partial(attend_forward, columns, last),
        deps,
        ATTEND_MIB,
        in_specs=[SMEM, SMEM] + [VMEM] * 5,
        out_specs=[VMEM] * len(out_shape),
        out_shape=out_shape,
        scratch_shapes=[pltpu.VMEM((seq, seq), F32)],
        cost_estimate=cost(8),
        name="attend_forward",
    )(meta, lengths, tokens, before, lines, *quarters)


def ffn_forward(blocks, first, before, *refs):
    slope_out, sum_out = refs[-2:]

    def chunk(rows):
        low = first[rows].astype(BF16)
        total = before[rows]
        outs = list(refs[2:-2])
        for quarter in range(2):
            value, slope = gelu_both(dot(low, refs[quarter][...]))
            slope_out[quarter, rows] = slope.astype(BF16)
            value = value.astype(BF16)
            start = 0
            for _ in range(blocks):
                out = outs.pop(0)
                total = total + dot(value[:, start : start + out.shape[0]], out[...])
                start += out.shape[0]
        sum_out[rows] = total

    by_chunks(first.shape[0], chunk)


def call_ffn_forward(deps, first, before, in_quarters, out_quarters):
    seq, width = first.shape
    hidden = in_quarters[0].shape[1]
    return kernel(
        functools.partial(ffn_forward, len(out_quarters) // 2),
        deps,
        FFN_MIB,
        in_specs=[VMEM] * (4 + len(out_quarters)),
        out_specs=[VMEM] * 2,
        out_shape=[sds((2, seq, hidden), BF16), sds((seq, width), F32)],
        cost_estimate=cost(5),
        name="ffn_forward",
    )(first, before, *in_quarters, *out_quarters)


def assemble(name, meta, weights, tiles):
    n_mats = tiles[0][0].shape[0] // (2 * len(tiles[0][1]))
    rows, half = tiles[0][0].shape[1:]
    count = sum(2 * len(parts) for _, parts, _ in tiles)
    before = [] if weights is None else [weights]

    def body(meta_ref, *refs):
        refs = refs[len(before) :]
        out, sems = refs[-2:]
        copies = []
        for ref, (_, parts, core_rel) in zip(refs, tiles):
            side = pl.multiple_of((meta_ref[CORE] ^ core_rel) * half, LANES)
            for j, (y_rel, z_rel) in enumerate(parts):
                for x_rel in range(2):
                    chip = ((meta_ref[DEPTH] ^ z_rel) * 2 + (meta_ref[PAIR_Y] ^ y_rel)) * 2
                    chip = chip + (meta_ref[ACROSS] ^ x_rel)
                    first = pl.multiple_of(chip * rows, 16)
                    target = out.at[:, pl.ds(first, rows), pl.ds(side, half)]
                    source = ref.at[pl.ds((2 * j + x_rel) * n_mats, n_mats)]
                    copies.append(pltpu.make_async_copy(source, target, sems.at[len(copies)]))
        for copy in copies:
            copy.start()
        for copy in copies:
            copy.wait()

    return kernel(
        body,
        [],
        16,
        in_specs=[SMEM] + [ANY] * len(before) + [VMEM] * len(tiles),
        out_specs=ANY,
        out_shape=sds((n_mats, 2 * half, 2 * half), BF16),
        input_output_aliases={1: 0} if before else {},
        scratch_shapes=[pltpu.SemaphoreType.DMA((count,))],
        cost_estimate=cost(0),
        name=name,
    )(meta, *before, *(tile for tile, _, _ in tiles))


def split_lines(total):
    high = total.astype(BF16).astype(F32)
    return jnp.concatenate([high, total - high], axis=0)


def merging(n_adapters, meta, lengths, sums, lines, out_grad, matrices, *refs):
    layer_out, part_out, fquery_out, middle_out, keep_out, send_out = refs[:6]
    grads, sum_lines, states, probes, blends, values, fqueries = refs[6:]
    seq, width = sums.shape
    scale = width**-0.5
    down, up, query, key, value = (matrices.at[i] for i in range(5))
    gain2, shift2 = line_of(lines, GAIN2), line_of(lines, SHIFT2)
    gain3, shift3 = line_of(lines, GAIN3), line_of(lines, SHIFT3)
    spread = jnp.where(
        lax.broadcasted_iota(jnp.int32, (LANES, width), 0)
        == lax.broadcasted_iota(jnp.int32, (LANES, width), 1) // (width // n_adapters),
        1.0,
        0.0,
    ).astype(BF16)
    lane = lax.broadcasted_iota(jnp.int32, (1, LANES), 1)
    count = jnp.int32(0)
    for i in range(lengths.shape[1]):
        count = count + lengths[meta[ROW], i]
    sum_lines[...] = jnp.zeros_like(sum_lines)

    def by_adapter(terms):
        high = terms.astype(BF16)
        rest = (terms - high.astype(F32)).astype(BF16)
        return dot_last(high, spread) + dot_last(rest, spread)

    def chunk(rows):
        normed2, _ = normalize(sums[rows])
        second = normed2 * gain2 + shift2
        second_low = second.astype(BF16)
        states[rows] = second_low
        act, slope = (v.astype(BF16) for v in gelu_both(dot(second_low, down[...])))
        fquery = dot(second_low, query[...]).astype(BF16)
        fqueries[rows] = fquery
        probe = dot_last(fquery, key[...]).astype(BF16)
        probe_up = dot(probe, up[...])
        logits = scale * (
            jnp.sum(probe.astype(F32) * second, axis=1, keepdims=True)
            + by_adapter(act * probe_up)
        )
        logits = jnp.where(lane < n_adapters, logits, BIG_NEGATIVE)
        exponent = jnp.exp(logits - jnp.max(logits, axis=1, keepdims=True))
        mix = exponent / jnp.sum(exponent, axis=1, keepdims=True)
        mix_low = mix.astype(BF16)
        mix_sum = jnp.sum(mix_low.astype(F32), axis=1, keepdims=True)
        mix_wide = dot(mix_low, spread).astype(BF16)
        blended = second * mix_sum + dot_last((mix_wide * act).astype(BF16), up[...])
        blended = blended.astype(BF16)
        blends[rows] = blended
        normed3, inv_std3 = normalize(second + dot(blended, value[...]))
        layer_out[rows] = normed3 * gain3 + shift3

        token = rows.start + lax.broadcasted_iota(jnp.int32, (CHUNK, 1), 0)
        keep = jnp.where(token < count, 1.0, 0.0)
        cot = out_grad[rows].astype(F32) * keep
        mass = jnp.sum(mix * keep, axis=0, keepdims=True)
        mass = jnp.where(lane == n_adapters, jnp.sum(keep), mass)
        sum_lines[0:1] += jnp.sum(cot * normed3, axis=0, keepdims=True)
        sum_lines[1:2] += jnp.sum(cot, axis=0, keepdims=True)
        sum_lines[2:3, :LANES] += mass

        grad_pre = norm_back(cot * gain3, normed3, inv_std3)
        grad_proj = grad_pre.astype(BF16)
        values[rows] = grad_proj
        grad_blend = dot_last(grad_proj, value[...]).astype(BF16)
        blend_up = dot(grad_blend, up[...])
        grad_mix = jnp.sum(
            grad_blend.astype(F32) * second, axis=1, keepdims=True
        ) + by_adapter(act * blend_up)
        grad_logits = mix * (grad_mix - jnp.sum(grad_mix * mix, axis=1, keepdims=True))
        grad_logits = grad_logits.astype(BF16)
        logit_sum = jnp.sum(grad_logits.astype(F32), axis=1, keepdims=True)
        logit_wide = dot(grad_logits, spread).astype(BF16)
        grad_probe = second * logit_sum + dot_last((logit_wide * act).astype(BF16), up[...])
        grad_probe = (scale * grad_probe).astype(BF16)
        probes[rows] = grad_probe
        fquery_out[rows] = dot(grad_probe, key[...]).astype(BF16)
        grad_act = mix_wide.astype(F32) * blend_up + (scale * logit_wide.astype(F32)) * probe_up
        middle_out[rows] = (grad_act * slope.astype(F32)).astype(BF16)
        part_out[rows] = (
            grad_pre + grad_blend.astype(F32) * mix_sum + probe.astype(F32) * (scale * logit_sum)
        )

    by_chunks(seq, chunk)
    grads[0] = dot_first(states[...], fquery_out[...])
    grads[1] = dot_first(probes[...], fqueries[...])
    grads[2] = dot_first(blends[...], values[...])
    tail = split_lines(sum_lines[0:4])
    rows = width // 32

    @pl.loop(0, 16)
    def _(chip):
        z_rel = (chip // 4) ^ meta[DEPTH]
        y_rel = (chip // 2 % 2) ^ meta[PAIR_Y]
        x_rel = (chip % 2) ^ meta[ACROSS]
        for core_rel, out in ((0, keep_out), (1, send_out)):
            first = pl.multiple_of((chip * 2 + (meta[CORE] ^ core_rel)) * rows, 8)
            block = [grads[i, pl.ds(first, rows)] for i in range(3)] + [tail]
            out[x_rel, y_rel, z_rel] = jnp.concatenate(block, axis=0).astype(BF16)


def call_merging(n_adapters, meta, lengths, sums, lines, out_grad, matrices):
    seq, width = sums.shape
    block = 3 * width // 32 + 8
    return pl.pallas_call(
        functools.partial(merging, n_adapters),
        in_specs=[SMEM, SMEM] + [VMEM] * 4,
        out_specs=[VMEM] * 6,
        out_shape=[sds((seq, width), F32)] * 2
        + [sds((seq, width), BF16)] * 2
        + [sds((2, 2, 4, block, width), BF16)] * 2,
        scratch_shapes=[pltpu.VMEM((3, width, width), F32), pltpu.VMEM((8, width), F32)]
        + [pltpu.VMEM((seq, width), BF16)] * 5,
        compiler_params=params(MERGE_MIB),
        cost_estimate=cost(18),
        name="merging",
    )(meta, lengths, sums, lines, out_grad, matrices)


def merging_input(sums, lines, part, grad_fquery, grad_middle, matrices, grad_out, grad_low_out):
    def chunk(rows):
        normed, inv_std = normalize(sums[rows])
        grad = part[rows] + dot_last(grad_fquery[rows], matrices[2])
        grad = grad + dot_last(grad_middle[rows], matrices[0])
        grad = norm_back(grad * line_of(lines, GAIN2), normed, inv_std)
        grad_out[rows] = grad
        grad_low_out[rows] = grad.astype(BF16)

    by_chunks(part.shape[0], chunk)


def call_merging_input(deps, sums, lines, part, grad_fquery, grad_middle, matrices):
    return kernel(
        merging_input,
        deps,
        FFN_MIB,
        in_specs=[VMEM] * 6,
        out_specs=[VMEM] * 2,
        out_shape=[sds(part.shape, F32), sds(part.shape, BF16)],
        cost_estimate=cost(3),
        name="merging_input",
    )(sums, lines, part, grad_fquery, grad_middle, matrices)


def ffn_backward(last, blocks, grad_low, before, slope, in0, in1, *refs):
    all_outs, refs = refs[: 2 * blocks], refs[2 * blocks :]

    def chunk(rows):
        low = grad_low[rows]
        total = before[rows]
        outs = list(all_outs)
        for quarter, into in enumerate((in0, in1)):
            grad_act = [dot_last(low, outs.pop(0)[...]) for _ in range(blocks)]
            grad_act = grad_act[0] if blocks == 1 else jnp.concatenate(grad_act, axis=1)
            grad_pre = (grad_act * slope[quarter, rows].astype(F32)).astype(BF16)
            total = total + dot_last(grad_pre, into[...])
        if not last:
            refs[0][rows] = total
            return
        normed1, inv_std1, lines, grad_out, grad_low_out = refs
        grad = norm_back(total * line_of(lines, GAIN1), normed1[rows], inv_std1[rows])
        grad_out[rows] = grad
        grad_low_out[rows] = grad.astype(BF16)

    by_chunks(before.shape[0], chunk)


def call_ffn_backward(deps, grad_low, before, slope, in_quarters, out_quarters, *for_norm):
    seq, width = before.shape
    last = bool(for_norm)
    return kernel(
        functools.partial(ffn_backward, last, len(out_quarters) // 2),
        deps,
        FFN_MIB,
        in_specs=[VMEM] * (5 + len(out_quarters) + len(for_norm)),
        out_specs=[VMEM] * (1 + last),
        out_shape=[sds((seq, width), F32)] + [sds((seq, width), BF16)] * last,
        cost_estimate=cost(5),
        name="ffn_backward",
    )(grad_low, before, slope, *in_quarters, *out_quarters, *for_norm)


def attend_backward(
    columns, grad_low, before, turned_ref, att_ref, prob_ref, weight, input_grad, token, grad_turned, grad_att
):
    width = 3 * HEAD_DIM
    root = HEAD_DIM**-0.5
    grad_att[...] = dot_last(weight[columns:], grad_low[...]).astype(BF16)

    @pl.loop(0, columns // width)
    def _(head):
        base = pl.multiple_of(head * width, width)
        places = [pl.ds(base + i * HEAD_DIM, HEAD_DIM) for i in range(3)]
        queries, keys, values = (turned_ref[place] for place in places)
        part = pl.ds(pl.multiple_of(head * HEAD_DIM, HEAD_DIM), HEAD_DIM)
        grad = grad_att[part]
        prob = prob_ref[head]
        row_dot = jnp.sum(grad.astype(F32) * att_ref[part].astype(F32), axis=0, keepdims=True)
        grad_scores = (prob.astype(F32) * (dot(values.T, grad) - row_dot)).astype(BF16)
        grad_turned[places[0]] = (dot(keys, grad_scores) * root).astype(BF16)
        grad_turned[places[1]] = (dot_last(queries, grad_scores) * root).astype(BF16)
        grad_turned[places[2]] = dot_last(grad, prob).astype(BF16)

    input_grad[...] = before[...] + dot(grad_turned[...].T, weight[:columns])
    token[...] = jnp.zeros_like(token)


def call_attend_backward(deps, columns, grad_low, before, saved, quarter):
    seq, width = before.shape
    inner = columns // 3
    return kernel(
        functools.partial(attend_backward, columns),
        deps,
        ATTEND_MIB,
        in_specs=[VMEM] * 6,
        out_specs=[VMEM] * 2,
        out_shape=[sds((seq, width), F32), sds((8, LANES), F32)],
        scratch_shapes=[pltpu.VMEM((columns, seq), BF16), pltpu.VMEM((inner, seq), BF16)],
        cost_estimate=cost(8),
        name="attend_backward",
    )(grad_low, before, *saved, quarter)


def prepare(meta, down, up, query, key, value, g1, s1, g2, s2, g3, s3, keep, send, lines, shard):
    n_adapters, _, rank = down.shape
    for i in range(n_adapters):
        shard[0, :, i * rank : (i + 1) * rank] = down[i].astype(F32)
        shard[1, :, i * rank : (i + 1) * rank] = up[i].astype(F32)
    for i, ref in enumerate((query, key, value)):
        shard[2 + i] = ref[...].astype(F32)
    half = keep.shape[2]
    mine = pl.multiple_of(meta[CORE] * half, LANES)
    other = pl.multiple_of((1 - meta[CORE]) * half, LANES)
    keep[...] = shard[:, :, pl.ds(mine, half)].astype(BF16)
    send[...] = shard[:, :, pl.ds(other, half)].astype(BF16)
    for i, ref in enumerate((g1, s1, g2, s2, g3, s3)):
        lines[i : i + 1] = ref[...].reshape(1, -1)
    lines[6:8] = jnp.zeros((2, lines.shape[1]), F32)


def call_prepare(meta, down, up, query, key, value, *vectors):
    rows, width = query.shape
    half = sds((5, rows, width // 2), BF16)
    return pl.pallas_call(
        prepare,
        in_specs=[SMEM] + [VMEM] * 11,
        out_specs=[VMEM] * 3,
        out_shape=[half, half, sds((8, width), F32)],
        scratch_shapes=[pltpu.VMEM((5, rows, width), F32)],
        compiler_params=params(16),
        cost_estimate=cost(1),
        name="prepare",
    )(meta, *(in_hbm(a) for a in (down, up, query, key, value, *vectors)))


def prepare_frozen(meta, qkv_turned, attn_out, into, attn, attn_half, in_half):
    columns = qkv_turned.shape[0]
    attn[:columns] = qkv_turned[...]
    attn[columns:] = attn_out[...]
    for entry, whole, half in ((PAIR_Y, attn, attn_half), (PAIR_Z, into, in_half)):
        rows = half.shape[0]
        half[...] = whole[pl.ds(pl.multiple_of(meta[entry] * rows, 16), rows)]


def call_prepare_frozen(meta, qkv_turned, attn_out, into):
    rows, width = qkv_turned.shape[0] + attn_out.shape[0], attn_out.shape[1]
    return kernel(
        prepare_frozen,
        [],
        16,
        in_specs=[SMEM] + [VMEM] * 3,
        out_specs=[VMEM] * 3,
        out_shape=[
            sds((rows, width), BF16),
            sds((rows // 2, width), BF16),
            sds((into.shape[0] // 2, into.shape[1]), BF16),
        ],
        cost_estimate=cost(1),
        name="prepare_frozen",
    )(meta, *(in_hbm(a) for a in (qkv_turned, attn_out, into)))


def chip_tile(meta, keep, got, tile):
    mine, other = keep[...].astype(F32), got[...].astype(F32)
    lower = jnp.where(meta[CORE] == 0, mine, other)
    upper = jnp.where(meta[CORE] == 0, other, mine)
    tile[...] = jnp.concatenate([lower, upper], axis=1).astype(BF16)


def call_chip_tile(meta, keep, got):
    n_mats, rows, half = keep.shape
    return kernel(
        chip_tile,
        [],
        16,
        in_specs=[SMEM] + [VMEM] * 2,
        out_specs=VMEM,
        out_shape=sds((n_mats, 2 * rows, half), BF16),
        cost_estimate=cost(1),
        name="chip_tile",
    )(meta, keep, got)


def add_blocks(*blocks):
    total = functools.reduce(jnp.add, (b.astype(F32) for b in blocks))
    tail = total[-8:-4] + total[-4:]
    return jnp.concatenate([total[:-8], split_lines(tail)], axis=0)


def sum_cores(keep, got, p_keep, p_send, q_keep, q_send):
    half = p_keep.shape[-1]
    for x in range(2):
        for y in range(2):

            @pl.loop(0, 4)
            def _(z, x=x, y=y):
                total = add_blocks(keep[x, y, z], got[x, y, z]).astype(BF16)
                (p_send if x else p_keep)[y, z] = total[:, :half]
                (q_send if y else q_keep)[x, z] = total[:, half:]


def sum_first(p_keep, p_got, q_keep, q_got, p2_keep, p2_send, q2_keep, q2_send):
    @pl.loop(0, 4)
    def _(z):
        for out, index in ((p2_keep, 0), (p2_send, 1)):
            out[z] = add_blocks(p_keep[index, z], p_got[index, z]).astype(BF16)
        for out, index in ((q2_keep, 0), (q2_send, 1)):
            out[z] = add_blocks(q_keep[index, z], q_got[index, z]).astype(BF16)


def sum_second(p_keep, p_got, q_keep, q_got, *outs):
    half = p_keep.shape[-1]
    for z in range(4):
        outs[z][:, :half] = add_blocks(p_keep[z], p_got[z]).astype(BF16)
        outs[z][:, half:] = add_blocks(q_keep[z], q_got[z]).astype(BF16)


def sum_last(n_adapters, keep, got1, got2, got3, query, key, value, gain, bias, mass):
    total = add_blocks(keep[...], got1[...], got2[...], got3[...])
    rows = query.shape[0]
    for i, out in enumerate((query, key, value)):
        out[...] = total[i * rows : (i + 1) * rows]
    lines = total[-8:-4] + total[-4:]
    gain[...] = lines[0]
    bias[...] = lines[1]
    mass[...] = lines[2, :n_adapters] / lines[2:3, n_adapters : n_adapters + 1].reshape(1)


def small_call(body, name, out_shape, dep, *operands):
    return kernel(
        body,
        (dep,),
        16,
        in_specs=[VMEM] * len(operands),
        out_specs=[VMEM] * len(out_shape),
        out_shape=out_shape,
        cost_estimate=cost(1),
        name=name,
    )(*operands)


def sum_gradients(hops, keep, send, n_adapters, works):
    block, width = keep.shape[3:]
    half = width // 2
    pair = [sds((2, 4, block, half), BF16)] * 4
    single = [sds((4, block, half), BF16)] * 4
    got = hops.flip(send, 1)
    dep = works[0](())
    pk, ps, qk, qs = small_call(sum_cores, "sum_cores", pair, dep, keep, got)
    pg, qg = hops.flip(ps, ALONG_X), hops.flip(qs, ALONG_Y)
    dep = works[1]([pk])
    pk, ps, qk, qs = small_call(sum_first, "sum_first", single, dep, pk, pg, qk, qg)
    pg, qg = hops.flip(ps, ALONG_Y), hops.flip(qs, ALONG_X)
    dep = works[2]([pk])
    parts = small_call(
        sum_second, "sum_second", [sds((block, width), BF16)] * 4, dep, pk, pg, qk, qg
    )
    got = [hops.flip(part, z * ALONG_Z) for z, part in enumerate(parts) if z]
    dep = works[3]([parts[0]])
    rows = (block - 8) // 3
    outs = [sds((rows, width), F32)] * 3 + [sds((width,), F32)] * 2 + [sds((n_adapters,), F32)]
    last = functools.partial(sum_last, n_adapters)
    return small_call(last, "sum_last", outs, dep, parts[0], *got)


ALONG_X, ALONG_Y, ALONG_Z = 2, 4, 8


class Hops:
    def __init__(self, mesh):
        self.count = mesh.size
        self.tiled = mesh.shape["dp"] == 8 and mesh.shape["tensor"] == 4

    def flip(self, array, bits):
        return lax.ppermute(array, AXES, [(i, i ^ bits) for i in range(self.count)])


def half_of(block, parity):
    half = block.shape[0] // 2
    return lax.dynamic_slice_in_dim(block, parity * half, half, 0)


def plain_schedule(
    meta, doc_lengths, tokens, out_grad, lines, columns, n_adapters, attn, into, out, shard
):
    attn, into, out = (lax.all_gather(w, "tensor", axis=0) for w in (attn, into, out))
    weights = lax.all_gather(shard, AXES, axis=1, tiled=True)
    pairs = [slice(i, i + 2) for i in range(0, attn.shape[0], 2)]
    before, saved, slopes = tokens, [], []
    for pair in pairs:
        last = pair is pairs[-1]
        results = call_attend_forward(
            [], columns, last, meta, doc_lengths, tokens, before, lines, tuple(attn[pair])
        )
        saved += [results[:3], results[3:6]]
        before = results[6]
    first, normed1, inv_std1 = results[6:]
    sums = first
    for pair in pairs:
        slope, sums = call_ffn_forward([], first, sums, tuple(into[pair]), tuple(out[pair]))
        slopes.append(slope)
    layer_out, *parts, keep, send = call_merging(
        n_adapters, meta, doc_lengths, sums, lines, out_grad, weights
    )
    total, low = call_merging_input([], sums, lines, *parts, weights)
    width = tokens.shape[1]
    blocks = jnp.transpose(jnp.stack([keep, send]), (3, 2, 1, 0, 4, 5)).reshape(32, -1, width)
    squares = blocks[:, :-8].reshape(32, 3, width // 32, width)
    squares = jnp.transpose(squares, (1, 0, 2, 3)).reshape(3, width, width).astype(F32)
    squares = lax.psum_scatter(squares, AXES, scatter_dimension=1, tiled=True)
    tail = blocks[0, -8:].astype(F32)
    totals = lax.psum(tail[:4] + tail[4:], AXES)
    for pair, slope in zip(pairs, slopes):
        for_norm = (normed1, inv_std1, lines) if pair is pairs[-1] else ()
        total, *rest = call_ffn_backward(
            [], low, total, slope, tuple(into[pair]), tuple(out[pair]), *for_norm
        )
    (low,) = rest
    for quarter, kept in zip(attn, saved):
        total, _ = call_attend_backward([], columns, low, total, kept, quarter)
    mass = totals[2, :n_adapters] / totals[2, n_adapters]
    return (layer_out, total, squares[0], squares[1], squares[2], totals[0], totals[1], mass)


def per_device(
    hops,
    tokens,
    doc_lengths,
    qkv_weight,
    attn_out_weight,
    norm1_gain,
    norm1_bias,
    ffn_in_weight,
    ffn_out_weight,
    norm2_gain,
    norm2_bias,
    adapter_down,
    adapter_up,
    merging_query,
    merging_key,
    merging_value,
    merging_gain,
    merging_bias,
    out_grad,
):
    n_adapters, rows, rank = adapter_down.shape
    columns = qkv_weight.shape[1]
    tensor, dp = lax.axis_index("tensor"), lax.axis_index("dp")
    pair_y, pair_z = dp % 2, dp // 2 % 2
    meta = jnp.stack([tensor % 2, tensor // 2, pair_y, pair_z, dp // 2, tensor]).astype(jnp.int32)
    flip = hops.flip
    if not hops.tiled:
        meta = meta * (jnp.arange(meta.shape[0]) == ROW)

    keep, send, lines = call_prepare(
        meta,
        adapter_down,
        jnp.transpose(adapter_up, (0, 2, 1)),
        merging_query,
        merging_key,
        merging_value,
        norm1_gain,
        norm1_bias,
        norm2_gain,
        norm2_bias,
        merging_gain,
        merging_bias,
    )
    attn, attn_half, in_half = call_prepare_frozen(
        meta, qkv_weight.T, attn_out_weight, ffn_in_weight
    )
    if not hops.tiled:
        shard = jnp.concatenate([keep, send], axis=2)
        return plain_schedule(
            meta, doc_lengths, tokens, out_grad, lines, columns, n_adapters, attn, ffn_in_weight, ffn_out_weight, shard
        )
    cut = ffn_out_weight.shape[0] // 3
    out_a, out_b = ffn_out_weight[:cut], ffn_out_weight[cut:]
    attn_core = flip(attn, 1)
    in_core, out_core = flip(ffn_in_weight, 1), flip(ffn_out_weight, 1)
    tile = call_chip_tile(meta, keep, flip(send, 1))
    tile_x = flip(tile, ALONG_X)
    both, attn_half = sync("phase1", meta, [[tile, tile_x]], [attn_half], [attn_core])
    z2, attn_x, y0 = flip(both, 2 * ALONG_Z), flip(attn_half, ALONG_X), flip(both, ALONG_Y)
    saved_near = call_attend_forward(
        [both], columns, False, meta, doc_lengths, tokens, tokens, lines, (attn, attn_core)
    )
    joined, in_half, out_a, attn_x, y0, z2 = sync(
        "phase2", meta, [[both, z2]], [in_half, out_a, attn_x, y0, z2], [saved_near[6]]
    )
    attn_y, z1, in_x = flip(attn_x, ALONG_Y), flip(joined, ALONG_Z), flip(in_half, ALONG_X)
    y2, out_ax = flip(z2, ALONG_Y), flip(out_a, ALONG_X)
    joined_c, y0_c = flip(joined, 1), flip(y0, 1)
    attn_far, in_x, out_ax, out_b, z1, y2 = sync(
        "phase3",
        meta,
        [[PAIR_Y, attn_x, attn_y]],
        [in_x, out_ax, out_b, z1, y2],
        [in_core, out_core, joined_c, y0_c],
    )
    attn_far_c = flip(attn_far, 1)
    y1, out_bx, in_z = flip(z1, ALONG_Y), flip(out_b, ALONG_X), flip(in_x, ALONG_Z)
    z1_c, y2_c, out_ax_c = flip(z1, 1), flip(y2, 1), flip(out_ax, 1)
    *saved_far, first, normed1, inv_std1 = call_attend_forward(
        [], columns, True, meta, doc_lengths, tokens, saved_near[6], lines, (attn_far, attn_far_c)
    )
    slope_near, sums = call_ffn_forward(
        [], first, first, (ffn_in_weight, in_core), (ffn_out_weight, out_core)
    )
    own, other = 0, 1
    weights = assemble(
        "assemble",
        meta,
        None,
        [
            (joined, ((0, 0), (0, 2)), own),
            (joined_c, ((0, 0), (0, 2)), other),
            (z1, ((0, 1), (0, 3)), own),
            (z1_c, ((0, 1), (0, 3)), other),
            (y0, ((1, 0),), own),
            (y0_c, ((1, 0),), other),
            (y2, ((1, 2),), own),
            (y2_c, ((1, 2),), other),
        ],
    )
    in_far, out_bx, y1 = sync(
        "phase4", meta, [[PAIR_Z, in_x, in_z]], [out_bx, y1], [sums, weights, out_ax_c]
    )
    in_far_c, out_bx_c, y1_c = flip(in_far, 1), flip(out_bx, 1), flip(y1, 1)
    out_far = (out_ax, out_bx, out_ax_c, out_bx_c)
    slope_far, sums = call_ffn_forward([], first, sums, (in_far, in_far_c), out_far)
    last_parts = ((1, 1), (1, 3))
    weights = assemble(
        "assemble_last", meta, weights, [(y1, last_parts, own), (y1_c, last_parts, other)]
    )
    layer_out, *parts, grad_keep, grad_send = call_merging(
        n_adapters, meta, doc_lengths, sums, lines, out_grad, weights
    )
    done = {}
    attn_quarters = (attn, attn_core, attn_far, attn_far_c)
    saved = (saved_near[:3], saved_near[3:6], saved_far[:3], saved_far[3:6])

    def attention(deps, *quarters):
        for i in quarters:
            done["sum"], token = call_attend_backward(
                deps, columns, done["low"], done["sum"], saved[i], attn_quarters[i]
            )
        return token

    def first_work(deps):
        grad, low = call_merging_input(deps, sums, lines, *parts, weights)
        done["low"] = low
        (done["sum"],) = call_ffn_backward(
            [], low, grad, slope_near, (ffn_in_weight, in_core), (ffn_out_weight, out_core)
        )
        return done["sum"]

    def second_work(deps):
        done["sum"], done["low"] = call_ffn_backward(
            deps,
            done["low"],
            done["sum"],
            slope_far,
            (in_far, in_far_c),
            out_far,
            normed1,
            inv_std1,
            lines,
        )
        return attention([], 0)

    works = (
        first_work,
        second_work,
        lambda deps: attention(deps, 1),
        lambda deps: attention(deps, 2, 3),
    )
    summed = sum_gradients(hops, grad_keep, grad_send, n_adapters, works)
    return (layer_out, done["sum"], *summed)


def solution(mesh):
    split = P(AXES, None)
    in_specs = (
        split,
        P("dp", None),
        P(None, "tensor"),
        P("tensor", None),
        P(),
        P(),
        P(None, "tensor"),
        P("tensor", None),
        P(),
        P(),
        P(None, AXES, None),
        P(None, None, AXES),
        split,
        split,
        split,
        P(),
        P(),
        split,
    )
    out_specs = (split, split, split, split, split, P(), P(), P())
    return jax.shard_map(
        functools.partial(per_device, Hops(mesh)),
        mesh=mesh,
        in_specs=in_specs,
        out_specs=out_specs,
        check_vma=False,
    )
```

profile of v0, /device:TPU:0, one launch (start us, length us, event | category | flops | bytes accessed | tf_op | source)
XLA Modules:
  0.0 154.4 jit_solution(13719157357669143296)
XLA Ops:
  0.8 1.9 %prepare_frozen.1 = (bf16[768,768]{1,0:T(8,128)(2,1)S(1)}, bf16[384,768]{1,0:T(8,128)(2,1)S(1)}, bf16[384,768]{1,0:T(8,128)(2,1)S(1)}) custom-call(s32[6]{0:T(128)S(1)} %stack.27.refs_0_.meta.refs_1_.refs_4_.refs_3_, bf16[576,768]{1,0:T(8,128)(2,1)} %bitcast.8, bf16[192,768]{1,0:T(8,128)(2,1)} %refs_2_.4, bf16[768,768]{1,0:T(8,128)(2,1)} %refs_3_.5), custom_call_target="tpu_custom_call" | custom-call | bytes 1024 | tf_op jit(solution)/shard_map/prepare_frozen/pallas_call | solution.py:550
  5.1 2.5 %collective-permute-done.1.refs_2_ = bf16[5,24,384]{2,1,0:T(8,128)(2,1)S(1)} collective-permute-done((bf16[5,24,384]{2,1,0:T(8,128)(2,1)S(1)}, bf16[5,24,384]{2,1,0:T(8,128)(2,1)S(1)}, u32[]{:S(2)}, u32[]{:S(2)}) %collective-permute-start.1) | collective-permute-done | bytes 92192 | tf_op jit(solution)/shard_map/ppermute | solution.py:678
  8.1 2.9 %collective-permute-start.2 = (bf16[5,48,384]{2,1,0:T(8,128)(2,1)S(1)}, bf16[5,48,384]{2,1,0:T(8,128)(2,1)S(1)}, u32[]{:S(2)}, u32[]{:S(2)}) collective-permute-start(bf16[5,48,384]{2,1,0:T(8,128)(2,1)S(1)} %chip_tile.1.refs_3_), channel_id=1, source_target_pairs={{0,2},{1,3},{2,0},{3,1},{4,6},{5,7},{6,4},{7,5},{8,10},{9,11},{10,... | collective-permute-start | bytes 552968 | tf_op jit(solution)/shard_map/ppermute | solution.py:678
  11.0 4.9 %collective-permute-done.2.refs_4_ = bf16[5,48,384]{2,1,0:T(8,128)(2,1)S(1)} collective-permute-done((bf16[5,48,384]{2,1,0:T(8,128)(2,1)S(1)}, bf16[5,48,384]{2,1,0:T(8,128)(2,1)S(1)}, u32[]{:S(2)}, u32[]{:S(2)}) %collective-permute-start.2) | collective-permute-done | bytes 184352 | tf_op jit(solution)/shard_map/ppermute | solution.py:678
  18.4 2.6 %collective-permute-start.7 = (bf16[10,48,384]{2,1,0:T(8,128)(2,1)S(1)}, bf16[10,48,384]{2,1,0:T(8,128)(2,1)S(1)}, u32[]{:S(2)}, u32[]{:S(2)}) collective-permute-start(bf16[10,48,384]{2,1,0:T(8,128)(2,1)S(1)} %get-tuple-element.90.refs_0_.refs_7_), channel_id=1, source_target_pairs={{0,16},{1,17},{2,18},{3,19},{4,20},{5,21},{6,22},{7,23},{8,24},{9,... | collective-permute-start | bytes 1105928 | tf_op jit(solution)/shard_map/ppermute | solution.py:678
  22.5 8.9 %attend_forward.2 = (bf16[576,512]{1,0:T(8,128)(2,1)}, bf16[192,512]{1,0:T(8,128)(2,1)}, bf16[3,512,512]{2,1,0:T(8,128)(2,1)}, bf16[576,512]{1,0:T(8,128)(2,1)},...) custom-call(bf16[10,48,384]{2,1,0:T(8,128)(2,1)S(1)} %get-tuple-element.90.refs_0_.refs_7_, ...), custom_call_target="tpu_custom_call" | custom-call | bytes 1024 | tf_op jit(solution)/shard_map/attend_forward/pallas_call | solution.py:192
  31.5 5.2 %collective-permute-done.7.refs_8_ = bf16[10,48,384]{2,1,0:T(8,128)(2,1)S(1)} collective-permute-done((bf16[10,48,384]{2,1,0:T(8,128)(2,1)S(1)}, bf16[10,48,384]{2,1,0:T(8,128)(2,1)S(1)}, u32[]{:S(2)}, u32[]{:S(2)}) %collective-permute-start.7) | collective-permute-done | bytes 368672 | tf_op jit(solution)/shard_map/ppermute | solution.py:678
  40.4 6.5 %collective-permute-done.13.refs_9_ = bf16[10,48,384]{2,1,0:T(8,128)(2,1)S(1)} collective-permute-done((bf16[10,48,384]{2,1,0:T(8,128)(2,1)S(1)}, bf16[10,48,384]{2,1,0:T(8,128)(2,1)S(1)}, u32[]{:S(2)}, u32[]{:S(2)}) %collective-permute-start.13) | collective-permute-done | bytes 368672 | tf_op jit(solution)/shard_map/ppermute | solution.py:678
  49.0 14.8 %collective-permute-done.11.refs_6_ = bf16[256,768]{1,0:T(8,128)(2,1)S(1)} collective-permute-done((bf16[256,768]{1,0:T(8,128)(2,1)S(1)}, bf16[256,768]{1,0:T(8,128)(2,1)S(1)}, u32[]{:S(2)}, u32[]{:S(2)}) %collective-permute-start.11) | collective-permute-done | bytes 393248 | tf_op jit(solution)/shard_map/ppermute | solution.py:678
  66.2 2.8 %collective-permute-done.17.refs_8_ = bf16[10,48,384]{2,1,0:T(8,128)(2,1)S(1)} collective-permute-done((bf16[10,48,384]{2,1,0:T(8,128)(2,1)S(1)}, bf16[10,48,384]{2,1,0:T(8,128)(2,1)S(1)}, u32[]{:S(2)}, u32[]{:S(2)}) %collective-permute-start.17) | collective-permute-done | bytes 368672 | tf_op jit(solution)/shard_map/ppermute | solution.py:678
  71.7 9.8 %attend_forward.3 = (bf16[576,512]{1,0:T(8,128)(2,1)}, bf16[192,512]{1,0:T(8,128)(2,1)}, bf16[3,512,512]{2,1,0:T(8,128)(2,1)}, bf16[576,512]{1,0:T(8,128)(2,1)},...) custom-call(s32[6]{0:T(128)S(1)} %stack.27.refs_0_.meta.refs_1_.refs, ...), custom_call_target="tpu_custom_call" | custom-call | bytes 1024 | tf_op jit(solution)/shard_map/attend_forward/pallas_call | solution.py:192
  81.5 3.5 %ffn_forward.2 = (bf16[2,512,768]{2,1,0:T(8,128)(2,1)S(1)}, f32[512,768]{1,0:T(8,128)S(1)}) custom-call(f32[512,768]{1,0:T(8,128)S(1)} %get-tuple-element.102.refs_0_.refs_1_, f32[512,768]{1,0:T(8,128)S(1)} %get-tuple-element.102.refs_0_.refs_1_, bf16[768,768]{1,0:T(8,128)(2,1)S(1)} %copy-done, ...), custom_call_target="tpu_custom_call" | custom-call | bytes 1024 | tf_op jit(solution)/shard_map/ffn_forward/pallas_call | solution.py:229
  86.7 4.1 %collective-permute-done.24.refs_3_ = bf16[20,48,384]{2,1,0:T(8,128)(2,1)S(1)} collective-permute-done((bf16[20,48,384]{2,1,0:T(8,128)(2,1)S(1)}, bf16[20,48,384]{2,1,0:T(8,128)(2,1)S(1)}, u32[]{:S(2)}, u32[]{:S(2)}) %collective-permute-start.24) | collective-permute-done | bytes 737312 | tf_op jit(solution)/shard_map/ppermute | solution.py:678
  91.7 3.7 %ffn_forward.3 = (bf16[2,512,768]{2,1,0:T(8,128)(2,1)S(1)}, f32[512,768]{1,0:T(8,128)S(1)}) custom-call(f32[512,768]{1,0:T(8,128)S(1)} %get-tuple-element.102.refs_0_.refs_1_, f32[512,768]{1,0:T(8,128)S(1)} %get-tuple-element.103.refs_0_.refs_1_, bf16[768,768]{1,0:T(8,128)(2,1)S(1)} %get-tuple-element.109.refs_2_.refs_4_, ...), custom_call_target="tpu_custom_call" | custom-call | bytes 1024 | tf_op jit(solution)/shard_map/ffn_forward/pallas_call | solution.py:229
  95.4 16.7 %merging.1 = (f32[512,768]{1,0:T(8,128)}, f32[512,768]{1,0:T(8,128)S(1)}, bf16[512,768]{1,0:T(8,128)(2,1)S(1)}, bf16[512,768]{1,0:T(8,128)(2,1)S(1)}, bf16[2,2,4...) custom-call(s32[6]{0:T(128)S(1)} %stack.27.refs_0_.meta.refs_1_.refs_4_.refs_3_, ...), custom_call_target="tpu_custom_call" | custom-call | bytes 1024 | tf_op jit(solution)/shard_map/merging/pallas_call | solution.py:388
  112.4 2.0 %merging_input.1 = (f32[512,768]{1,0:T(8,128)S(1)}, bf16[512,768]{1,0:T(8,128)(2,1)S(1)}) custom-call(f32[512,768]{1,0:T(8,128)S(1)} %get-tuple-element.111.sums.refs_0_, f32[8,768]{1,0:T(8,128)S(1)} %get-tuple-element.91.refs_5_.refs_4_.lines.refs_1_.refs_12_, f32[512,768]{1,0:T(8,128)S(1)} %get-tuple-element.114.refs_2_, ...), custom_call_target="tpu_custom_call" | custom-call | bytes 1024 | tf_op jit(solution)/shard_map/merging_input/pallas_call | solution.py:416
  114.5 3.1 %ffn_backward.2.refs_0_.refs_2_ = f32[512,768]{1,0:T(8,128)S(1)} custom-call(bf16[512,768]{1,0:T(8,128)(2,1)S(1)} %get-tuple-element.117.refs_0_.refs_1_, f32[512,768]{1,0:T(8,128)S(1)} %get-tuple-element.118.refs_1_, bf16[2,512,768]{2,1,0:T(8,128)(2,1)S(1)} %get-tuple-element.119.refs_2_, bf16[768,768]{1,0:T(8,128)(2,1)S(1)} %copy-done, ...), custom_call_target="tpu_custom_call" | custom-call | bytes 1024 | tf_op jit(solution)/shard_map/ffn_backward/pallas_call | solution.py:454
  119.5 3.5 %ffn_backward.3 = (f32[512,768]{1,0:T(8,128)S(1)}, bf16[512,768]{1,0:T(8,128)(2,1)S(1)}) custom-call(bf16[2,4,80,384]{3,2,1,0:T(8,128)(2,1)S(1)} %get-tuple-element.122.refs_0_.refs_1_, bf16[512,768]{1,0:T(8,128)(2,1)S(1)} %get-tuple-element.117.refs_0_.refs_1_, f32[512,768]{1,0:T(8,128)S(1)} %ffn_backward.2.refs_0_.refs_2_, ...), custom_call_target="tpu_custom_call" | custom-call | bytes 1024 | tf_op jit(solution)/shard_map/ffn_backward/pallas_call | solution.py:454
  123.0 3.8 %attend_backward.4 = (f32[512,768]{1,0:T(8,128)S(1)}, f32[8,128]{1,0:T(8,128)S(1)}) custom-call(bf16[512,768]{1,0:T(8,128)(2,1)S(1)} %get-tuple-element.126.refs_0_.refs_1_, f32[512,768]{1,0:T(8,128)S(1)} %get-tuple-element.127.refs_1_, bf16[576,512]{1,0:T(8,128)(2,1)S(1)} %copy-done.9, bf16[192,512]{1,0:T(8,128)(2,1)S(1)} %copy-done.13, ...), custom_call_target="tpu_custom_call" | custom-call | bytes 1024 | tf_op jit(solution)/shard_map/attend_backward/pallas_call | solution.py:494
  126.8 4.8 %collective-permute-done.26.refs_2_ = bf16[2,4,80,384]{3,2,1,0:T(8,128)(2,1)S(1)} collective-permute-done((bf16[2,4,80,384]{3,2,1,0:T(8,128)(2,1)S(1)}, bf16[2,4,80,384]{3,2,1,0:T(8,128)(2,1)S(1)}, u32[]{:S(2)}, u32[]{:S(2)}) %collective-permute-start.26) | collective-permute-done | bytes 491552 | tf_op jit(solution)/shard_map/ppermute | solution.py:678
  134.3 3.6 %attend_backward.5 = (f32[512,768]{1,0:T(8,128)S(1)}, f32[8,128]{1,0:T(8,128)S(1)}) custom-call(bf16[4,80,384]{2,1,0:T(8,128)(2,1)S(1)} %get-tuple-element.135.refs_0_.refs_1_, bf16[512,768]{1,0:T(8,128)(2,1)S(1)} %get-tuple-element.126.refs_0_.refs_1_, f32[512,768]{1,0:T(8,128)S(1)} %get-tuple-element.136.refs_2_, bf16[576,512]{1,0:T(8,128)(2,1)S(1)} %copy-done.8, ...), custom_call_target="tpu_custom_call" | custom-call | bytes 1024 | tf_op jit(solution)/shard_map/attend_backward/pallas_call | solution.py:494
  141.3 2.4 %collective-permute-start.31 = (bf16[80,768]{1,0:T(8,128)(2,1)S(1)}, bf16[80,768]{1,0:T(8,128)(2,1)S(1)}, u32[]{:S(2)}, u32[]{:S(2)}) collective-permute-start(bf16[80,768]{1,0:T(8,128)(2,1)S(1)} %get-tuple-element.156), channel_id=1, source_target_pairs={{0,16},{1,17},{2,18},{3,19},{4,20},{5,21},{6,22},{7,23},{8,24},{9,... | collective-permute-start | bytes 368648 | tf_op jit(solution)/shard_map/ppermute | solution.py:678
  144.8 4.1 %attend_backward.6 = (f32[512,768]{1,0:T(8,128)S(1)}, f32[8,128]{1,0:T(8,128)}) custom-call(bf16[80,768]{1,0:T(8,128)(2,1)S(1)} %get-tuple-element.144.refs_0_.refs_1_, bf16[512,768]{1,0:T(8,128)(2,1)S(1)} %get-tuple-element.126.refs_0_.refs_1_, f32[512,768]{1,0:T(8,128)S(1)} %get-tuple-element.145.refs_2_, bf16[576,512]{1,0:T(8,128)(2,1)S(1)} %copy-done.11, ...), custom_call_target="tpu_custom_call" | custom-call | bytes 1024 | tf_op jit(solution)/shard_map/attend_backward/pallas_call | solution.py:494
  148.9 4.8 %attend_backward.7 = (f32[512,768]{1,0:T(8,128)}, f32[8,128]{1,0:T(8,128)S(1)}) custom-call(bf16[80,768]{1,0:T(8,128)(2,1)S(1)} %get-tuple-element.144.refs_0_.refs_1_, bf16[512,768]{1,0:T(8,128)(2,1)S(1)} %get-tuple-element.126.refs_0_.refs_1_, f32[512,768]{1,0:T(8,128)S(1)} %get-tuple-element.149.refs_2_, bf16[576,512]{1,0:T(8,128)(2,1)S(1)} %copy-done.10, ...), custom_call_target="tpu_custom_call" | custom-call | bytes 1024 | tf_op jit(solution)/shard_map/attend_backward/pallas_call | solution.py:494
  (105 shorter events, 30.4 us)
Async XLA Ops:
  2.7 13.3 %collective-permute-start = (bf16[768,768]{1,0:T(8,128)(2,1)S(1)}, bf16[768,768]{1,0:T(8,128)(2,1)S(1)}, u32[]{:S(2)}, u32[]{:S(2)}) collective-permute-start(bf16[768,768]{1,0:T(8,128)(2,1)S(1)} %get-tuple-element.86.refs_6_.refs_5_), channel_id=1, source_target_pairs={{0,1},{1,0},{2,3},{3,2},{4,5},{5,4},{6,7},{7,6},{8,9},{9,8},{10,11... | collective-permute-start | bytes 3538952 | tf_op jit(solution)/shard_map/ppermute | solution.py:678
  3.2 36.4 %collective-permute-start.3 = (bf16[768,768]{1,0:T(8,128)(2,1)S(1)}, bf16[768,768]{1,0:T(8,128)(2,1)S(1)}, u32[]{:S(2)}, u32[]{:S(2)}) collective-permute-start(bf16[768,768]{1,0:T(8,128)(2,1)S(1)} %copy-done), channel_id=1, source_target_pairs={{0,1},{1,0},{2,3},{3,2},{4,5},{5,4},{6,7},{7,6},{8,9},{9,8},{10,11... | collective-permute-start | bytes 3538952 | tf_op jit(solution)/shard_map/ppermute | solution.py:678
  5.0 34.9 %collective-permute-start.4 = (bf16[768,768]{1,0:T(8,128)(2,1)S(1)}, bf16[768,768]{1,0:T(8,128)(2,1)S(1)}, u32[]{:S(2)}, u32[]{:S(2)}) collective-permute-start(bf16[768,768]{1,0:T(8,128)(2,1)S(1)} %copy-done.1), channel_id=1, source_target_pairs={{0,1},{1,0},{2,3},{3,2},{4,5},{5,4},{6,7},{7,6},{8,9},{9,8},{10,11... | collective-permute-start | bytes 3538952 | tf_op jit(solution)/shard_map/ppermute | solution.py:678
  8.1 7.9 %collective-permute-start.2 = (bf16[5,48,384]{2,1,0:T(8,128)(2,1)S(1)}, bf16[5,48,384]{2,1,0:T(8,128)(2,1)S(1)}, u32[]{:S(2)}, u32[]{:S(2)}) collective-permute-start(bf16[5,48,384]{2,1,0:T(8,128)(2,1)S(1)} %chip_tile.1.refs_3_), channel_id=1, source_target_pairs={{0,2},{1,3},{2,0},{3,1},{4,6},{5,7},{6,4},{7,5},{8,10},{9,11},{10,... | collective-permute-start | bytes 552968 | tf_op jit(solution)/shard_map/ppermute | solution.py:678
  16.6 20.2 %collective-permute-start.5 = (bf16[384,768]{1,0:T(8,128)(2,1)S(1)}, bf16[384,768]{1,0:T(8,128)(2,1)S(1)}, u32[]{:S(2)}, u32[]{:S(2)}) collective-permute-start(bf16[384,768]{1,0:T(8,128)(2,1)S(1)} %get-tuple-element.94), channel_id=1, source_target_pairs={{0,2},{1,3},{2,0},{3,1},{4,6},{5,7},{6,4},{7,5},{8,10},{9,11},{10,... | collective-permute-start | bytes 1769480 | tf_op jit(solution)/shard_map/ppermute | solution.py:678
  18.4 18.3 %collective-permute-start.7 = (bf16[10,48,384]{2,1,0:T(8,128)(2,1)S(1)}, bf16[10,48,384]{2,1,0:T(8,128)(2,1)S(1)}, u32[]{:S(2)}, u32[]{:S(2)}) collective-permute-start(bf16[10,48,384]{2,1,0:T(8,128)(2,1)S(1)} %get-tuple-element.90.refs_0_.refs_7_), channel_id=1, source_target_pairs={{0,16},{1,17},{2,18},{3,19},{4,20},{5,21},{6,22},{7,23},{8,24},{9,... | collective-permute-start | bytes 1105928 | tf_op jit(solution)/shard_map/ppermute | solution.py:678
  21.0 15.8 %collective-permute-start.6 = (bf16[10,48,384]{2,1,0:T(8,128)(2,1)S(1)}, bf16[10,48,384]{2,1,0:T(8,128)(2,1)S(1)}, u32[]{:S(2)}, u32[]{:S(2)}) collective-permute-start(bf16[10,48,384]{2,1,0:T(8,128)(2,1)S(1)} %get-tuple-element.90.refs_0_.refs_7_), channel_id=1, source_target_pairs={{0,4},{1,5},{2,6},{3,7},{4,0},{5,1},{6,2},{7,3},{8,12},{9,13},{10,... | collective-permute-start | bytes 1105928 | tf_op jit(solution)/shard_map/ppermute | solution.py:678
  37.4 9.5 %collective-permute-start.13 = (bf16[10,48,384]{2,1,0:T(8,128)(2,1)S(1)}, bf16[10,48,384]{2,1,0:T(8,128)(2,1)S(1)}, u32[]{:S(2)}, u32[]{:S(2)}) collective-permute-start(bf16[10,48,384]{2,1,0:T(8,128)(2,1)S(1)} %get-tuple-element.99), channel_id=1, source_target_pairs={{0,4},{1,5},{2,6},{3,7},{4,0},{5,1},{6,2},{7,3},{8,12},{9,13},{10,... | collective-permute-start | bytes 1105928 | tf_op jit(solution)/shard_map/ppermute | solution.py:678
  39.0 9.4 %collective-permute-start.9 = (bf16[10,48,384]{2,1,0:T(8,128)(2,1)S(1)}, bf16[10,48,384]{2,1,0:T(8,128)(2,1)S(1)}, u32[]{:S(2)}, u32[]{:S(2)}) collective-permute-start(bf16[10,48,384]{2,1,0:T(8,128)(2,1)S(1)} %get-tuple-element.96.refs_5_), channel_id=1, source_target_pairs={{0,1},{1,0},{2,3},{3,2},{4,5},{5,4},{6,7},{7,6},{8,9},{9,8},{10,11... | collective-permute-start | bytes 1105928 | tf_op jit(solution)/shard_map/ppermute | solution.py:678
  39.0 24.9 %collective-permute-start.12 = (bf16[20,48,384]{2,1,0:T(8,128)(2,1)S(1)}, bf16[20,48,384]{2,1,0:T(8,128)(2,1)S(1)}, u32[]{:S(2)}, u32[]{:S(2)}) collective-permute-start(bf16[20,48,384]{2,1,0:T(8,128)(2,1)S(1)} %get-tuple-element.95.refs_1_), channel_id=1, source_target_pairs={{0,8},{1,9},{2,10},{3,11},{4,12},{5,13},{6,14},{7,15},{8,0},{9,1},... | collective-permute-start | bytes 2211848 | tf_op jit(solution)/shard_map/ppermute | solution.py:678
  39.6 24.2 %collective-permute-start.8 = (bf16[20,48,384]{2,1,0:T(8,128)(2,1)S(1)}, bf16[20,48,384]{2,1,0:T(8,128)(2,1)S(1)}, u32[]{:S(2)}, u32[]{:S(2)}) collective-permute-start(bf16[20,48,384]{2,1,0:T(8,128)(2,1)S(1)} %get-tuple-element.95.refs_1_), channel_id=1, source_target_pairs={{0,1},{1,0},{2,3},{3,2},{4,5},{5,4},{6,7},{7,6},{8,9},{9,8},{10,11... | collective-permute-start | bytes 2211848 | tf_op jit(solution)/shard_map/ppermute | solution.py:678
  39.9 23.9 %collective-permute-start.10 = (bf16[384,768]{1,0:T(8,128)(2,1)S(1)}, bf16[384,768]{1,0:T(8,128)(2,1)S(1)}, u32[]{:S(2)}, u32[]{:S(2)}) collective-permute-start(bf16[384,768]{1,0:T(8,128)(2,1)S(1)} %get-tuple-element.97), channel_id=1, source_target_pairs={{0,2},{1,3},{2,0},{3,1},{4,6},{5,7},{6,4},{7,5},{8,10},{9,11},{10,... | collective-permute-start | bytes 1769480 | tf_op jit(solution)/shard_map/ppermute | solution.py:678
  46.9 16.9 %collective-permute-start.14 = (bf16[384,768]{1,0:T(8,128)(2,1)S(1)}, bf16[384,768]{1,0:T(8,128)(2,1)S(1)}, u32[]{:S(2)}, u32[]{:S(2)}) collective-permute-start(bf16[384,768]{1,0:T(8,128)(2,1)S(1)} %get-tuple-element.100.refs_10_), channel_id=1, source_target_pairs={{0,4},{1,5},{2,6},{3,7},{4,0},{5,1},{6,2},{7,3},{8,12},{9,13},{10,... | collective-permute-start | bytes 1769480 | tf_op jit(solution)/shard_map/ppermute | solution.py:678
  48.4 15.4 %collective-permute-start.11 = (bf16[256,768]{1,0:T(8,128)(2,1)S(1)}, bf16[256,768]{1,0:T(8,128)(2,1)S(1)}, u32[]{:S(2)}, u32[]{:S(2)}) collective-permute-start(bf16[256,768]{1,0:T(8,128)(2,1)S(1)} %get-tuple-element.98), channel_id=1, source_target_pairs={{0,2},{1,3},{2,0},{3,1},{4,6},{5,7},{6,4},{7,5},{8,10},{9,11},{10,... | collective-permute-start | bytes 1179656 | tf_op jit(solution)/shard_map/ppermute | solution.py:678
  64.5 7.2 %collective-permute-start.15 = (bf16[768,768]{1,0:T(8,128)(2,1)S(1)}, bf16[768,768]{1,0:T(8,128)(2,1)S(1)}, u32[]{:S(2)}, u32[]{:S(2)}) collective-permute-start(bf16[768,768]{1,0:T(8,128)(2,1)S(1)} %get-tuple-element.101.refs_5_.refs_6_), channel_id=1, source_target_pairs={{0,1},{1,0},{2,3},{3,2},{4,5},{5,4},{6,7},{7,6},{8,9},{9,8},{10,11... | collective-permute-start | bytes 3538952 | tf_op jit(solution)/shard_map/ppermute | solution.py:678
  65.1 19.9 %collective-permute-start.19 = (bf16[512,768]{1,0:T(8,128)(2,1)S(1)}, bf16[512,768]{1,0:T(8,128)(2,1)S(1)}, u32[]{:S(2)}, u32[]{:S(2)}) collective-permute-start(bf16[512,768]{1,0:T(8,128)(2,1)S(1)} %get-tuple-element.107), channel_id=1, source_target_pairs={{0,2},{1,3},{2,0},{3,1},{4,6},{5,7},{6,4},{7,5},{8,10},{9,11},{10,... | collective-permute-start | bytes 2359304 | tf_op jit(solution)/shard_map/ppermute | solution.py:678
  65.7 19.3 %collective-permute-start.20 = (bf16[20,48,384]{2,1,0:T(8,128)(2,1)S(1)}, bf16[20,48,384]{2,1,0:T(8,128)(2,1)S(1)}, u32[]{:S(2)}, u32[]{:S(2)}) collective-permute-start(bf16[20,48,384]{2,1,0:T(8,128)(2,1)S(1)} %get-tuple-element.104.refs_3_), channel_id=1, source_target_pairs={{0,4},{1,5},{2,6},{3,7},{4,0},{5,1},{6,2},{7,3},{8,12},{9,13},{10,... | collective-permute-start | bytes 2211848 | tf_op jit(solution)/shard_map/ppermute | solution.py:678
  69.0 16.0 %collective-permute-start.21 = (bf16[384,768]{1,0:T(8,128)(2,1)S(1)}, bf16[384,768]{1,0:T(8,128)(2,1)S(1)}, u32[]{:S(2)}, u32[]{:S(2)}) collective-permute-start(bf16[384,768]{1,0:T(8,128)(2,1)S(1)} %get-tuple-element.108.refs_6_), channel_id=1, source_target_pairs={{0,8},{1,9},{2,10},{3,11},{4,12},{5,13},{6,14},{7,15},{8,0},{9,1},... | collective-permute-start | bytes 1769480 | tf_op jit(solution)/shard_map/ppermute | solution.py:678
  70.3 14.6 %collective-permute-start.18 = (bf16[256,768]{1,0:T(8,128)(2,1)S(1)}, bf16[256,768]{1,0:T(8,128)(2,1)S(1)}, u32[]{:S(2)}, u32[]{:S(2)}) collective-permute-start(bf16[256,768]{1,0:T(8,128)(2,1)S(1)} %get-tuple-element.106.refs_4_.refs_6_), channel_id=1, source_target_pairs={{0,1},{1,0},{2,3},{3,2},{4,5},{5,4},{6,7},{7,6},{8,9},{9,8},{10,11... | collective-permute-start | bytes 1179656 | tf_op jit(solution)/shard_map/ppermute | solution.py:678
  118.3 13.3 %collective-permute-start.26 = (bf16[2,4,80,384]{3,2,1,0:T(8,128)(2,1)S(1)}, bf16[2,4,80,384]{3,2,1,0:T(8,128)(2,1)S(1)}, u32[]{:S(2)}, u32[]{:S(2)}) collective-permute-start(bf16[2,4,80,384]{3,2,1,0:T(8,128)(2,1)S(1)} %get-tuple-element.132), channel_id=1, source_target_pairs={{0,2},{1,3},{2,0},{3,1},{4,6},{5,7},{6,4},{7,5},{8,10},{9,11},{10,... | collective-permute-start | bytes 1474568 | tf_op jit(solution)/shard_map/ppermute | solution.py:678
  118.9 13.1 %collective-permute-start.27 = (bf16[2,4,80,384]{3,2,1,0:T(8,128)(2,1)S(1)}, bf16[2,4,80,384]{3,2,1,0:T(8,128)(2,1)S(1)}, u32[]{:S(2)}, u32[]{:S(2)}) collective-permute-start(bf16[2,4,80,384]{3,2,1,0:T(8,128)(2,1)S(1)} %get-tuple-element.134), channel_id=1, source_target_pairs={{0,4},{1,5},{2,6},{3,7},{4,0},{5,1},{6,2},{7,3},{8,12},{9,13},{10,... | collective-permute-start | bytes 1474568 | tf_op jit(solution)/shard_map/ppermute | solution.py:678
  139.7 14.0 %collective-permute-start.30 = (bf16[80,768]{1,0:T(8,128)(2,1)S(1)}, bf16[80,768]{1,0:T(8,128)(2,1)S(1)}, u32[]{:S(2)}, u32[]{:S(2)}) collective-permute-start(bf16[80,768]{1,0:T(8,128)(2,1)S(1)} %get-tuple-element.155), channel_id=1, source_target_pairs={{0,8},{1,9},{2,10},{3,11},{4,12},{5,13},{6,14},{7,15},{8,0},{9,1},... | collective-permute-start | bytes 368648 | tf_op jit(solution)/shard_map/ppermute | solution.py:678
  141.3 12.4 %collective-permute-start.31 = (bf16[80,768]{1,0:T(8,128)(2,1)S(1)}, bf16[80,768]{1,0:T(8,128)(2,1)S(1)}, u32[]{:S(2)}, u32[]{:S(2)}) collective-permute-start(bf16[80,768]{1,0:T(8,128)(2,1)S(1)} %get-tuple-element.156), channel_id=1, source_target_pairs={{0,16},{1,17},{2,18},{3,19},{4,20},{5,21},{6,22},{7,23},{8,24},{9,... | collective-permute-start | bytes 368648 | tf_op jit(solution)/shard_map/ppermute | solution.py:678
  143.7 10.0 %collective-permute-start.32 = (bf16[80,768]{1,0:T(8,128)(2,1)S(1)}, bf16[80,768]{1,0:T(8,128)(2,1)S(1)}, u32[]{:S(2)}, u32[]{:S(2)}) collective-permute-start(bf16[80,768]{1,0:T(8,128)(2,1)S(1)} %get-tuple-element.157), channel_id=1, source_target_pairs={{0,24},{1,25},{2,26},{3,27},{4,28},{5,29},{6,30},{7,31},{8,16},{9,... | collective-permute-start | bytes 368648 | tf_op jit(solution)/shard_map/ppermute | solution.py:678
  (26 other events, 169.2 us)
where the time goes:
time: 155 us; the launch traced here: 154 us
  Pallas kernels  77.6 us (50%)
  waiting for transfers between devices  47.7 us (31%)
  starting transfers between devices  27.8 us (18%)
    ppermute x33, waiting for transfers between devices, flip(): return lax.ppermute(array, AXES, [(i, i ^ bits) for i in range(self.count)])  47.7 us
    ppermute x33, starting transfers between devices, flip(): return lax.ppermute(array, AXES, [(i, i ^ bits) for i in range(self.count)])  27.8 us
    pallas_call x2, Pallas kernels, call_attend_forward(): kernel(functools.partial(attend_forward, columns, last), deps, ATTEND_MIB...  18.7 us
    pallas_call x1, Pallas kernels, call_merging(): pl.pallas_call(functools.partial(merging, n_adapters), in_specs=[SMEM, SM...  16.7 us
    pallas_call x4, Pallas kernels, call_attend_backward(): kernel(functools.partial(attend_backward, columns), deps, ATTEND_MIB, in_...  16.3 us
    pallas_call x2, Pallas kernels, call_ffn_forward(): kernel(functools.partial(ffn_forward, len(out_quarters) // 2), deps, FFN_...  7.16 us
    pallas_call x2, Pallas kernels, call_ffn_backward(): kernel(functools.partial(ffn_backward, last, len(out_quarters) // 2), dep...  6.58 us
  transfers between devices with their start and end apart: 33, of which 12 were waited for; matrix products, arithmetic and copies ran while one was open for 0% of the time, Pallas kernels for 34%

commit v1 on v0

--- a/solution.py
+++ b/solution.py
@@ -140,22 +140,22 @@
 def sync(name, meta, joins, carries, deps):
     sides = [j[0] if isinstance(j[0], int) else None for j in joins]
     parts = [j[1:] if isinstance(j[0], int) else j for j in joins]
-    flat = [p for j in parts for p in j]
+    parts = [[p if isinstance(p, tuple) else (p, 0, p.shape[0]) for p in j] for j in parts]
+    flat = [p[0] for j in parts for p in j]
 
     def body(meta_ref, *refs):
         refs = refs[len(carries) :]
         sources, outs = list(refs[: len(flat)]), refs[len(flat) : len(flat) + len(parts)]
         for side, join, out in zip(sides, parts, outs):
             row = 0
-            for i, part in enumerate(join):
-                size = part.shape[0]
+            for i, (_, start, size) in enumerate(join):
                 if side is not None:
                     n = len(join) // 2
                     row = pl.multiple_of(((meta_ref[side] ^ (i // n)) * n + i % n) * size, 16)
-                out[pl.ds(row, size)] = sources.pop(0)[...]
+                out[pl.ds(row, size)] = sources.pop(0)[start : start + size]
                 row = row + size
 
-    joined = [sds((sum(p.shape[0] for p in j), *j[0].shape[1:]), j[0].dtype) for j in parts]
+    joined = [sds((sum(p[2] for p in j), *j[0][0].shape[1:]), j[0][0].dtype) for j in parts]
     n_deps = len(deps)
     out = kernel(
         body,
@@ -202,14 +202,14 @@
     )(meta, lengths, tokens, before, lines, *quarters)
 
 
-def ffn_forward(blocks, first, before, *refs):
+def ffn_forward(quarters, blocks, first, before, *refs):
     slope_out, sum_out = refs[-2:]
 
     def chunk(rows):
         low = first[rows].astype(BF16)
         total = before[rows]
-        outs = list(refs[2:-2])
-        for quarter in range(2):
+        outs = list(refs[quarters:-2])
+        for quarter in range(quarters):
             value, slope = gelu_both(dot(low, refs[quarter][...]))
             slope_out[quarter, rows] = slope.astype(BF16)
             value = value.astype(BF16)
@@ -226,19 +226,20 @@
 def call_ffn_forward(deps, first, before, in_quarters, out_quarters):
     seq, width = first.shape
     hidden = in_quarters[0].shape[1]
+    quarters = len(in_quarters)
     return kernel(
-        functools.partial(ffn_forward, len(out_quarters) // 2),
+        functools.partial(ffn_forward, quarters, len(out_quarters) // quarters),
         deps,
         FFN_MIB,
-        in_specs=[VMEM] * (4 + len(out_quarters)),
+        in_specs=[VMEM] * (2 + quarters + len(out_quarters)),
         out_specs=[VMEM] * 2,
-        out_shape=[sds((2, seq, hidden), BF16), sds((seq, width), F32)],
+        out_shape=[sds((quarters, seq, hidden), BF16), sds((seq, width), F32)],
         cost_estimate=cost(5),
         name="ffn_forward",
     )(first, before, *in_quarters, *out_quarters)
 
 
-def assemble(name, meta, weights, tiles):
+def assemble(name, deps, meta, weights, tiles):
     n_mats = tiles[0][0].shape[0] // (2 * len(tiles[0][1]))
     rows, half = tiles[0][0].shape[1:]
     count = sum(2 * len(parts) for _, parts, _ in tiles)
@@ -265,12 +266,12 @@
 
     return kernel(
         body,
-        [],
+        deps,
         16,
         in_specs=[SMEM] + [ANY] * len(before) + [VMEM] * len(tiles),
         out_specs=ANY,
         out_shape=sds((n_mats, 2 * half, 2 * half), BF16),
-        input_output_aliases={1: 0} if before else {},
+        input_output_aliases={len(deps) + 1: 0} if before else {},
         scratch_shapes=[pltpu.SemaphoreType.DMA((count,))],
         cost_estimate=cost(0),
         name=name,
@@ -365,9 +366,14 @@
         )
 
     by_chunks(seq, chunk)
-    grads[0] = dot_first(states[...], fquery_out[...])
-    grads[1] = dot_first(probes[...], fqueries[...])
-    grads[2] = dot_first(blends[...], values[...])
+
+    @pl.loop(0, width // CHUNK)
+    def _(i):
+        part = pl.ds(pl.multiple_of(i * CHUNK, CHUNK), CHUNK)
+        grads[0, part] = dot_first(states[:, part], fquery_out[...])
+        grads[1, part] = dot_first(probes[:, part], fqueries[...])
+        grads[2, part] = dot_first(blends[:, part], values[...])
+
     tail = split_lines(sum_lines[0:4])
     rows = width // 32
 
@@ -425,7 +431,9 @@
     )(sums, lines, part, grad_fquery, grad_middle, matrices)
 
 
-def ffn_backward(last, blocks, grad_low, before, slope, in0, in1, *refs):
+def ffn_backward(last, blocks, n_slopes, grad_low, before, *refs):
+    slopes, (in0, in1), refs = refs[:n_slopes], refs[n_slopes : n_slopes + 2], refs[n_slopes + 2 :]
+    slopes = [slope.at[i] for slope in slopes for i in range(slope.shape[0])]
     all_outs, refs = refs[: 2 * blocks], refs[2 * blocks :]
 
     def chunk(rows):
@@ -435,7 +443,7 @@
         for quarter, into in enumerate((in0, in1)):
             grad_act = [dot_last(low, outs.pop(0)[...]) for _ in range(blocks)]
             grad_act = grad_act[0] if blocks == 1 else jnp.concatenate(grad_act, axis=1)
-            grad_pre = (grad_act * slope[quarter, rows].astype(F32)).astype(BF16)
+            grad_pre = (grad_act * slopes[quarter][rows].astype(F32)).astype(BF16)
             total = total + dot_last(grad_pre, into[...])
         if not last:
             refs[0][rows] = total
@@ -448,19 +456,19 @@
     by_chunks(before.shape[0], chunk)
 
 
-def call_ffn_backward(deps, grad_low, before, slope, in_quarters, out_quarters, *for_norm):
+def call_ffn_backward(deps, grad_low, before, slopes, in_quarters, out_quarters, *for_norm):
     seq, width = before.shape
     last = bool(for_norm)
     return kernel(
-        functools.partial(ffn_backward, last, len(out_quarters) // 2),
+        functools.partial(ffn_backward, last, len(out_quarters) // 2, len(slopes)),
         deps,
         FFN_MIB,
-        in_specs=[VMEM] * (5 + len(out_quarters) + len(for_norm)),
+        in_specs=[VMEM] * (4 + len(slopes) + len(out_quarters) + len(for_norm)),
         out_specs=[VMEM] * (1 + last),
         out_shape=[sds((seq, width), F32)] + [sds((seq, width), BF16)] * last,
         cost_estimate=cost(5),
         name="ffn_backward",
-    )(grad_low, before, slope, *in_quarters, *out_quarters, *for_norm)
+    )(grad_low, before, *slopes, *in_quarters, *out_quarters, *for_norm)
 
 
 def attend_backward(
@@ -470,7 +478,7 @@
     root = HEAD_DIM**-0.5
     grad_att[...] = dot_last(weight[columns:], grad_low[...]).astype(BF16)
 
-    @pl.loop(0, columns // width)
+    @pl.loop(0, columns // width, unroll=True)
     def _(head):
         base = pl.multiple_of(head * width, width)
         places = [pl.ds(base + i * HEAD_DIM, HEAD_DIM) for i in range(3)]
@@ -536,31 +544,37 @@
     )(meta, *(in_hbm(a) for a in (down, up, query, key, value, *vectors)))
 
 
-def prepare_frozen(meta, qkv_turned, attn_out, into, attn, attn_half, in_half):
+def prepare_frozen(meta, qkv_turned, attn_out, into, out, attn, with_attn, with_in, out_last, *copies):
     columns = qkv_turned.shape[0]
     attn[:columns] = qkv_turned[...]
     attn[columns:] = attn_out[...]
-    for entry, whole, half in ((PAIR_Y, attn, attn_half), (PAIR_Z, into, in_half)):
-        rows = half.shape[0]
-        half[...] = whole[pl.ds(pl.multiple_of(meta[entry] * rows, 16), rows)]
-
-
-def call_prepare_frozen(meta, qkv_turned, attn_out, into):
+    row = 0
+    for entry, whole, share in ((PAIR_Y, attn, with_attn), (PAIR_Z, into, with_in)):
+        half = whole.shape[0] // 2
+        cut = share.shape[0] - half
+        share[:half] = whole[pl.ds(pl.multiple_of(meta[entry] * half, 16), half)]
+        share[half:] = out[row : row + cut]
+        row += cut
+    out_last[...] = out[row:]
+    for source, copy in zip((into, out), copies):
+        copy[...] = source[...]
+
+
+def call_prepare_frozen(deps, meta, qkv_turned, attn_out, into, out):
     rows, width = qkv_turned.shape[0] + attn_out.shape[0], attn_out.shape[1]
+    cut = out.shape[0] // 6
+    shares = (rows, rows // 2 + cut, into.shape[0] // 2 + cut, out.shape[0] - 2 * cut)
+    shares = shares + (into.shape[0], out.shape[0])
     return kernel(
         prepare_frozen,
-        [],
+        deps,
         16,
-        in_specs=[SMEM] + [VMEM] * 3,
-        out_specs=[VMEM] * 3,
-        out_shape=[
-            sds((rows, width), BF16),
-            sds((rows // 2, width), BF16),
-            sds((into.shape[0] // 2, into.shape[1]), BF16),
-        ],
+        in_specs=[SMEM] + [VMEM] * 4,
+        out_specs=[VMEM] * 6,
+        out_shape=[sds((n, width), BF16) for n in shares],
         cost_estimate=cost(1),
         name="prepare_frozen",
-    )(meta, *(in_hbm(a) for a in (qkv_turned, attn_out, into)))
+    )(meta, *(in_hbm(a) for a in (qkv_turned, attn_out, into, out)))
 
 
 def chip_tile(meta, keep, got, tile):
@@ -716,7 +730,7 @@
     for pair, slope in zip(pairs, slopes):
         for_norm = (normed1, inv_std1, lines) if pair is pairs[-1] else ()
         total, *rest = call_ffn_backward(
-            [], low, total, slope, tuple(into[pair]), tuple(out[pair]), *for_norm
+            [], low, total, [slope], tuple(into[pair]), tuple(out[pair]), *for_norm
         )
     (low,) = rest
     for quarter, kept in zip(attn, saved):
@@ -769,41 +783,50 @@
         merging_gain,
         merging_bias,
     )
-    attn, attn_half, in_half = call_prepare_frozen(
-        meta, qkv_weight.T, attn_out_weight, ffn_in_weight
+    tile = call_chip_tile(meta, keep, flip(send, 1)) if hops.tiled else keep
+    attn, with_attn, with_in, out_2, into, out = call_prepare_frozen(
+        [tile], meta, qkv_weight.T, attn_out_weight, ffn_in_weight, ffn_out_weight
     )
     if not hops.tiled:
         shard = jnp.concatenate([keep, send], axis=2)
         return plain_schedule(
-            meta, doc_lengths, tokens, out_grad, lines, columns, n_adapters, attn, ffn_in_weight, ffn_out_weight, shard
+            meta, doc_lengths, tokens, out_grad, lines, columns, n_adapters, attn, into, out, shard
         )
-    cut = ffn_out_weight.shape[0] // 3
-    out_a, out_b = ffn_out_weight[:cut], ffn_out_weight[cut:]
+    tile_x = flip(tile, ALONG_X)
     attn_core = flip(attn, 1)
-    in_core, out_core = flip(ffn_in_weight, 1), flip(ffn_out_weight, 1)
-    tile = call_chip_tile(meta, keep, flip(send, 1))
-    tile_x = flip(tile, ALONG_X)
-    both, attn_half = sync("phase1", meta, [[tile, tile_x]], [attn_half], [attn_core])
-    z2, attn_x, y0 = flip(both, 2 * ALONG_Z), flip(attn_half, ALONG_X), flip(both, ALONG_Y)
+    both, with_attn, into, out = sync(
+        "phase1", meta, [[tile, tile_x]], [with_attn, into, out], [attn_core]
+    )
+    z2, y0, with_attn_x = flip(both, 2 * ALONG_Z), flip(both, ALONG_Y), flip(with_attn, ALONG_X)
+    in_core, out_core = flip(into, 1), flip(out, 1)
     saved_near = call_attend_forward(
         [both], columns, False, meta, doc_lengths, tokens, tokens, lines, (attn, attn_core)
     )
-    joined, in_half, out_a, attn_x, y0, z2 = sync(
-        "phase2", meta, [[both, z2]], [in_half, out_a, attn_x, y0, z2], [saved_near[6]]
-    )
-    attn_y, z1, in_x = flip(attn_x, ALONG_Y), flip(joined, ALONG_Z), flip(in_half, ALONG_X)
-    y2, out_ax = flip(z2, ALONG_Y), flip(out_a, ALONG_X)
+    half = attn.shape[0] // 2
+    joined, attn_x, with_in, y0, z2 = sync(
+        "phase2",
+        meta,
+        [[both, z2], [(with_attn_x, 0, half)]],
+        [with_in, y0, z2],
+        [saved_near[6], in_core, out_core],
+    )
+    with_in_x, attn_y, z1 = flip(with_in, ALONG_X), flip(attn_x, ALONG_Y), flip(joined, ALONG_Z)
+    y2 = flip(z2, ALONG_Y)
     joined_c, y0_c = flip(joined, 1), flip(y0, 1)
-    attn_far, in_x, out_ax, out_b, z1, y2 = sync(
+    attn_far, in_x, out_a, out_2, z1, y2 = sync(
         "phase3",
         meta,
-        [[PAIR_Y, attn_x, attn_y]],
-        [in_x, out_ax, out_b, z1, y2],
-        [in_core, out_core, joined_c, y0_c],
+        [
+            [PAIR_Y, attn_x, attn_y],
+            [(with_in_x, 0, half)],
+            [(share, half, share.shape[0] - half) for share in (with_attn_x, with_in_x)],
+        ],
+        [out_2, z1, y2],
+        [joined_c, y0_c],
     )
     attn_far_c = flip(attn_far, 1)
-    y1, out_bx, in_z = flip(z1, ALONG_Y), flip(out_b, ALONG_X), flip(in_x, ALONG_Z)
-    z1_c, y2_c, out_ax_c = flip(z1, 1), flip(y2, 1), flip(out_ax, 1)
+    y1, out_b, in_z = flip(z1, ALONG_Y), flip(out_2, ALONG_X), flip(in_x, ALONG_Z)
+    z1_c, y2_c, out_a_c = flip(z1, 1), flip(y2, 1), flip(out_a, 1)
     *saved_far, first, normed1, inv_std1 = call_attend_forward(
         [], columns, True, meta, doc_lengths, tokens, saved_near[6], lines, (attn_far, attn_far_c)
     )
@@ -813,6 +836,7 @@
     own, other = 0, 1
     weights = assemble(
         "assemble",
+        [],
         meta,
         None,
         [
@@ -826,15 +850,18 @@
             (y2_c, ((1, 2),), other),
         ],
     )
-    in_far, out_bx, y1 = sync(
-        "phase4", meta, [[PAIR_Z, in_x, in_z]], [out_bx, y1], [sums, weights, out_ax_c]
-    )
-    in_far_c, out_bx_c, y1_c = flip(in_far, 1), flip(out_bx, 1), flip(y1, 1)
-    out_far = (out_ax, out_bx, out_ax_c, out_bx_c)
-    slope_far, sums = call_ffn_forward([], first, sums, (in_far, in_far_c), out_far)
+    in_far, out_b, y1 = sync(
+        "phase4", meta, [[PAIR_Z, in_x, in_z]], [out_b, y1], [sums, weights, out_a_c]
+    )
+    in_far_c, out_b_c, y1_c = flip(in_far, 1), flip(out_b, 1), flip(y1, 1)
+    out_far = (out_a, out_b, out_a_c, out_b_c)
+    slopes_far = []
+    for quarter, blocks in ((in_far, out_far[:2]), (in_far_c, out_far[2:])):
+        slope, sums = call_ffn_forward([], first, sums, (quarter,), blocks)
+        slopes_far.append(slope)
     last_parts = ((1, 1), (1, 3))
     weights = assemble(
-        "assemble_last", meta, weights, [(y1, last_parts, own), (y1_c, last_parts, other)]
+        "assemble_last", [sums], meta, weights, [(y1, last_parts, own), (y1_c, last_parts, other)]
     )
     layer_out, *parts, grad_keep, grad_send = call_merging(
         n_adapters, meta, doc_lengths, sums, lines, out_grad, weights
@@ -850,26 +877,37 @@
             )
         return token
 
-    def first_work(deps):
-        grad, low = call_merging_input(deps, sums, lines, *parts, weights)
-        done["low"] = low
+    def near(deps):
         (done["sum"],) = call_ffn_backward(
-            [], low, grad, slope_near, (ffn_in_weight, in_core), (ffn_out_weight, out_core)
+            deps,
+            done["low"],
+            done["sum"],
+            [slope_near],
+            (ffn_in_weight, in_core),
+            (ffn_out_weight, out_core),
         )
         return done["sum"]
 
-    def second_work(deps):
+    def far(deps):
         done["sum"], done["low"] = call_ffn_backward(
             deps,
             done["low"],
             done["sum"],
-            slope_far,
+            slopes_far,
             (in_far, in_far_c),
             out_far,
             normed1,
             inv_std1,
             lines,
         )
+
+    def first_work(deps):
+        done["sum"], done["low"] = call_merging_input(deps, sums, lines, *parts, weights)
+        return done["sum"]
+
+    def second_work(deps):
+        near(deps)
+        far([])
         return attention([], 0)
 
     works = (

time: 155 us -> 149 us (0.961)
  waiting for transfers between devices: 47.7 us -> 38.6 us
  starting transfers between devices: 27.8 us -> 30.8 us
    ppermute x33 -> x32, waiting for transfers between devices: 47.7 us -> 38.6 us  [flip(): return lax.ppermute(array, AXES, [(i, i ^ bits) for i in range(self.count)])]
    ppermute x33 -> x32, starting transfers between devices: 27.8 us -> 30.8 us  [flip(): return lax.ppermute(array, AXES, [(i, i ^ bits) for i in range(self.count)])]
    pallas_call x4, Pallas kernels: 16.3 us -> 14 us  [call_attend_backward(): kernel(functools.partial(attend_backward, columns), deps, ATTEND_MIB, in_...]
    pallas_call x7 -> x8, Pallas kernels: 17.8 us -> 19.6 us  [the longest x3 8.28 us: call_ffn_forward(): kernel(functools.partial(ffn_forward, quarters, len(out_quarters) // quar...]
  transfers between devices with their start and end apart: 33 -> 32, of which waited for: 12 -> 13; matrix products, arithmetic and copies ran while one was open for 0% -> 0% of each run, Pallas kernels for 34% -> 34%
where the time goes in v1:
time: 149 us
  Pallas kernels  77.7 us (52%)
  waiting for transfers between devices  38.6 us (26%)
  starting transfers between devices  30.8 us (21%)
    ppermute x32, waiting for transfers between devices, flip(): return lax.ppermute(array, AXES, [(i, i ^ bits) for i in range(self.count)])  38.6 us
    ppermute x32, starting transfers between devices, flip(): return lax.ppermute(array, AXES, [(i, i ^ bits) for i in range(self.count)])  30.8 us
    pallas_call x2, Pallas kernels, call_attend_forward(): kernel(functools.partial(attend_forward, columns, last), deps, ATTEND_MIB...  18.7 us
    pallas_call x1, Pallas kernels, call_merging(): pl.pallas_call(functools.partial(merging, n_adapters), in_specs=[SMEM, SM...  17.1 us
    pallas_call x4, Pallas kernels, call_attend_backward(): kernel(functools.partial(attend_backward, columns), deps, ATTEND_MIB, in_...  14 us
    pallas_call x3, Pallas kernels, call_ffn_forward(): kernel(functools.partial(ffn_forward, quarters, len(out_quarters) // quar...  8.28 us
    pallas_call x2, Pallas kernels, call_ffn_backward(): kernel(functools.partial(ffn_backward, last, len(out_quarters) // 2, len(...  6.8 us
  transfers between devices with their start and end apart: 32, of which 13 were waited for; matrix products, arithmetic and copies ran while one was open for 0% of the time, Pallas kernels for 34%

profile of v1, /device:TPU:0, one launch (start us, length us, event | category | flops | bytes accessed | tf_op | source)
XLA Modules:
  0.0 148.7 jit_solution(4092818725728751719)
XLA Ops:
  4.0 2.4 %prepare_frozen.1 = (bf16[768,768]{1,0:T(8,128)(2,1)S(1)}, bf16[512,768]{1,0:T(8,128)(2,1)S(1)}, bf16[512,768]{1,0:T(8,128)(2,1)S(1)}, bf16[512,768]{1,0:T(8,128...) custom-call(bf16[5,48,384]{2,1,0:T(8,128)(2,1)S(1)} %chip_tile.1.refs_0_.refs_5_, ...), custom_call_target="tpu_custom_call" | custom-call | bytes 1024 | tf_op jit(solution)/shard_map/prepare_frozen/pallas_call | solution.py:568
  6.8 2.6 %collective-permute-start.2 = (bf16[5,48,384]{2,1,0:T(8,128)(2,1)S(1)}, bf16[5,48,384]{2,1,0:T(8,128)(2,1)S(1)}, u32[]{:S(2)}, u32[]{:S(2)}) collective-permute-start(bf16[5,48,384]{2,1,0:T(8,128)(2,1)S(1)} %chip_tile.1.refs_0_.refs_5_), channel_id=1, source_target_pairs={{0,2},{1,3},{2,0},{3,1},{4,6},{5,7},{6,4},{7,5},{8,10},{9,11},{10,... | collective-permute-start | bytes 552968 | tf_op jit(solution)/shard_map/ppermute | solution.py:692
  9.4 5.1 %collective-permute-done.2.refs_6_ = bf16[5,48,384]{2,1,0:T(8,128)(2,1)S(1)} collective-permute-done((bf16[5,48,384]{2,1,0:T(8,128)(2,1)S(1)}, bf16[5,48,384]{2,1,0:T(8,128)(2,1)S(1)}, u32[]{:S(2)}, u32[]{:S(2)}) %collective-permute-start.2) | collective-permute-done | bytes 184352 | tf_op jit(solution)/shard_map/ppermute | solution.py:692
  15.8 1.7 %collective-permute-start.7 = (bf16[512,768]{1,0:T(8,128)(2,1)S(1)}, bf16[512,768]{1,0:T(8,128)(2,1)S(1)}, u32[]{:S(2)}, u32[]{:S(2)}) collective-permute-start(bf16[512,768]{1,0:T(8,128)(2,1)S(1)} %get-tuple-element.104), channel_id=1, source_target_pairs={{0,2},{1,3},{2,0},{3,1},{4,6},{5,7},{6,4},{7,5},{8,10},{9,11},{10,... | collective-permute-start | bytes 2359304 | tf_op jit(solution)/shard_map/ppermute | solution.py:692
  17.5 2.6 %collective-permute-start.6 = (bf16[10,48,384]{2,1,0:T(8,128)(2,1)S(1)}, bf16[10,48,384]{2,1,0:T(8,128)(2,1)S(1)}, u32[]{:S(2)}, u32[]{:S(2)}) collective-permute-start(bf16[10,48,384]{2,1,0:T(8,128)(2,1)S(1)} %get-tuple-element.98.refs_0_.refs_7_), channel_id=1, source_target_pairs={{0,16},{1,17},{2,18},{3,19},{4,20},{5,21},{6,22},{7,23},{8,24},{9,... | collective-permute-start | bytes 1105928 | tf_op jit(solution)/shard_map/ppermute | solution.py:692
  21.6 8.9 %attend_forward.2 = (bf16[576,512]{1,0:T(8,128)(2,1)}, bf16[192,512]{1,0:T(8,128)(2,1)}, bf16[3,512,512]{2,1,0:T(8,128)(2,1)}, bf16[576,512]{1,0:T(8,128)(2,1)},...) custom-call(bf16[10,48,384]{2,1,0:T(8,128)(2,1)S(1)} %get-tuple-element.98.refs_0_.refs_7_, ...), custom_call_target="tpu_custom_call" | custom-call | bytes 1024 | tf_op jit(solution)/shard_map/attend_forward/pallas_call | solution.py:192
  30.5 6.1 %collective-permute-done.6.refs_8_ = bf16[10,48,384]{2,1,0:T(8,128)(2,1)S(1)} collective-permute-done((bf16[10,48,384]{2,1,0:T(8,128)(2,1)S(1)}, bf16[10,48,384]{2,1,0:T(8,128)(2,1)S(1)}, u32[]{:S(2)}, u32[]{:S(2)}) %collective-permute-start.6) | collective-permute-done | bytes 368672 | tf_op jit(solution)/shard_map/ppermute | solution.py:692
  41.4 8.0 %collective-permute-done.11.refs_5_ = bf16[10,48,384]{2,1,0:T(8,128)(2,1)S(1)} collective-permute-done((bf16[10,48,384]{2,1,0:T(8,128)(2,1)S(1)}, bf16[10,48,384]{2,1,0:T(8,128)(2,1)S(1)}, u32[]{:S(2)}, u32[]{:S(2)}) %collective-permute-start.11) | collective-permute-done | bytes 368672 | tf_op jit(solution)/shard_map/ppermute | solution.py:692
  49.4 1.7 %collective-permute-done.9.refs_1_.refs_6_ = bf16[10,48,384]{2,1,0:T(8,128)(2,1)S(1)} collective-permute-done((bf16[10,48,384]{2,1,0:T(8,128)(2,1)S(1)}, bf16[10,48,384]{2,1,0:T(8,128)(2,1)S(1)}, u32[]{:S(2)}, u32[]{:S(2)}) %collective-permute-start.9) | collective-permute-done | bytes 368672 | tf_op jit(solution)/shard_map/ppermute | solution.py:692
  51.1 8.8 %collective-permute-done.12.refs_7_ = bf16[384,768]{1,0:T(8,128)(2,1)S(1)} collective-permute-done((bf16[384,768]{1,0:T(8,128)(2,1)S(1)}, bf16[384,768]{1,0:T(8,128)(2,1)S(1)}, u32[]{:S(2)}, u32[]{:S(2)}) %collective-permute-start.12) | collective-permute-done | bytes 589856 | tf_op jit(solution)/shard_map/ppermute | solution.py:692
  68.1 9.7 %attend_forward.3 = (bf16[576,512]{1,0:T(8,128)(2,1)}, bf16[192,512]{1,0:T(8,128)(2,1)}, bf16[3,512,512]{2,1,0:T(8,128)(2,1)}, bf16[576,512]{1,0:T(8,128)(2,1)},...) custom-call(s32[6]{0:T(128)S(1)} %stack.27.meta.refs_0_.refs_1_.refs, ...), custom_call_target="tpu_custom_call" | custom-call | bytes 1024 | tf_op jit(solution)/shard_map/attend_forward/pallas_call | solution.py:192
  77.8 3.5 %ffn_forward.3 = (bf16[2,512,768]{2,1,0:T(8,128)(2,1)S(1)}, f32[512,768]{1,0:T(8,128)S(1)}) custom-call(f32[512,768]{1,0:T(8,128)S(1)} %get-tuple-element.112.refs_0_.refs_1_, f32[512,768]{1,0:T(8,128)S(1)} %get-tuple-element.112.refs_0_.refs_1_, bf16[768,768]{1,0:T(8,128)(2,1)S(1)} %copy-done, ...), custom_call_target="tpu_custom_call" | custom-call | bytes 1024 | tf_op jit(solution)/shard_map/ffn_forward/pallas_call | solution.py:230
  83.0 2.4 %ffn_forward.4 = (bf16[1,512,768]{2,1,0:T(8,128)(2,1)S(1)}, f32[512,768]{1,0:T(8,128)S(1)}) custom-call(f32[512,768]{1,0:T(8,128)S(1)} %get-tuple-element.112.refs_0_.refs_1_, f32[512,768]{1,0:T(8,128)S(1)} %get-tuple-element.113.refs_0_.refs_1_, bf16[768,768]{1,0:T(8,128)(2,1)S(1)} %get-tuple-element.119.refs_2_.refs_4_, ...), custom_call_target="tpu_custom_call" | custom-call | bytes 1024 | tf_op jit(solution)/shard_map/ffn_forward/pallas_call | solution.py:230
  86.1 2.4 %ffn_forward.5 = (bf16[1,512,768]{2,1,0:T(8,128)(2,1)S(1)}, f32[512,768]{1,0:T(8,128)S(1)}) custom-call(f32[512,768]{1,0:T(8,128)S(1)} %get-tuple-element.112.refs_0_.refs_1_, f32[512,768]{1,0:T(8,128)S(1)} %get-tuple-element.121.refs_1_, bf16[768,768]{1,0:T(8,128)(2,1)S(1)} %collective-permute-done.21.refs_2_.refs_5_, ...), custom_call_target="tpu_custom_call" | custom-call | bytes 1024 | tf_op jit(solution)/shard_map/ffn_forward/pallas_call | solution.py:230
  89.7 17.1 %merging.1 = (f32[512,768]{1,0:T(8,128)}, f32[512,768]{1,0:T(8,128)S(1)}, bf16[512,768]{1,0:T(8,128)(2,1)S(1)}, bf16[512,768]{1,0:T(8,128)(2,1)S(1)}, bf16[2,2,4...) custom-call(s32[6]{0:T(128)S(1)} %stack.27.meta.refs_0_.refs_1_.refs_3_.refs_2_, ...), custom_call_target="tpu_custom_call" | custom-call | bytes 1024 | tf_op jit(solution)/shard_map/merging/pallas_call | solution.py:394
  107.2 2.1 %merging_input.1 = (f32[512,768]{1,0:T(8,128)S(1)}, bf16[512,768]{1,0:T(8,128)(2,1)S(1)}) custom-call(f32[512,768]{1,0:T(8,128)S(1)} %get-tuple-element.122.refs_0_.sums, f32[8,768]{1,0:T(8,128)S(1)} %get-tuple-element.99.refs_5_.refs_4_.lines.refs_1_.refs_12_, f32[512,768]{1,0:T(8,128)S(1)} %get-tuple-element.125.refs_2_, ...), custom_call_target="tpu_custom_call" | custom-call | bytes 1024 | tf_op jit(solution)/shard_map/merging_input/pallas_call | solution.py:422
  114.6 3.1 %ffn_backward.2.refs_1_ = f32[512,768]{1,0:T(8,128)S(1)} custom-call(bf16[2,4,80,384]{3,2,1,0:T(8,128)(2,1)S(1)} %get-tuple-element.132.refs_0_.refs_1_, bf16[512,768]{1,0:T(8,128)(2,1)S(1)} %get-tuple-element.128.refs_1_.refs_0_, f32[512,768]{1,0:T(8,128)S(1)} %get-tuple-element.129.refs_0_.refs_2_, bf16[2,512,768]{2,1,0:T(8,128)(2,1)S(1)} %get-tuple-element.133.refs_3_, ...), custom_call_target="tpu_custom_call" | custom-call | bytes 1024 | tf_op jit(solution)/shard_map/ffn_backward/pallas_call | solution.py:462
  117.7 3.7 %ffn_backward.3 = (f32[512,768]{1,0:T(8,128)S(1)}, bf16[512,768]{1,0:T(8,128)(2,1)S(1)}) custom-call(bf16[512,768]{1,0:T(8,128)(2,1)S(1)} %get-tuple-element.128.refs_1_.refs_0_, f32[512,768]{1,0:T(8,128)S(1)} %ffn_backward.2.refs_1_, bf16[1,512,768]{2,1,0:T(8,128)(2,1)S(1)} %get-tuple-element.134.refs_2_, ...), custom_call_target="tpu_custom_call" | custom-call | bytes 1024 | tf_op jit(solution)/shard_map/ffn_backward/pallas_call | solution.py:462
  121.5 3.1 %attend_backward.4 = (f32[512,768]{1,0:T(8,128)S(1)}, f32[8,128]{1,0:T(8,128)S(1)}) custom-call(bf16[512,768]{1,0:T(8,128)(2,1)S(1)} %get-tuple-element.138.refs_0_.refs_1_, f32[512,768]{1,0:T(8,128)S(1)} %get-tuple-element.139.refs_1_, bf16[576,512]{1,0:T(8,128)(2,1)S(1)} %copy-done.9, bf16[192,512]{1,0:T(8,128)(2,1)S(1)} %copy-done.13, ...), custom_call_target="tpu_custom_call" | custom-call | bytes 1024 | tf_op jit(solution)/shard_map/attend_backward/pallas_call | solution.py:502
  128.8 3.1 %attend_backward.5 = (f32[512,768]{1,0:T(8,128)S(1)}, f32[8,128]{1,0:T(8,128)S(1)}) custom-call(bf16[4,80,384]{2,1,0:T(8,128)(2,1)S(1)} %get-tuple-element.147.refs_0_.refs_1_, bf16[512,768]{1,0:T(8,128)(2,1)S(1)} %get-tuple-element.138.refs_0_.refs_1_, f32[512,768]{1,0:T(8,128)S(1)} %get-tuple-element.148.refs_2_, bf16[576,512]{1,0:T(8,128)(2,1)S(1)} %copy-done.8, ...), custom_call_target="tpu_custom_call" | custom-call | bytes 1024 | tf_op jit(solution)/shard_map/attend_backward/pallas_call | solution.py:502
  131.9 1.9 %collective-permute-done.27.refs_2_ = bf16[4,80,384]{2,1,0:T(8,128)(2,1)S(1)} collective-permute-done((bf16[4,80,384]{2,1,0:T(8,128)(2,1)S(1)}, bf16[4,80,384]{2,1,0:T(8,128)(2,1)S(1)}, u32[]{:S(2)}, u32[]{:S(2)}) %collective-permute-start.27) | collective-permute-done | bytes 245792 | tf_op jit(solution)/shard_map/ppermute | solution.py:692
  136.0 3.4 %collective-permute-start.30 = (bf16[80,768]{1,0:T(8,128)(2,1)S(1)}, bf16[80,768]{1,0:T(8,128)(2,1)S(1)}, u32[]{:S(2)}, u32[]{:S(2)}) collective-permute-start(bf16[80,768]{1,0:T(8,128)(2,1)S(1)} %get-tuple-element.168), channel_id=1, source_target_pairs={{0,16},{1,17},{2,18},{3,19},{4,20},{5,21},{6,22},{7,23},{8,24},{9,... | collective-permute-start | bytes 368648 | tf_op jit(solution)/shard_map/ppermute | solution.py:692
  140.1 3.6 %attend_backward.6 = (f32[512,768]{1,0:T(8,128)S(1)}, f32[8,128]{1,0:T(8,128)}) custom-call(bf16[80,768]{1,0:T(8,128)(2,1)S(1)} %get-tuple-element.156.refs_0_.refs_1_, bf16[512,768]{1,0:T(8,128)(2,1)S(1)} %get-tuple-element.138.refs_0_.refs_1_, f32[512,768]{1,0:T(8,128)S(1)} %get-tuple-element.157.refs_2_, bf16[576,512]{1,0:T(8,128)(2,1)S(1)} %copy-done.11, ...), custom_call_target="tpu_custom_call" | custom-call | bytes 1024 | tf_op jit(solution)/shard_map/attend_backward/pallas_call | solution.py:502
  143.7 4.2 %attend_backward.7 = (f32[512,768]{1,0:T(8,128)}, f32[8,128]{1,0:T(8,128)S(1)}) custom-call(bf16[80,768]{1,0:T(8,128)(2,1)S(1)} %get-tuple-element.156.refs_0_.refs_1_, bf16[512,768]{1,0:T(8,128)(2,1)S(1)} %get-tuple-element.138.refs_0_.refs_1_, f32[512,768]{1,0:T(8,128)S(1)} %get-tuple-element.161.refs_2_, bf16[576,512]{1,0:T(8,128)(2,1)S(1)} %copy-done.10, ...), custom_call_target="tpu_custom_call" | custom-call | bytes 1024 | tf_op jit(solution)/shard_map/attend_backward/pallas_call | solution.py:502
  (102 shorter events, 36.3 us)
Async XLA Ops:
  6.4 8.2 %collective-permute-start.1 = (bf16[768,768]{1,0:T(8,128)(2,1)S(1)}, bf16[768,768]{1,0:T(8,128)(2,1)S(1)}, u32[]{:S(2)}, u32[]{:S(2)}) collective-permute-start(bf16[768,768]{1,0:T(8,128)(2,1)S(1)} %get-tuple-element.94.refs_6_.refs_5_), channel_id=1, source_target_pairs={{0,1},{1,0},{2,3},{3,2},{4,5},{5,4},{6,7},{7,6},{8,9},{9,8},{10,11... | collective-permute-start | bytes 3538952 | tf_op jit(solution)/shard_map/ppermute | solution.py:692
  6.8 7.8 %collective-permute-start.2 = (bf16[5,48,384]{2,1,0:T(8,128)(2,1)S(1)}, bf16[5,48,384]{2,1,0:T(8,128)(2,1)S(1)}, u32[]{:S(2)}, u32[]{:S(2)}) collective-permute-start(bf16[5,48,384]{2,1,0:T(8,128)(2,1)S(1)} %chip_tile.1.refs_0_.refs_5_), channel_id=1, source_target_pairs={{0,2},{1,3},{2,0},{3,1},{4,6},{5,7},{6,4},{7,5},{8,10},{9,11},{10,... | collective-permute-start | bytes 552968 | tf_op jit(solution)/shard_map/ppermute | solution.py:692
  15.2 21.5 %collective-permute-start.3 = (bf16[768,768]{1,0:T(8,128)(2,1)S(1)}, bf16[768,768]{1,0:T(8,128)(2,1)S(1)}, u32[]{:S(2)}, u32[]{:S(2)}) collective-permute-start(bf16[768,768]{1,0:T(8,128)(2,1)S(1)} %get-tuple-element.101), channel_id=1, source_target_pairs={{0,1},{1,0},{2,3},{3,2},{4,5},{5,4},{6,7},{7,6},{8,9},{9,8},{10,11... | collective-permute-start | bytes 3538952 | tf_op jit(solution)/shard_map/ppermute | solution.py:692
  15.3 21.4 %collective-permute-start.4 = (bf16[768,768]{1,0:T(8,128)(2,1)S(1)}, bf16[768,768]{1,0:T(8,128)(2,1)S(1)}, u32[]{:S(2)}, u32[]{:S(2)}) collective-permute-start(bf16[768,768]{1,0:T(8,128)(2,1)S(1)} %get-tuple-element.102), channel_id=1, source_target_pairs={{0,1},{1,0},{2,3},{3,2},{4,5},{5,4},{6,7},{7,6},{8,9},{9,8},{10,11... | collective-permute-start | bytes 3538952 | tf_op jit(solution)/shard_map/ppermute | solution.py:692
  15.8 20.9 %collective-permute-start.7 = (bf16[512,768]{1,0:T(8,128)(2,1)S(1)}, bf16[512,768]{1,0:T(8,128)(2,1)S(1)}, u32[]{:S(2)}, u32[]{:S(2)}) collective-permute-start(bf16[512,768]{1,0:T(8,128)(2,1)S(1)} %get-tuple-element.104), channel_id=1, source_target_pairs={{0,2},{1,3},{2,0},{3,1},{4,6},{5,7},{6,4},{7,5},{8,10},{9,11},{10,... | collective-permute-start | bytes 2359304 | tf_op jit(solution)/shard_map/ppermute | solution.py:692
  17.5 19.1 %collective-permute-start.6 = (bf16[10,48,384]{2,1,0:T(8,128)(2,1)S(1)}, bf16[10,48,384]{2,1,0:T(8,128)(2,1)S(1)}, u32[]{:S(2)}, u32[]{:S(2)}) collective-permute-start(bf16[10,48,384]{2,1,0:T(8,128)(2,1)S(1)} %get-tuple-element.98.refs_0_.refs_7_), channel_id=1, source_target_pairs={{0,16},{1,17},{2,18},{3,19},{4,20},{5,21},{6,22},{7,23},{8,24},{9,... | collective-permute-start | bytes 1105928 | tf_op jit(solution)/shard_map/ppermute | solution.py:692
  20.1 16.5 %collective-permute-start.5 = (bf16[10,48,384]{2,1,0:T(8,128)(2,1)S(1)}, bf16[10,48,384]{2,1,0:T(8,128)(2,1)S(1)}, u32[]{:S(2)}, u32[]{:S(2)}) collective-permute-start(bf16[10,48,384]{2,1,0:T(8,128)(2,1)S(1)} %get-tuple-element.98.refs_0_.refs_7_), channel_id=1, source_target_pairs={{0,4},{1,5},{2,6},{3,7},{4,0},{5,1},{6,2},{7,3},{8,12},{9,13},{10,... | collective-permute-start | bytes 1105928 | tf_op jit(solution)/shard_map/ppermute | solution.py:692
  37.3 22.6 %collective-permute-start.13 = (bf16[512,768]{1,0:T(8,128)(2,1)S(1)}, bf16[512,768]{1,0:T(8,128)(2,1)S(1)}, u32[]{:S(2)}, u32[]{:S(2)}) collective-permute-start(bf16[512,768]{1,0:T(8,128)(2,1)S(1)} %get-tuple-element.110), channel_id=1, source_target_pairs={{0,2},{1,3},{2,0},{3,1},{4,6},{5,7},{6,4},{7,5},{8,10},{9,11},{10,... | collective-permute-start | bytes 2359304 | tf_op jit(solution)/shard_map/ppermute | solution.py:692
  37.9 11.5 %collective-permute-start.11 = (bf16[10,48,384]{2,1,0:T(8,128)(2,1)S(1)}, bf16[10,48,384]{2,1,0:T(8,128)(2,1)S(1)}, u32[]{:S(2)}, u32[]{:S(2)}) collective-permute-start(bf16[10,48,384]{2,1,0:T(8,128)(2,1)S(1)} %get-tuple-element.108), channel_id=1, source_target_pairs={{0,4},{1,5},{2,6},{3,7},{4,0},{5,1},{6,2},{7,3},{8,12},{9,13},{10,... | collective-permute-start | bytes 1105928 | tf_op jit(solution)/shard_map/ppermute | solution.py:692
  39.4 20.4 %collective-permute-start.10 = (bf16[20,48,384]{2,1,0:T(8,128)(2,1)S(1)}, bf16[20,48,384]{2,1,0:T(8,128)(2,1)S(1)}, u32[]{:S(2)}, u32[]{:S(2)}) collective-permute-start(bf16[20,48,384]{2,1,0:T(8,128)(2,1)S(1)} %get-tuple-element.105.refs_1_), channel_id=1, source_target_pairs={{0,8},{1,9},{2,10},{3,11},{4,12},{5,13},{6,14},{7,15},{8,0},{9,1},... | collective-permute-start | bytes 2211848 | tf_op jit(solution)/shard_map/ppermute | solution.py:692
  40.8 19.0 %collective-permute-start.8 = (bf16[20,48,384]{2,1,0:T(8,128)(2,1)S(1)}, bf16[20,48,384]{2,1,0:T(8,128)(2,1)S(1)}, u32[]{:S(2)}, u32[]{:S(2)}) collective-permute-start(bf16[20,48,384]{2,1,0:T(8,128)(2,1)S(1)} %get-tuple-element.105.refs_1_), channel_id=1, source_target_pairs={{0,1},{1,0},{2,3},{3,2},{4,5},{5,4},{6,7},{7,6},{8,9},{9,8},{10,11... | collective-permute-start | bytes 2211848 | tf_op jit(solution)/shard_map/ppermute | solution.py:692
  40.8 19.0 %collective-permute-start.12 = (bf16[384,768]{1,0:T(8,128)(2,1)S(1)}, bf16[384,768]{1,0:T(8,128)(2,1)S(1)}, u32[]{:S(2)}, u32[]{:S(2)}) collective-permute-start(bf16[384,768]{1,0:T(8,128)(2,1)S(1)} %get-tuple-element.109.refs_6_), channel_id=1, source_target_pairs={{0,4},{1,5},{2,6},{3,7},{4,0},{5,1},{6,2},{7,3},{8,12},{9,13},{10,... | collective-permute-start | bytes 1769480 | tf_op jit(solution)/shard_map/ppermute | solution.py:692
  60.6 7.5 %collective-permute-start.14 = (bf16[768,768]{1,0:T(8,128)(2,1)S(1)}, bf16[768,768]{1,0:T(8,128)(2,1)S(1)}, u32[]{:S(2)}, u32[]{:S(2)}) collective-permute-start(bf16[768,768]{1,0:T(8,128)(2,1)S(1)} %get-tuple-element.111.refs_5_.refs_6_), channel_id=1, source_target_pairs={{0,1},{1,0},{2,3},{3,2},{4,5},{5,4},{6,7},{7,6},{8,9},{9,8},{10,11... | collective-permute-start | bytes 3538952 | tf_op jit(solution)/shard_map/ppermute | solution.py:692
  61.2 20.1 %collective-permute-start.18 = (bf16[512,768]{1,0:T(8,128)(2,1)S(1)}, bf16[512,768]{1,0:T(8,128)(2,1)S(1)}, u32[]{:S(2)}, u32[]{:S(2)}) collective-permute-start(bf16[512,768]{1,0:T(8,128)(2,1)S(1)} %get-tuple-element.117), channel_id=1, source_target_pairs={{0,2},{1,3},{2,0},{3,1},{4,6},{5,7},{6,4},{7,5},{8,10},{9,11},{10,... | collective-permute-start | bytes 2359304 | tf_op jit(solution)/shard_map/ppermute | solution.py:692
  62.6 18.7 %collective-permute-start.19 = (bf16[20,48,384]{2,1,0:T(8,128)(2,1)S(1)}, bf16[20,48,384]{2,1,0:T(8,128)(2,1)S(1)}, u32[]{:S(2)}, u32[]{:S(2)}) collective-permute-start(bf16[20,48,384]{2,1,0:T(8,128)(2,1)S(1)} %get-tuple-element.114.refs_3_), channel_id=1, source_target_pairs={{0,4},{1,5},{2,6},{3,7},{4,0},{5,1},{6,2},{7,3},{8,12},{9,13},{10,... | collective-permute-start | bytes 2211848 | tf_op jit(solution)/shard_map/ppermute | solution.py:692
  65.1 16.2 %collective-permute-start.20 = (bf16[384,768]{1,0:T(8,128)(2,1)S(1)}, bf16[384,768]{1,0:T(8,128)(2,1)S(1)}, u32[]{:S(2)}, u32[]{:S(2)}) collective-permute-start(bf16[384,768]{1,0:T(8,128)(2,1)S(1)} %get-tuple-element.118.refs_6_), channel_id=1, source_target_pairs={{0,8},{1,9},{2,10},{3,11},{4,12},{5,13},{6,14},{7,15},{8,0},{9,1},... | collective-permute-start | bytes 1769480 | tf_op jit(solution)/shard_map/ppermute | solution.py:692
  66.7 14.6 %collective-permute-start.17 = (bf16[256,768]{1,0:T(8,128)(2,1)S(1)}, bf16[256,768]{1,0:T(8,128)(2,1)S(1)}, u32[]{:S(2)}, u32[]{:S(2)}) collective-permute-start(bf16[256,768]{1,0:T(8,128)(2,1)S(1)} %get-tuple-element.116.refs_3_.refs_6_), channel_id=1, source_target_pairs={{0,1},{1,0},{2,3},{3,2},{4,5},{5,4},{6,7},{7,6},{8,9},{9,8},{10,11... | collective-permute-start | bytes 1179656 | tf_op jit(solution)/shard_map/ppermute | solution.py:692
  111.5 13.6 %collective-permute-start.25 = (bf16[2,4,80,384]{3,2,1,0:T(8,128)(2,1)S(1)}, bf16[2,4,80,384]{3,2,1,0:T(8,128)(2,1)S(1)}, u32[]{:S(2)}, u32[]{:S(2)}) collective-permute-start(bf16[2,4,80,384]{3,2,1,0:T(8,128)(2,1)S(1)} %get-tuple-element.144), channel_id=1, source_target_pairs={{0,2},{1,3},{2,0},{3,1},{4,6},{5,7},{6,4},{7,5},{8,10},{9,11},{10,... | collective-permute-start | bytes 1474568 | tf_op jit(solution)/shard_map/ppermute | solution.py:692
  113.1 13.2 %collective-permute-start.26 = (bf16[2,4,80,384]{3,2,1,0:T(8,128)(2,1)S(1)}, bf16[2,4,80,384]{3,2,1,0:T(8,128)(2,1)S(1)}, u32[]{:S(2)}, u32[]{:S(2)}) collective-permute-start(bf16[2,4,80,384]{3,2,1,0:T(8,128)(2,1)S(1)} %get-tuple-element.146), channel_id=1, source_target_pairs={{0,4},{1,5},{2,6},{3,7},{4,0},{5,1},{6,2},{7,3},{8,12},{9,13},{10,... | collective-permute-start | bytes 1474568 | tf_op jit(solution)/shard_map/ppermute | solution.py:692
  126.6 7.2 %collective-permute-start.27 = (bf16[4,80,384]{2,1,0:T(8,128)(2,1)S(1)}, bf16[4,80,384]{2,1,0:T(8,128)(2,1)S(1)}, u32[]{:S(2)}, u32[]{:S(2)}) collective-permute-start(bf16[4,80,384]{2,1,0:T(8,128)(2,1)S(1)} %get-tuple-element.153), channel_id=1, source_target_pairs={{0,4},{1,5},{2,6},{3,7},{4,0},{5,1},{6,2},{7,3},{8,12},{9,13},{10,... | collective-permute-start | bytes 737288 | tf_op jit(solution)/shard_map/ppermute | solution.py:692
  128.2 6.8 %collective-permute-start.28 = (bf16[4,80,384]{2,1,0:T(8,128)(2,1)S(1)}, bf16[4,80,384]{2,1,0:T(8,128)(2,1)S(1)}, u32[]{:S(2)}, u32[]{:S(2)}) collective-permute-start(bf16[4,80,384]{2,1,0:T(8,128)(2,1)S(1)} %get-tuple-element.155), channel_id=1, source_target_pairs={{0,2},{1,3},{2,0},{3,1},{4,6},{5,7},{6,4},{7,5},{8,10},{9,11},{10,... | collective-permute-start | bytes 737288 | tf_op jit(solution)/shard_map/ppermute | solution.py:692
  135.2 12.8 %collective-permute-start.29 = (bf16[80,768]{1,0:T(8,128)(2,1)S(1)}, bf16[80,768]{1,0:T(8,128)(2,1)S(1)}, u32[]{:S(2)}, u32[]{:S(2)}) collective-permute-start(bf16[80,768]{1,0:T(8,128)(2,1)S(1)} %get-tuple-element.167), channel_id=1, source_target_pairs={{0,8},{1,9},{2,10},{3,11},{4,12},{5,13},{6,14},{7,15},{8,0},{9,1},... | collective-permute-start | bytes 368648 | tf_op jit(solution)/shard_map/ppermute | solution.py:692
  136.0 11.9 %collective-permute-start.30 = (bf16[80,768]{1,0:T(8,128)(2,1)S(1)}, bf16[80,768]{1,0:T(8,128)(2,1)S(1)}, u32[]{:S(2)}, u32[]{:S(2)}) collective-permute-start(bf16[80,768]{1,0:T(8,128)(2,1)S(1)} %get-tuple-element.168), channel_id=1, source_target_pairs={{0,16},{1,17},{2,18},{3,19},{4,20},{5,21},{6,22},{7,23},{8,24},{9,... | collective-permute-start | bytes 368648 | tf_op jit(solution)/shard_map/ppermute | solution.py:692
  139.4 8.6 %collective-permute-start.31 = (bf16[80,768]{1,0:T(8,128)(2,1)S(1)}, bf16[80,768]{1,0:T(8,128)(2,1)S(1)}, u32[]{:S(2)}, u32[]{:S(2)}) collective-permute-start(bf16[80,768]{1,0:T(8,128)(2,1)S(1)} %get-tuple-element.169), channel_id=1, source_target_pairs={{0,24},{1,25},{2,26},{3,27},{4,28},{5,29},{6,30},{7,31},{8,16},{9,... | collective-permute-start | bytes 368648 | tf_op jit(solution)/shard_map/ppermute | solution.py:692
  (25 other events, 137.2 us)

commit v2 on v1

--- a/solution.py
+++ b/solution.py
@@ -9,7 +9,7 @@
 
 HEAD_DIM = 64
 AXES = ("dp", "tensor")
-ATTEND_MIB, FFN_MIB, MERGE_MIB = 16, 16, 22
+ATTEND_MIB, FFN_MIB, MERGE_MIB = 16, 16, 24
 LANES = 128
 COST = 0.0
 CHUNK = 256
@@ -28,10 +28,10 @@
 HBM = pl.BlockSpec(memory_space=pltpu.HBM)
 
 
-def by_chunks(count, body):
-    @pl.loop(0, count // CHUNK)
+def by_chunks(count, body, size=CHUNK):
+    @pl.loop(0, count // size)
     def _(i):
-        body(pl.ds(pl.multiple_of(i * CHUNK, CHUNK), CHUNK))
+        body(pl.ds(pl.multiple_of(i * size, size), size))
 
 
 def line_of(lines, i):
@@ -184,10 +184,11 @@
     heads = columns // (3 * HEAD_DIM)
     inner = heads * HEAD_DIM
     square, narrow = sds((seq, width), F32), sds((seq, 1), F32)
+    place = pltpu.HBM
     out_shape = [
-        pltpu.HBM((columns, seq), BF16),
-        pltpu.HBM((inner, seq), BF16),
-        pltpu.HBM((heads, seq, seq), BF16),
+        place((columns, seq), BF16),
+        place((inner, seq), BF16),
+        place((heads, seq, seq), BF16),
     ] * 2 + [square] + [square, narrow] * last
     return kernel(
         functools.partial(attend_forward, columns, last),
@@ -334,7 +335,7 @@
         normed3, inv_std3 = normalize(second + dot(blended, value[...]))
         layer_out[rows] = normed3 * gain3 + shift3
 
-        token = rows.start + lax.broadcasted_iota(jnp.int32, (CHUNK, 1), 0)
+        token = rows.start + lax.broadcasted_iota(jnp.int32, (rows.size, 1), 0)
         keep = jnp.where(token < count, 1.0, 0.0)
         cot = out_grad[rows].astype(F32) * keep
         mass = jnp.sum(mix * keep, axis=0, keepdims=True)
@@ -365,7 +366,7 @@
             grad_pre + grad_blend.astype(F32) * mix_sum + probe.astype(F32) * (scale * logit_sum)
         )
 
-    by_chunks(seq, chunk)
+    by_chunks(seq, chunk, seq)
 
     @pl.loop(0, width // CHUNK)
     def _(i):
@@ -472,13 +473,13 @@
 
 
 def attend_backward(
-    columns, grad_low, before, turned_ref, att_ref, prob_ref, weight, input_grad, token, grad_turned, grad_att
+    columns, unroll, grad_low, before, turned_ref, att_ref, prob_ref, weight, input_grad, token, grad_turned, grad_att
 ):
     width = 3 * HEAD_DIM
     root = HEAD_DIM**-0.5
     grad_att[...] = dot_last(weight[columns:], grad_low[...]).astype(BF16)
 
-    @pl.loop(0, columns // width, unroll=True)
+    @pl.loop(0, columns // width, unroll=unroll)
     def _(head):
         base = pl.multiple_of(head * width, width)
         places = [pl.ds(base + i * HEAD_DIM, HEAD_DIM) for i in range(3)]
@@ -496,11 +497,11 @@
     token[...] = jnp.zeros_like(token)
 
 
-def call_attend_backward(deps, columns, grad_low, before, saved, quarter):
+def call_attend_backward(deps, columns, unroll, grad_low, before, saved, quarter):
     seq, width = before.shape
     inner = columns // 3
     return kernel(
-        functools.partial(attend_backward, columns),
+        functools.partial(attend_backward, columns, unroll),
         deps,
         ATTEND_MIB,
         in_specs=[VMEM] * 6,
@@ -548,22 +549,27 @@
     columns = qkv_turned.shape[0]
     attn[:columns] = qkv_turned[...]
     attn[columns:] = attn_out[...]
-    row = 0
-    for entry, whole, share in ((PAIR_Y, attn, with_attn), (PAIR_Z, into, with_in)):
-        half = whole.shape[0] // 2
-        cut = share.shape[0] - half
-        share[:half] = whole[pl.ds(pl.multiple_of(meta[entry] * half, 16), half)]
-        share[half:] = out[row : row + cut]
-        row += cut
-    out_last[...] = out[row:]
+    half = attn.shape[0] // 2
+    more = half // 3
+    mine = pl.multiple_of(meta[PAIR_Y] * half, 16)
+    other = pl.multiple_of((1 - meta[PAIR_Y]) * half + 2 * more, 16)
+    with_attn[:half] = attn[pl.ds(mine, half)]
+    with_attn[half : half + more] = attn[pl.ds(other, more)]
+    cut = with_attn.shape[0] - half - more
+    with_attn[half + more :] = out[:cut]
+    half = into.shape[0] // 2
+    with_in[:half] = into[pl.ds(pl.multiple_of(meta[PAIR_Z] * half, 16), half)]
+    end = cut + with_in.shape[0] - half
+    with_in[half:] = out[cut:end]
+    out_last[...] = out[end:]
     for source, copy in zip((into, out), copies):
         copy[...] = source[...]
 
 
 def call_prepare_frozen(deps, meta, qkv_turned, attn_out, into, out):
     rows, width = qkv_turned.shape[0] + attn_out.shape[0], attn_out.shape[1]
-    cut = out.shape[0] // 6
-    shares = (rows, rows // 2 + cut, into.shape[0] // 2 + cut, out.shape[0] - 2 * cut)
+    unit = out.shape[0] // 12
+    shares = (rows, rows // 2 + rows // 6 + unit, into.shape[0] // 2 + 3 * unit, 8 * unit)
     shares = shares + (into.shape[0], out.shape[0])
     return kernel(
         prepare_frozen,
@@ -734,7 +740,7 @@
         )
     (low,) = rest
     for quarter, kept in zip(attn, saved):
-        total, _ = call_attend_backward([], columns, low, total, kept, quarter)
+        total, _ = call_attend_backward([], columns, False, low, total, kept, quarter)
     mass = totals[2, :n_adapters] / totals[2, n_adapters]
     return (layer_out, total, squares[0], squares[1], squares[2], totals[0], totals[1], mass)
 
@@ -803,10 +809,11 @@
         [both], columns, False, meta, doc_lengths, tokens, tokens, lines, (attn, attn_core)
     )
     half = attn.shape[0] // 2
+    third = half // 3
     joined, attn_x, with_in, y0, z2 = sync(
         "phase2",
         meta,
-        [[both, z2], [(with_attn_x, 0, half)]],
+        [[both, z2], [(with_attn_x, 0, 2 * third)]],
         [with_in, y0, z2],
         [saved_near[6], in_core, out_core],
     )
@@ -817,9 +824,14 @@
         "phase3",
         meta,
         [
-            [PAIR_Y, attn_x, attn_y],
+            [PAIR_Y]
+            + [(with_attn_x, i * third, third) for i in range(3)]
+            + [(attn_y, 0, third), (attn_y, third, third), (with_attn_x, half, third)],
             [(with_in_x, 0, half)],
-            [(share, half, share.shape[0] - half) for share in (with_attn_x, with_in_x)],
+            [
+                (share, start, share.shape[0] - start)
+                for share, start in ((with_attn_x, half + third), (with_in_x, half))
+            ],
         ],
         [out_2, z1, y2],
         [joined_c, y0_c],
@@ -836,7 +848,7 @@
     own, other = 0, 1
     weights = assemble(
         "assemble",
-        [],
+        [first],
         meta,
         None,
         [
@@ -873,7 +885,7 @@
     def attention(deps, *quarters):
         for i in quarters:
             done["sum"], token = call_attend_backward(
-                deps, columns, done["low"], done["sum"], saved[i], attn_quarters[i]
+                deps, columns, i > 1, done["low"], done["sum"], saved[i], attn_quarters[i]
             )
         return token
 

time: 149 us -> 144 us (0.966)
  waiting for transfers between devices: 38.6 us -> 34.7 us
    ppermute x32, waiting for transfers between devices: 38.6 us -> 34.7 us  [flip(): return lax.ppermute(array, AXES, [(i, i ^ bits) for i in range(self.count)])]
    pallas_call x1, Pallas kernels: 17.1 us -> 15.1 us  [call_merging(): pl.pallas_call(functools.partial(merging, n_adapters), in_specs=[SMEM, SM...]
  transfers between devices with their start and end apart: 32 -> 32, of which waited for: 13 -> 16; matrix products, arithmetic and copies ran while one was open for 0% -> 0% of each run, Pallas kernels for 34% -> 36%
where the time goes in v2:
time: 144 us
  Pallas kernels  76.9 us (53%)
  waiting for transfers between devices  34.7 us (24%)
  starting transfers between devices  31.3 us (22%)
    ppermute x32, waiting for transfers between devices, flip(): return lax.ppermute(array, AXES, [(i, i ^ bits) for i in range(self.count)])  34.7 us
    ppermute x32, starting transfers between devices, flip(): return lax.ppermute(array, AXES, [(i, i ^ bits) for i in range(self.count)])  31.3 us
    pallas_call x2, Pallas kernels, call_attend_forward(): kernel(functools.partial(attend_forward, columns, last), deps, ATTEND_MIB...  18.7 us
    pallas_call x1, Pallas kernels, call_merging(): pl.pallas_call(functools.partial(merging, n_adapters), in_specs=[SMEM, SM...  15.1 us
    pallas_call x4, Pallas kernels, call_attend_backward(): kernel(functools.partial(attend_backward, columns, unroll), deps, ATTEND_...  15.1 us
    pallas_call x3, Pallas kernels, call_ffn_forward(): kernel(functools.partial(ffn_forward, quarters, len(out_quarters) // quar...  8.31 us
    pallas_call x2, Pallas kernels, call_ffn_backward(): kernel(functools.partial(ffn_backward, last, len(out_quarters) // 2, len(...  6.58 us
  transfers between devices with their start and end apart: 32, of which 16 were waited for; matrix products, arithmetic and copies ran while one was open for 0% of the time, Pallas kernels for 36%

profile of v2, /device:TPU:0, one launch (start us, length us, event | category | flops | bytes accessed | tf_op | source)
XLA Modules:
  0.0 144.2 jit_solution(10319756100224256690)
XLA Ops:
  4.0 2.4 %prepare_frozen.1 = (bf16[768,768]{1,0:T(8,128)(2,1)S(1)}, bf16[576,768]{1,0:T(8,128)(2,1)S(1)}, bf16[576,768]{1,0:T(8,128)(2,1)S(1)}, bf16[512,768]{1,0:T(8,128...) custom-call(bf16[5,48,384]{2,1,0:T(8,128)(2,1)S(1)} %chip_tile.1.refs_0_.refs_5_, ...), custom_call_target="tpu_custom_call" | custom-call | bytes 1024 | tf_op jit(solution)/shard_map/prepare_frozen/pallas_call | solution.py:574
  6.8 2.6 %collective-permute-start.2 = (bf16[5,48,384]{2,1,0:T(8,128)(2,1)S(1)}, bf16[5,48,384]{2,1,0:T(8,128)(2,1)S(1)}, u32[]{:S(2)}, u32[]{:S(2)}) collective-permute-start(bf16[5,48,384]{2,1,0:T(8,128)(2,1)S(1)} %chip_tile.1.refs_0_.refs_5_), channel_id=1, source_target_pairs={{0,2},{1,3},{2,0},{3,1},{4,6},{5,7},{6,4},{7,5},{8,10},{9,11},{10,... | collective-permute-start | bytes 552968 | tf_op jit(solution)/shard_map/ppermute | solution.py:698
  9.5 5.1 %collective-permute-done.2.refs_6_ = bf16[5,48,384]{2,1,0:T(8,128)(2,1)S(1)} collective-permute-done((bf16[5,48,384]{2,1,0:T(8,128)(2,1)S(1)}, bf16[5,48,384]{2,1,0:T(8,128)(2,1)S(1)}, u32[]{:S(2)}, u32[]{:S(2)}) %collective-permute-start.2) | collective-permute-done | bytes 184352 | tf_op jit(solution)/shard_map/ppermute | solution.py:698
  15.8 1.7 %collective-permute-start.7 = (bf16[576,768]{1,0:T(8,128)(2,1)S(1)}, bf16[576,768]{1,0:T(8,128)(2,1)S(1)}, u32[]{:S(2)}, u32[]{:S(2)}) collective-permute-start(bf16[576,768]{1,0:T(8,128)(2,1)S(1)} %get-tuple-element.104), channel_id=1, source_target_pairs={{0,2},{1,3},{2,0},{3,1},{4,6},{5,7},{6,4},{7,5},{8,10},{9,11},{10,... | collective-permute-start | bytes 2654216 | tf_op jit(solution)/shard_map/ppermute | solution.py:698
  17.5 2.6 %collective-permute-start.6 = (bf16[10,48,384]{2,1,0:T(8,128)(2,1)S(1)}, bf16[10,48,384]{2,1,0:T(8,128)(2,1)S(1)}, u32[]{:S(2)}, u32[]{:S(2)}) collective-permute-start(bf16[10,48,384]{2,1,0:T(8,128)(2,1)S(1)} %get-tuple-element.98.refs_0_.refs_7_), channel_id=1, source_target_pairs={{0,16},{1,17},{2,18},{3,19},{4,20},{5,21},{6,22},{7,23},{8,24},{9,... | collective-permute-start | bytes 1105928 | tf_op jit(solution)/shard_map/ppermute | solution.py:698
  21.6 8.9 %attend_forward.2 = (bf16[576,512]{1,0:T(8,128)(2,1)}, bf16[192,512]{1,0:T(8,128)(2,1)}, bf16[3,512,512]{2,1,0:T(8,128)(2,1)}, bf16[576,512]{1,0:T(8,128)(2,1)},...) custom-call(bf16[10,48,384]{2,1,0:T(8,128)(2,1)S(1)} %get-tuple-element.98.refs_0_.refs_7_, ...), custom_call_target="tpu_custom_call" | custom-call | bytes 1024 | tf_op jit(solution)/shard_map/attend_forward/pallas_call | solution.py:193
  30.6 6.0 %collective-permute-done.6.refs_8_ = bf16[10,48,384]{2,1,0:T(8,128)(2,1)S(1)} collective-permute-done((bf16[10,48,384]{2,1,0:T(8,128)(2,1)S(1)}, bf16[10,48,384]{2,1,0:T(8,128)(2,1)S(1)}, u32[]{:S(2)}, u32[]{:S(2)}) %collective-permute-start.6) | collective-permute-done | bytes 368672 | tf_op jit(solution)/shard_map/ppermute | solution.py:698
  38.0 1.8 %collective-permute-start.13 = (bf16[576,768]{1,0:T(8,128)(2,1)S(1)}, bf16[576,768]{1,0:T(8,128)(2,1)S(1)}, u32[]{:S(2)}, u32[]{:S(2)}) collective-permute-start(bf16[576,768]{1,0:T(8,128)(2,1)S(1)} %get-tuple-element.110), channel_id=1, source_target_pairs={{0,2},{1,3},{2,0},{3,1},{4,6},{5,7},{6,4},{7,5},{8,10},{9,11},{10,... | collective-permute-start | bytes 2654216 | tf_op jit(solution)/shard_map/ppermute | solution.py:698
  43.5 7.9 %collective-permute-done.11.refs_5_ = bf16[10,48,384]{2,1,0:T(8,128)(2,1)S(1)} collective-permute-done((bf16[10,48,384]{2,1,0:T(8,128)(2,1)S(1)}, bf16[10,48,384]{2,1,0:T(8,128)(2,1)S(1)}, u32[]{:S(2)}, u32[]{:S(2)}) %collective-permute-start.11) | collective-permute-done | bytes 368672 | tf_op jit(solution)/shard_map/ppermute | solution.py:698
  53.1 4.7 %collective-permute-done.12.refs_9_.refs_10_ = bf16[256,768]{1,0:T(8,128)(2,1)S(1)} collective-permute-done((bf16[256,768]{1,0:T(8,128)(2,1)S(1)}, bf16[256,768]{1,0:T(8,128)(2,1)S(1)}, u32[]{:S(2)}, u32[]{:S(2)}) %collective-permute-start.12) | collective-permute-done | bytes 393248 | tf_op jit(solution)/shard_map/ppermute | solution.py:698
  60.2 1.7 %collective-permute-start.18 = (bf16[512,768]{1,0:T(8,128)(2,1)S(1)}, bf16[512,768]{1,0:T(8,128)(2,1)S(1)}, u32[]{:S(2)}, u32[]{:S(2)}) collective-permute-start(bf16[512,768]{1,0:T(8,128)(2,1)S(1)} %get-tuple-element.117), channel_id=1, source_target_pairs={{0,2},{1,3},{2,0},{3,1},{4,6},{5,7},{6,4},{7,5},{8,10},{9,11},{10,... | collective-permute-start | bytes 2359304 | tf_op jit(solution)/shard_map/ppermute | solution.py:698
  65.0 9.8 %attend_forward.3 = (bf16[576,512]{1,0:T(8,128)(2,1)}, bf16[192,512]{1,0:T(8,128)(2,1)}, bf16[3,512,512]{2,1,0:T(8,128)(2,1)}, bf16[576,512]{1,0:T(8,128)(2,1)},...) custom-call(s32[6]{0:T(128)S(1)} %stack.27.meta.refs_0_.refs_1_.refs, ...), custom_call_target="tpu_custom_call" | custom-call | bytes 1024 | tf_op jit(solution)/shard_map/attend_forward/pallas_call | solution.py:193
  74.8 3.5 %ffn_forward.3 = (bf16[2,512,768]{2,1,0:T(8,128)(2,1)S(1)}, f32[512,768]{1,0:T(8,128)S(1)}) custom-call(f32[512,768]{1,0:T(8,128)S(1)} %get-tuple-element.112.refs_0_.refs_1_, f32[512,768]{1,0:T(8,128)S(1)} %get-tuple-element.112.refs_0_.refs_1_, bf16[768,768]{1,0:T(8,128)(2,1)S(1)} %copy-done, ...), custom_call_target="tpu_custom_call" | custom-call | bytes 1024 | tf_op jit(solution)/shard_map/ffn_forward/pallas_call | solution.py:231
  82.1 2.4 %ffn_forward.4 = (bf16[1,512,768]{2,1,0:T(8,128)(2,1)S(1)}, f32[512,768]{1,0:T(8,128)S(1)}) custom-call(f32[512,768]{1,0:T(8,128)S(1)} %get-tuple-element.112.refs_0_.refs_1_, f32[512,768]{1,0:T(8,128)S(1)} %get-tuple-element.113.refs_0_.refs_1_, bf16[768,768]{1,0:T(8,128)(2,1)S(1)} %get-tuple-element.119.refs_2_.refs_4_, ...), custom_call_target="tpu_custom_call" | custom-call | bytes 1024 | tf_op jit(solution)/shard_map/ffn_forward/pallas_call | solution.py:231
  85.5 2.4 %ffn_forward.5 = (bf16[1,512,768]{2,1,0:T(8,128)(2,1)S(1)}, f32[512,768]{1,0:T(8,128)S(1)}) custom-call(f32[512,768]{1,0:T(8,128)S(1)} %get-tuple-element.112.refs_0_.refs_1_, f32[512,768]{1,0:T(8,128)S(1)} %get-tuple-element.121.refs_1_, bf16[768,768]{1,0:T(8,128)(2,1)S(1)} %collective-permute-done.21.refs_2_.refs_5_, ...), custom_call_target="tpu_custom_call" | custom-call | bytes 1024 | tf_op jit(solution)/shard_map/ffn_forward/pallas_call | solution.py:231
  89.1 15.1 %merging.1 = (f32[512,768]{1,0:T(8,128)}, f32[512,768]{1,0:T(8,128)S(1)}, bf16[512,768]{1,0:T(8,128)(2,1)S(1)}, bf16[512,768]{1,0:T(8,128)(2,1)S(1)}, bf16[2,2,4...) custom-call(s32[6]{0:T(128)S(1)} %stack.27.meta.refs_0_.refs_1_.refs_3_.refs_2_, ...), custom_call_target="tpu_custom_call" | custom-call | bytes 1024 | tf_op jit(solution)/shard_map/merging/pallas_call | solution.py:395
  104.3 2.1 %merging_input.1 = (f32[512,768]{1,0:T(8,128)S(1)}, bf16[512,768]{1,0:T(8,128)(2,1)S(1)}) custom-call(f32[512,768]{1,0:T(8,128)S(1)} %get-tuple-element.122.refs_0_.sums, f32[8,768]{1,0:T(8,128)S(1)} %get-tuple-element.99.refs_5_.refs_4_.lines.refs_1_.refs_12_, f32[512,768]{1,0:T(8,128)S(1)} %get-tuple-element.125.refs_2_, ...), custom_call_target="tpu_custom_call" | custom-call | bytes 1024 | tf_op jit(solution)/shard_map/merging_input/pallas_call | solution.py:423
  111.1 3.1 %ffn_backward.2.refs_1_ = f32[512,768]{1,0:T(8,128)S(1)} custom-call(bf16[2,4,80,384]{3,2,1,0:T(8,128)(2,1)S(1)} %get-tuple-element.132.refs_0_.refs_1_, bf16[512,768]{1,0:T(8,128)(2,1)S(1)} %get-tuple-element.128.refs_1_.refs_0_, f32[512,768]{1,0:T(8,128)S(1)} %get-tuple-element.129.refs_0_.refs_2_, bf16[2,512,768]{2,1,0:T(8,128)(2,1)S(1)} %get-tuple-element.133.refs_3_, ...), custom_call_target="tpu_custom_call" | custom-call | bytes 1024 | tf_op jit(solution)/shard_map/ffn_backward/pallas_call | solution.py:463
  114.2 3.5 %ffn_backward.3 = (f32[512,768]{1,0:T(8,128)S(1)}, bf16[512,768]{1,0:T(8,128)(2,1)S(1)}) custom-call(bf16[512,768]{1,0:T(8,128)(2,1)S(1)} %get-tuple-element.128.refs_1_.refs_0_, f32[512,768]{1,0:T(8,128)S(1)} %ffn_backward.2.refs_1_, bf16[1,512,768]{2,1,0:T(8,128)(2,1)S(1)} %get-tuple-element.134.refs_2_, ...), custom_call_target="tpu_custom_call" | custom-call | bytes 1024 | tf_op jit(solution)/shard_map/ffn_backward/pallas_call | solution.py:463
  117.7 3.6 %attend_backward.4 = (f32[512,768]{1,0:T(8,128)S(1)}, f32[8,128]{1,0:T(8,128)S(1)}) custom-call(bf16[512,768]{1,0:T(8,128)(2,1)S(1)} %get-tuple-element.138.refs_0_.refs_1_, f32[512,768]{1,0:T(8,128)S(1)} %get-tuple-element.139.refs_1_, bf16[576,512]{1,0:T(8,128)(2,1)S(1)} %copy-done.9, bf16[192,512]{1,0:T(8,128)(2,1)S(1)} %copy-done.13, ...), custom_call_target="tpu_custom_call" | custom-call | bytes 1024 | tf_op jit(solution)/shard_map/attend_backward/pallas_call | solution.py:503
  125.9 3.6 %attend_backward.5 = (f32[512,768]{1,0:T(8,128)S(1)}, f32[8,128]{1,0:T(8,128)S(1)}) custom-call(bf16[4,80,384]{2,1,0:T(8,128)(2,1)S(1)} %get-tuple-element.147.refs_0_.refs_1_, bf16[512,768]{1,0:T(8,128)(2,1)S(1)} %get-tuple-element.138.refs_0_.refs_1_, f32[512,768]{1,0:T(8,128)S(1)} %get-tuple-element.148.refs_2_, bf16[576,512]{1,0:T(8,128)(2,1)S(1)} %copy-done.8, ...), custom_call_target="tpu_custom_call" | custom-call | bytes 1024 | tf_op jit(solution)/shard_map/attend_backward/pallas_call | solution.py:503
  132.8 2.6 %collective-permute-start.30 = (bf16[80,768]{1,0:T(8,128)(2,1)S(1)}, bf16[80,768]{1,0:T(8,128)(2,1)S(1)}, u32[]{:S(2)}, u32[]{:S(2)}) collective-permute-start(bf16[80,768]{1,0:T(8,128)(2,1)S(1)} %get-tuple-element.168), channel_id=1, source_target_pairs={{0,16},{1,17},{2,18},{3,19},{4,20},{5,21},{6,22},{7,23},{8,24},{9,... | collective-permute-start | bytes 368648 | tf_op jit(solution)/shard_map/ppermute | solution.py:698
  135.6 3.6 %attend_backward.6 = (f32[512,768]{1,0:T(8,128)S(1)}, f32[8,128]{1,0:T(8,128)}) custom-call(bf16[80,768]{1,0:T(8,128)(2,1)S(1)} %get-tuple-element.156.refs_0_.refs_1_, bf16[512,768]{1,0:T(8,128)(2,1)S(1)} %get-tuple-element.138.refs_0_.refs_1_, f32[512,768]{1,0:T(8,128)S(1)} %get-tuple-element.157.refs_2_, bf16[576,512]{1,0:T(8,128)(2,1)S(1)} %copy-done.11, ...), custom_call_target="tpu_custom_call" | custom-call | bytes 1024 | tf_op jit(solution)/shard_map/attend_backward/pallas_call | solution.py:503
  139.2 4.2 %attend_backward.7 = (f32[512,768]{1,0:T(8,128)}, f32[8,128]{1,0:T(8,128)S(1)}) custom-call(bf16[80,768]{1,0:T(8,128)(2,1)S(1)} %get-tuple-element.156.refs_0_.refs_1_, bf16[512,768]{1,0:T(8,128)(2,1)S(1)} %get-tuple-element.138.refs_0_.refs_1_, f32[512,768]{1,0:T(8,128)S(1)} %get-tuple-element.161.refs_2_, bf16[576,512]{1,0:T(8,128)(2,1)S(1)} %copy-done.10, ...), custom_call_target="tpu_custom_call" | custom-call | bytes 1024 | tf_op jit(solution)/shard_map/attend_backward/pallas_call | solution.py:503
  (102 shorter events, 37.9 us)
Async XLA Ops:
  6.4 8.2 %collective-permute-start.1 = (bf16[768,768]{1,0:T(8,128)(2,1)S(1)}, bf16[768,768]{1,0:T(8,128)(2,1)S(1)}, u32[]{:S(2)}, u32[]{:S(2)}) collective-permute-start(bf16[768,768]{1,0:T(8,128)(2,1)S(1)} %get-tuple-element.94.refs_6_.refs_5_), channel_id=1, source_target_pairs={{0,1},{1,0},{2,3},{3,2},{4,5},{5,4},{6,7},{7,6},{8,9},{9,8},{10,11... | collective-permute-start | bytes 3538952 | tf_op jit(solution)/shard_map/ppermute | solution.py:698
  6.8 7.8 %collective-permute-start.2 = (bf16[5,48,384]{2,1,0:T(8,128)(2,1)S(1)}, bf16[5,48,384]{2,1,0:T(8,128)(2,1)S(1)}, u32[]{:S(2)}, u32[]{:S(2)}) collective-permute-start(bf16[5,48,384]{2,1,0:T(8,128)(2,1)S(1)} %chip_tile.1.refs_0_.refs_5_), channel_id=1, source_target_pairs={{0,2},{1,3},{2,0},{3,1},{4,6},{5,7},{6,4},{7,5},{8,10},{9,11},{10,... | collective-permute-start | bytes 552968 | tf_op jit(solution)/shard_map/ppermute | solution.py:698
  15.2 22.2 %collective-permute-start.3 = (bf16[768,768]{1,0:T(8,128)(2,1)S(1)}, bf16[768,768]{1,0:T(8,128)(2,1)S(1)}, u32[]{:S(2)}, u32[]{:S(2)}) collective-permute-start(bf16[768,768]{1,0:T(8,128)(2,1)S(1)} %get-tuple-element.101), channel_id=1, source_target_pairs={{0,1},{1,0},{2,3},{3,2},{4,5},{5,4},{6,7},{7,6},{8,9},{9,8},{10,11... | collective-permute-start | bytes 3538952 | tf_op jit(solution)/shard_map/ppermute | solution.py:698
  15.3 22.1 %collective-permute-start.4 = (bf16[768,768]{1,0:T(8,128)(2,1)S(1)}, bf16[768,768]{1,0:T(8,128)(2,1)S(1)}, u32[]{:S(2)}, u32[]{:S(2)}) collective-permute-start(bf16[768,768]{1,0:T(8,128)(2,1)S(1)} %get-tuple-element.102), channel_id=1, source_target_pairs={{0,1},{1,0},{2,3},{3,2},{4,5},{5,4},{6,7},{7,6},{8,9},{9,8},{10,11... | collective-permute-start | bytes 3538952 | tf_op jit(solution)/shard_map/ppermute | solution.py:698
  15.8 21.6 %collective-permute-start.7 = (bf16[576,768]{1,0:T(8,128)(2,1)S(1)}, bf16[576,768]{1,0:T(8,128)(2,1)S(1)}, u32[]{:S(2)}, u32[]{:S(2)}) collective-permute-start(bf16[576,768]{1,0:T(8,128)(2,1)S(1)} %get-tuple-element.104), channel_id=1, source_target_pairs={{0,2},{1,3},{2,0},{3,1},{4,6},{5,7},{6,4},{7,5},{8,10},{9,11},{10,... | collective-permute-start | bytes 2654216 | tf_op jit(solution)/shard_map/ppermute | solution.py:698
  17.5 19.1 %collective-permute-start.6 = (bf16[10,48,384]{2,1,0:T(8,128)(2,1)S(1)}, bf16[10,48,384]{2,1,0:T(8,128)(2,1)S(1)}, u32[]{:S(2)}, u32[]{:S(2)}) collective-permute-start(bf16[10,48,384]{2,1,0:T(8,128)(2,1)S(1)} %get-tuple-element.98.refs_0_.refs_7_), channel_id=1, source_target_pairs={{0,16},{1,17},{2,18},{3,19},{4,20},{5,21},{6,22},{7,23},{8,24},{9,... | collective-permute-start | bytes 1105928 | tf_op jit(solution)/shard_map/ppermute | solution.py:698
  20.1 16.5 %collective-permute-start.5 = (bf16[10,48,384]{2,1,0:T(8,128)(2,1)S(1)}, bf16[10,48,384]{2,1,0:T(8,128)(2,1)S(1)}, u32[]{:S(2)}, u32[]{:S(2)}) collective-permute-start(bf16[10,48,384]{2,1,0:T(8,128)(2,1)S(1)} %get-tuple-element.98.refs_0_.refs_7_), channel_id=1, source_target_pairs={{0,4},{1,5},{2,6},{3,7},{4,0},{5,1},{6,2},{7,3},{8,12},{9,13},{10,... | collective-permute-start | bytes 1105928 | tf_op jit(solution)/shard_map/ppermute | solution.py:698
  38.0 20.9 %collective-permute-start.13 = (bf16[576,768]{1,0:T(8,128)(2,1)S(1)}, bf16[576,768]{1,0:T(8,128)(2,1)S(1)}, u32[]{:S(2)}, u32[]{:S(2)}) collective-permute-start(bf16[576,768]{1,0:T(8,128)(2,1)S(1)} %get-tuple-element.110), channel_id=1, source_target_pairs={{0,2},{1,3},{2,0},{3,1},{4,6},{5,7},{6,4},{7,5},{8,10},{9,11},{10,... | collective-permute-start | bytes 2654216 | tf_op jit(solution)/shard_map/ppermute | solution.py:698
  39.9 11.5 %collective-permute-start.11 = (bf16[10,48,384]{2,1,0:T(8,128)(2,1)S(1)}, bf16[10,48,384]{2,1,0:T(8,128)(2,1)S(1)}, u32[]{:S(2)}, u32[]{:S(2)}) collective-permute-start(bf16[10,48,384]{2,1,0:T(8,128)(2,1)S(1)} %get-tuple-element.108), channel_id=1, source_target_pairs={{0,4},{1,5},{2,6},{3,7},{4,0},{5,1},{6,2},{7,3},{8,12},{9,13},{10,... | collective-permute-start | bytes 1105928 | tf_op jit(solution)/shard_map/ppermute | solution.py:698
  41.4 17.1 %collective-permute-start.10 = (bf16[20,48,384]{2,1,0:T(8,128)(2,1)S(1)}, bf16[20,48,384]{2,1,0:T(8,128)(2,1)S(1)}, u32[]{:S(2)}, u32[]{:S(2)}) collective-permute-start(bf16[20,48,384]{2,1,0:T(8,128)(2,1)S(1)} %get-tuple-element.105.refs_2_), channel_id=1, source_target_pairs={{0,8},{1,9},{2,10},{3,11},{4,12},{5,13},{6,14},{7,15},{8,0},{9,1},... | collective-permute-start | bytes 2211848 | tf_op jit(solution)/shard_map/ppermute | solution.py:698
  42.9 15.5 %collective-permute-start.8 = (bf16[20,48,384]{2,1,0:T(8,128)(2,1)S(1)}, bf16[20,48,384]{2,1,0:T(8,128)(2,1)S(1)}, u32[]{:S(2)}, u32[]{:S(2)}) collective-permute-start(bf16[20,48,384]{2,1,0:T(8,128)(2,1)S(1)} %get-tuple-element.105.refs_2_), channel_id=1, source_target_pairs={{0,1},{1,0},{2,3},{3,2},{4,5},{5,4},{6,7},{7,6},{8,9},{9,8},{10,11... | collective-permute-start | bytes 2211848 | tf_op jit(solution)/shard_map/ppermute | solution.py:698
  43.0 14.8 %collective-permute-start.12 = (bf16[256,768]{1,0:T(8,128)(2,1)S(1)}, bf16[256,768]{1,0:T(8,128)(2,1)S(1)}, u32[]{:S(2)}, u32[]{:S(2)}) collective-permute-start(bf16[256,768]{1,0:T(8,128)(2,1)S(1)} %get-tuple-element.109), channel_id=1, source_target_pairs={{0,4},{1,5},{2,6},{3,7},{4,0},{5,1},{6,2},{7,3},{8,12},{9,13},{10,... | collective-permute-start | bytes 1179656 | tf_op jit(solution)/shard_map/ppermute | solution.py:698
  60.2 20.6 %collective-permute-start.18 = (bf16[512,768]{1,0:T(8,128)(2,1)S(1)}, bf16[512,768]{1,0:T(8,128)(2,1)S(1)}, u32[]{:S(2)}, u32[]{:S(2)}) collective-permute-start(bf16[512,768]{1,0:T(8,128)(2,1)S(1)} %get-tuple-element.117), channel_id=1, source_target_pairs={{0,2},{1,3},{2,0},{3,1},{4,6},{5,7},{6,4},{7,5},{8,10},{9,11},{10,... | collective-permute-start | bytes 2359304 | tf_op jit(solution)/shard_map/ppermute | solution.py:698
  61.9 16.4 %collective-permute-start.15 = (bf16[20,48,384]{2,1,0:T(8,128)(2,1)S(1)}, bf16[20,48,384]{2,1,0:T(8,128)(2,1)S(1)}, u32[]{:S(2)}, u32[]{:S(2)}) collective-permute-start(bf16[20,48,384]{2,1,0:T(8,128)(2,1)S(1)} %get-tuple-element.114.refs_4_), channel_id=1, source_target_pairs={{0,1},{1,0},{2,3},{3,2},{4,5},{5,4},{6,7},{7,6},{8,9},{9,8},{10,11... | collective-permute-start | bytes 2211848 | tf_op jit(solution)/shard_map/ppermute | solution.py:698
  61.9 18.9 %collective-permute-start.19 = (bf16[20,48,384]{2,1,0:T(8,128)(2,1)S(1)}, bf16[20,48,384]{2,1,0:T(8,128)(2,1)S(1)}, u32[]{:S(2)}, u32[]{:S(2)}) collective-permute-start(bf16[20,48,384]{2,1,0:T(8,128)(2,1)S(1)} %get-tuple-element.114.refs_4_), channel_id=1, source_target_pairs={{0,4},{1,5},{2,6},{3,7},{4,0},{5,1},{6,2},{7,3},{8,12},{9,13},{10,... | collective-permute-start | bytes 2211848 | tf_op jit(solution)/shard_map/ppermute | solution.py:698
  63.4 16.2 %collective-permute-start.20 = (bf16[384,768]{1,0:T(8,128)(2,1)S(1)}, bf16[384,768]{1,0:T(8,128)(2,1)S(1)}, u32[]{:S(2)}, u32[]{:S(2)}) collective-permute-start(bf16[384,768]{1,0:T(8,128)(2,1)S(1)} %get-tuple-element.118.refs_6_), channel_id=1, source_target_pairs={{0,8},{1,9},{2,10},{3,11},{4,12},{5,13},{6,14},{7,15},{8,0},{9,1},... | collective-permute-start | bytes 1769480 | tf_op jit(solution)/shard_map/ppermute | solution.py:698
  65.0 14.6 %collective-permute-start.17 = (bf16[256,768]{1,0:T(8,128)(2,1)S(1)}, bf16[256,768]{1,0:T(8,128)(2,1)S(1)}, u32[]{:S(2)}, u32[]{:S(2)}) collective-permute-start(bf16[256,768]{1,0:T(8,128)(2,1)S(1)} %get-tuple-element.116.refs_3_.refs_6_), channel_id=1, source_target_pairs={{0,1},{1,0},{2,3},{3,2},{4,5},{5,4},{6,7},{7,6},{8,9},{9,8},{10,11... | collective-permute-start | bytes 1179656 | tf_op jit(solution)/shard_map/ppermute | solution.py:698
  108.9 13.3 %collective-permute-start.25 = (bf16[2,4,80,384]{3,2,1,0:T(8,128)(2,1)S(1)}, bf16[2,4,80,384]{3,2,1,0:T(8,128)(2,1)S(1)}, u32[]{:S(2)}, u32[]{:S(2)}) collective-permute-start(bf16[2,4,80,384]{3,2,1,0:T(8,128)(2,1)S(1)} %get-tuple-element.144), channel_id=1, source_target_pairs={{0,2},{1,3},{2,0},{3,1},{4,6},{5,7},{6,4},{7,5},{8,10},{9,11},{10,... | collective-permute-start | bytes 1474568 | tf_op jit(solution)/shard_map/ppermute | solution.py:698
  109.5 13.0 %collective-permute-start.26 = (bf16[2,4,80,384]{3,2,1,0:T(8,128)(2,1)S(1)}, bf16[2,4,80,384]{3,2,1,0:T(8,128)(2,1)S(1)}, u32[]{:S(2)}, u32[]{:S(2)}) collective-permute-start(bf16[2,4,80,384]{3,2,1,0:T(8,128)(2,1)S(1)} %get-tuple-element.146), channel_id=1, source_target_pairs={{0,4},{1,5},{2,6},{3,7},{4,0},{5,1},{6,2},{7,3},{8,12},{9,13},{10,... | collective-permute-start | bytes 1474568 | tf_op jit(solution)/shard_map/ppermute | solution.py:698
  122.9 6.9 %collective-permute-start.27 = (bf16[4,80,384]{2,1,0:T(8,128)(2,1)S(1)}, bf16[4,80,384]{2,1,0:T(8,128)(2,1)S(1)}, u32[]{:S(2)}, u32[]{:S(2)}) collective-permute-start(bf16[4,80,384]{2,1,0:T(8,128)(2,1)S(1)} %get-tuple-element.153), channel_id=1, source_target_pairs={{0,4},{1,5},{2,6},{3,7},{4,0},{5,1},{6,2},{7,3},{8,12},{9,13},{10,... | collective-permute-start | bytes 737288 | tf_op jit(solution)/shard_map/ppermute | solution.py:698
  124.4 6.6 %collective-permute-start.28 = (bf16[4,80,384]{2,1,0:T(8,128)(2,1)S(1)}, bf16[4,80,384]{2,1,0:T(8,128)(2,1)S(1)}, u32[]{:S(2)}, u32[]{:S(2)}) collective-permute-start(bf16[4,80,384]{2,1,0:T(8,128)(2,1)S(1)} %get-tuple-element.155), channel_id=1, source_target_pairs={{0,2},{1,3},{2,0},{3,1},{4,6},{5,7},{6,4},{7,5},{8,10},{9,11},{10,... | collective-permute-start | bytes 737288 | tf_op jit(solution)/shard_map/ppermute | solution.py:698
  131.2 12.3 %collective-permute-start.29 = (bf16[80,768]{1,0:T(8,128)(2,1)S(1)}, bf16[80,768]{1,0:T(8,128)(2,1)S(1)}, u32[]{:S(2)}, u32[]{:S(2)}) collective-permute-start(bf16[80,768]{1,0:T(8,128)(2,1)S(1)} %get-tuple-element.167), channel_id=1, source_target_pairs={{0,8},{1,9},{2,10},{3,11},{4,12},{5,13},{6,14},{7,15},{8,0},{9,1},... | collective-permute-start | bytes 368648 | tf_op jit(solution)/shard_map/ppermute | solution.py:698
  132.8 10.7 %collective-permute-start.30 = (bf16[80,768]{1,0:T(8,128)(2,1)S(1)}, bf16[80,768]{1,0:T(8,128)(2,1)S(1)}, u32[]{:S(2)}, u32[]{:S(2)}) collective-permute-start(bf16[80,768]{1,0:T(8,128)(2,1)S(1)} %get-tuple-element.168), channel_id=1, source_target_pairs={{0,16},{1,17},{2,18},{3,19},{4,20},{5,21},{6,22},{7,23},{8,24},{9,... | collective-permute-start | bytes 368648 | tf_op jit(solution)/shard_map/ppermute | solution.py:698
  135.4 8.1 %collective-permute-start.31 = (bf16[80,768]{1,0:T(8,128)(2,1)S(1)}, bf16[80,768]{1,0:T(8,128)(2,1)S(1)}, u32[]{:S(2)}, u32[]{:S(2)}) collective-permute-start(bf16[80,768]{1,0:T(8,128)(2,1)S(1)} %get-tuple-element.169), channel_id=1, source_target_pairs={{0,24},{1,25},{2,26},{3,27},{4,28},{5,29},{6,30},{7,31},{8,16},{9,... | collective-permute-start | bytes 368648 | tf_op jit(solution)/shard_map/ppermute | solution.py:698
  (25 other events, 132.6 us)

commit v3 on v2

--- a/solution.py
+++ b/solution.py
@@ -545,10 +545,27 @@
     )(meta, *(in_hbm(a) for a in (down, up, query, key, value, *vectors)))
 
 
-def prepare_frozen(meta, qkv_turned, attn_out, into, out, attn, with_attn, with_in, out_last, *copies):
+def join_attention(qkv_turned, attn_out, attn):
     columns = qkv_turned.shape[0]
     attn[:columns] = qkv_turned[...]
     attn[columns:] = attn_out[...]
+
+
+def call_join_attention(deps, qkv_turned, attn_out):
+    rows, width = qkv_turned.shape[0] + attn_out.shape[0], attn_out.shape[1]
+    return kernel(
+        join_attention,
+        deps,
+        16,
+        in_specs=[VMEM] * 2,
+        out_specs=VMEM,
+        out_shape=sds((rows, width), BF16),
+        cost_estimate=cost(1),
+        name="join_attention",
+    )(in_hbm(qkv_turned), in_hbm(attn_out))
+
+
+def prepare_shares(meta, attn, into, out, with_attn, with_in, out_last, *copies):
     half = attn.shape[0] // 2
     more = half // 3
     mine = pl.multiple_of(meta[PAIR_Y] * half, 16)
@@ -566,42 +583,43 @@
         copy[...] = source[...]
 
 
-def call_prepare_frozen(deps, meta, qkv_turned, attn_out, into, out):
-    rows, width = qkv_turned.shape[0] + attn_out.shape[0], attn_out.shape[1]
+def call_prepare_shares(deps, meta, attn, into, out):
+    rows, width = attn.shape
     unit = out.shape[0] // 12
-    shares = (rows, rows // 2 + rows // 6 + unit, into.shape[0] // 2 + 3 * unit, 8 * unit)
+    shares = (rows // 2 + rows // 6 + unit, into.shape[0] // 2 + 3 * unit, 8 * unit)
     shares = shares + (into.shape[0], out.shape[0])
     return kernel(
-        prepare_frozen,
+        prepare_shares,
         deps,
         16,
-        in_specs=[SMEM] + [VMEM] * 4,
-        out_specs=[VMEM] * 6,
+        in_specs=[SMEM] + [VMEM] * 3,
+        out_specs=[VMEM] * 5,
         out_shape=[sds((n, width), BF16) for n in shares],
         cost_estimate=cost(1),
-        name="prepare_frozen",
-    )(meta, *(in_hbm(a) for a in (qkv_turned, attn_out, into, out)))
-
-
-def chip_tile(meta, keep, got, tile):
+        name="prepare_shares",
+    )(meta, attn, in_hbm(into), in_hbm(out))
+
+
+def chip_tile(meta, keep, got, attn, tile, attn_out):
     mine, other = keep[...].astype(F32), got[...].astype(F32)
     lower = jnp.where(meta[CORE] == 0, mine, other)
     upper = jnp.where(meta[CORE] == 0, other, mine)
     tile[...] = jnp.concatenate([lower, upper], axis=1).astype(BF16)
 
 
-def call_chip_tile(meta, keep, got):
+def call_chip_tile(meta, keep, got, attn):
     n_mats, rows, half = keep.shape
     return kernel(
         chip_tile,
         [],
         16,
-        in_specs=[SMEM] + [VMEM] * 2,
-        out_specs=VMEM,
-        out_shape=sds((n_mats, 2 * rows, half), BF16),
+        in_specs=[SMEM] + [VMEM] * 2 + [ANY],
+        out_specs=[VMEM, ANY],
+        out_shape=[sds((n_mats, 2 * rows, half), BF16), sds(attn.shape, attn.dtype)],
+        input_output_aliases={3: 1},
         cost_estimate=cost(1),
         name="chip_tile",
-    )(meta, keep, got)
+    )(meta, keep, got, attn)
 
 
 def add_blocks(*blocks):
@@ -789,15 +807,16 @@
         merging_gain,
         merging_bias,
     )
-    tile = call_chip_tile(meta, keep, flip(send, 1)) if hops.tiled else keep
-    attn, with_attn, with_in, out_2, into, out = call_prepare_frozen(
-        [tile], meta, qkv_weight.T, attn_out_weight, ffn_in_weight, ffn_out_weight
-    )
+    attn = call_join_attention([keep], qkv_weight.T, attn_out_weight)
     if not hops.tiled:
         shard = jnp.concatenate([keep, send], axis=2)
         return plain_schedule(
-            meta, doc_lengths, tokens, out_grad, lines, columns, n_adapters, attn, into, out, shard
+            meta, doc_lengths, tokens, out_grad, lines, columns, n_adapters, attn, ffn_in_weight, ffn_out_weight, shard
         )
+    tile, attn = call_chip_tile(meta, keep, flip(send, 1), attn)
+    with_attn, with_in, out_2, into, out = call_prepare_shares(
+        [], meta, attn, ffn_in_weight, ffn_out_weight
+    )
     tile_x = flip(tile, ALONG_X)
     attn_core = flip(attn, 1)
     both, with_attn, into, out = sync(

time: 144 us -> 142 us (0.986)
  waiting for transfers between devices: 34.7 us -> 31.8 us
    ppermute x32, waiting for transfers between devices: 34.7 us -> 31.8 us  [flip(): return lax.ppermute(array, AXES, [(i, i ^ bits) for i in range(self.count)])]
    pallas_call x2 -> x3, Pallas kernels: 2.98 us -> 3.83 us  [the longest x1 1.95 us: call_prepare_shares(): kernel(prepare_shares, deps, 16, in_specs=[SMEM] + [VMEM] * 3, out_specs=...]
  transfers between devices with their start and end apart: 32 -> 32, of which waited for: 16 -> 15; matrix products, arithmetic and copies ran while one was open for 0% -> 0% of each run, Pallas kernels for 36% -> 39%
where the time goes in v3:
time: 142 us
  Pallas kernels  77.5 us (55%)
  waiting for transfers between devices  31.8 us (22%)
  starting transfers between devices  31.3 us (22%)
    ppermute x32, waiting for transfers between devices, flip(): return lax.ppermute(array, AXES, [(i, i ^ bits) for i in range(self.count)])  31.8 us
    ppermute x32, starting transfers between devices, flip(): return lax.ppermute(array, AXES, [(i, i ^ bits) for i in range(self.count)])  31.3 us
    pallas_call x2, Pallas kernels, call_attend_forward(): kernel(functools.partial(attend_forward, columns, last), deps, ATTEND_MIB...  18.6 us
    pallas_call x4, Pallas kernels, call_attend_backward(): kernel(functools.partial(attend_backward, columns, unroll), deps, ATTEND_...  15.1 us
    pallas_call x1, Pallas kernels, call_merging(): pl.pallas_call(functools.partial(merging, n_adapters), in_specs=[SMEM, SM...  15.1 us
    pallas_call x3, Pallas kernels, call_ffn_forward(): kernel(functools.partial(ffn_forward, quarters, len(out_quarters) // quar...  8.3 us
    pallas_call x2, Pallas kernels, call_ffn_backward(): kernel(functools.partial(ffn_backward, last, len(out_quarters) // 2, len(...  6.54 us
  transfers between devices with their start and end apart: 32, of which 15 were waited for; matrix products, arithmetic and copies ran while one was open for 0% of the time, Pallas kernels for 39%

profile of v3, /device:TPU:0, one launch (start us, length us, event | category | flops | bytes accessed | tf_op | source)
XLA Modules:
  0.0 141.9 jit_solution(15352902042948856741)
XLA Ops:
  4.5 2.9 %collective-permute-start.2 = (bf16[5,48,384]{2,1,0:T(8,128)(2,1)S(1)}, bf16[5,48,384]{2,1,0:T(8,128)(2,1)S(1)}, u32[]{:S(2)}, u32[]{:S(2)}) collective-permute-start(bf16[5,48,384]{2,1,0:T(8,128)(2,1)S(1)} %get-tuple-element.99.refs_5_), channel_id=1, source_target_pairs={{0,2},{1,3},{2,0},{3,1},{4,6},{5,7},{6,4},{7,5},{8,10},{9,11},{10,... | collective-permute-start | bytes 552968 | tf_op jit(solution)/shard_map/ppermute | solution.py:716
  7.4 2.0 %prepare_shares.1 = (bf16[576,768]{1,0:T(8,128)(2,1)S(1)}, bf16[576,768]{1,0:T(8,128)(2,1)S(1)}, bf16[512,768]{1,0:T(8,128)(2,1)S(1)}, bf16[768,768]{1,0:T(8,128)(2,1)S(1)}, bf16[768,768]{1,0:T(8,128)(2,1)S(1)}) custom-call(s32[6]{0:T(128)S(1)} %stack.27.meta.refs_0_.refs_1_.refs_3_.refs_2_, bf16[768,768]{1,0:T(8,128)(2,1)S(1)} %get-tuple-element.95.refs_1_.refs_6_.refs_5_, ...), custom_call_target="tpu_custom_call" | custom-call | bytes 1024 | tf_op jit(solution)/shard_map/prepare_shares/pallas_call | solution.py:591
  9.4 2.9 %collective-permute-done.2.refs_6_ = bf16[5,48,384]{2,1,0:T(8,128)(2,1)S(1)} collective-permute-done((bf16[5,48,384]{2,1,0:T(8,128)(2,1)S(1)}, bf16[5,48,384]{2,1,0:T(8,128)(2,1)S(1)}, u32[]{:S(2)}, u32[]{:S(2)}) %collective-permute-start.2) | collective-permute-done | bytes 184352 | tf_op jit(solution)/shard_map/ppermute | solution.py:716
  13.5 1.7 %collective-permute-start.7 = (bf16[576,768]{1,0:T(8,128)(2,1)S(1)}, bf16[576,768]{1,0:T(8,128)(2,1)S(1)}, u32[]{:S(2)}, u32[]{:S(2)}) collective-permute-start(bf16[576,768]{1,0:T(8,128)(2,1)S(1)} %get-tuple-element.106), channel_id=1, source_target_pairs={{0,2},{1,3},{2,0},{3,1},{4,6},{5,7},{6,4},{7,5},{8,10},{9,11},{10,... | collective-permute-start | bytes 2654216 | tf_op jit(solution)/shard_map/ppermute | solution.py:716
  15.2 2.6 %collective-permute-start.6 = (bf16[10,48,384]{2,1,0:T(8,128)(2,1)S(1)}, bf16[10,48,384]{2,1,0:T(8,128)(2,1)S(1)}, u32[]{:S(2)}, u32[]{:S(2)}) collective-permute-start(bf16[10,48,384]{2,1,0:T(8,128)(2,1)S(1)} %get-tuple-element.100.refs_0_.refs_7_), channel_id=1, source_target_pairs={{0,16},{1,17},{2,18},{3,19},{4,20},{5,21},{6,22},{7,23},{8,24},{9,... | collective-permute-start | bytes 1105928 | tf_op jit(solution)/shard_map/ppermute | solution.py:716
  19.3 8.9 %attend_forward.2 = (bf16[576,512]{1,0:T(8,128)(2,1)}, bf16[192,512]{1,0:T(8,128)(2,1)}, bf16[3,512,512]{2,1,0:T(8,128)(2,1)}, bf16[576,512]{1,0:T(8,128)(2,1)},...) custom-call(bf16[10,48,384]{2,1,0:T(8,128)(2,1)S(1)} %get-tuple-element.100.refs_0_.refs_7_, ...), custom_call_target="tpu_custom_call" | custom-call | bytes 1024 | tf_op jit(solution)/shard_map/attend_forward/pallas_call | solution.py:193
  28.2 6.1 %collective-permute-done.6.refs_8_ = bf16[10,48,384]{2,1,0:T(8,128)(2,1)S(1)} collective-permute-done((bf16[10,48,384]{2,1,0:T(8,128)(2,1)S(1)}, bf16[10,48,384]{2,1,0:T(8,128)(2,1)S(1)}, u32[]{:S(2)}, u32[]{:S(2)}) %collective-permute-start.6) | collective-permute-done | bytes 368672 | tf_op jit(solution)/shard_map/ppermute | solution.py:716
  35.7 1.8 %collective-permute-start.13 = (bf16[576,768]{1,0:T(8,128)(2,1)S(1)}, bf16[576,768]{1,0:T(8,128)(2,1)S(1)}, u32[]{:S(2)}, u32[]{:S(2)}) collective-permute-start(bf16[576,768]{1,0:T(8,128)(2,1)S(1)} %get-tuple-element.112), channel_id=1, source_target_pairs={{0,2},{1,3},{2,0},{3,1},{4,6},{5,7},{6,4},{7,5},{8,10},{9,11},{10,... | collective-permute-start | bytes 2654216 | tf_op jit(solution)/shard_map/ppermute | solution.py:716
  41.2 7.9 %collective-permute-done.11.refs_5_ = bf16[10,48,384]{2,1,0:T(8,128)(2,1)S(1)} collective-permute-done((bf16[10,48,384]{2,1,0:T(8,128)(2,1)S(1)}, bf16[10,48,384]{2,1,0:T(8,128)(2,1)S(1)}, u32[]{:S(2)}, u32[]{:S(2)}) %collective-permute-start.11) | collective-permute-done | bytes 368672 | tf_op jit(solution)/shard_map/ppermute | solution.py:716
  50.8 4.7 %collective-permute-done.12.refs_9_.refs_10_ = bf16[256,768]{1,0:T(8,128)(2,1)S(1)} collective-permute-done((bf16[256,768]{1,0:T(8,128)(2,1)S(1)}, bf16[256,768]{1,0:T(8,128)(2,1)S(1)}, u32[]{:S(2)}, u32[]{:S(2)}) %collective-permute-start.12) | collective-permute-done | bytes 393248 | tf_op jit(solution)/shard_map/ppermute | solution.py:716
  62.7 9.7 %attend_forward.3 = (bf16[576,512]{1,0:T(8,128)(2,1)}, bf16[192,512]{1,0:T(8,128)(2,1)}, bf16[3,512,512]{2,1,0:T(8,128)(2,1)}, bf16[576,512]{1,0:T(8,128)(2,1)},...) custom-call(s32[6]{0:T(128)S(1)} %stack.27.meta.refs_0_.refs_1_.refs, ...), custom_call_target="tpu_custom_call" | custom-call | bytes 1024 | tf_op jit(solution)/shard_map/attend_forward/pallas_call | solution.py:193
  72.5 3.5 %ffn_forward.3 = (bf16[2,512,768]{2,1,0:T(8,128)(2,1)S(1)}, f32[512,768]{1,0:T(8,128)S(1)}) custom-call(f32[512,768]{1,0:T(8,128)S(1)} %get-tuple-element.114.refs_0_.refs_1_, f32[512,768]{1,0:T(8,128)S(1)} %get-tuple-element.114.refs_0_.refs_1_, bf16[768,768]{1,0:T(8,128)(2,1)S(1)} %copy-done, ...), custom_call_target="tpu_custom_call" | custom-call | bytes 1024 | tf_op jit(solution)/shard_map/ffn_forward/pallas_call | solution.py:231
  79.8 2.4 %ffn_forward.4 = (bf16[1,512,768]{2,1,0:T(8,128)(2,1)S(1)}, f32[512,768]{1,0:T(8,128)S(1)}) custom-call(f32[512,768]{1,0:T(8,128)S(1)} %get-tuple-element.114.refs_0_.refs_1_, f32[512,768]{1,0:T(8,128)S(1)} %get-tuple-element.115.refs_0_.refs_1_, bf16[768,768]{1,0:T(8,128)(2,1)S(1)} %get-tuple-element.121.refs_2_.refs_4_, ...), custom_call_target="tpu_custom_call" | custom-call | bytes 1024 | tf_op jit(solution)/shard_map/ffn_forward/pallas_call | solution.py:231
  83.2 2.4 %ffn_forward.5 = (bf16[1,512,768]{2,1,0:T(8,128)(2,1)S(1)}, f32[512,768]{1,0:T(8,128)S(1)}) custom-call(f32[512,768]{1,0:T(8,128)S(1)} %get-tuple-element.114.refs_0_.refs_1_, f32[512,768]{1,0:T(8,128)S(1)} %get-tuple-element.123.refs_1_, bf16[768,768]{1,0:T(8,128)(2,1)S(1)} %collective-permute-done.21.refs_2_.refs_5_, ...), custom_call_target="tpu_custom_call" | custom-call | bytes 1024 | tf_op jit(solution)/shard_map/ffn_forward/pallas_call | solution.py:231
  86.8 15.1 %merging.1 = (f32[512,768]{1,0:T(8,128)}, f32[512,768]{1,0:T(8,128)S(1)}, bf16[512,768]{1,0:T(8,128)(2,1)S(1)}, bf16[512,768]{1,0:T(8,128)(2,1)S(1)}, bf16[2,2,4...) custom-call(s32[6]{0:T(128)S(1)} %stack.27.meta.refs_0_.refs_1_.refs_3_.refs_2_, ...), custom_call_target="tpu_custom_call" | custom-call | bytes 1024 | tf_op jit(solution)/shard_map/merging/pallas_call | solution.py:395
  102.0 2.0 %merging_input.1 = (f32[512,768]{1,0:T(8,128)S(1)}, bf16[512,768]{1,0:T(8,128)(2,1)S(1)}) custom-call(f32[512,768]{1,0:T(8,128)S(1)} %get-tuple-element.124.refs_0_.sums, f32[8,768]{1,0:T(8,128)S(1)} %get-tuple-element.101.refs_5_.refs_4_.lines.refs_1_.refs_12_, f32[512,768]{1,0:T(8,128)S(1)} %get-tuple-element.127.refs_2_, ...), custom_call_target="tpu_custom_call" | custom-call | bytes 1024 | tf_op jit(solution)/shard_map/merging_input/pallas_call | solution.py:423
  104.1 1.8 %collective-permute-done.24.refs_2_ = bf16[2,2,4,80,768]{4,3,2,1,0:T(8,128)(2,1)S(1)} collective-permute-done((bf16[2,2,4,80,768]{4,3,2,1,0:T(8,128)(2,1)S(1)}, bf16[2,2,4,80,768]{4,3,2,1,0:T(8,128)(2,1)S(1)}, u32[]{:S(2)}, u32[]{:S(2)}) %collective-permute-start.24) | collective-permute-done | bytes 1966112 | tf_op jit(solution)/shard_map/ppermute | solution.py:716
  108.8 3.1 %ffn_backward.2.refs_1_ = f32[512,768]{1,0:T(8,128)S(1)} custom-call(bf16[2,4,80,384]{3,2,1,0:T(8,128)(2,1)S(1)} %get-tuple-element.134.refs_0_.refs_1_, bf16[512,768]{1,0:T(8,128)(2,1)S(1)} %get-tuple-element.130.refs_1_.refs_0_, f32[512,768]{1,0:T(8,128)S(1)} %get-tuple-element.131.refs_0_.refs_2_, bf16[2,512,768]{2,1,0:T(8,128)(2,1)S(1)} %get-tuple-element.135.refs_3_, ...), custom_call_target="tpu_custom_call" | custom-call | bytes 1024 | tf_op jit(solution)/shard_map/ffn_backward/pallas_call | solution.py:463
  111.9 3.4 %ffn_backward.3 = (f32[512,768]{1,0:T(8,128)S(1)}, bf16[512,768]{1,0:T(8,128)(2,1)S(1)}) custom-call(bf16[512,768]{1,0:T(8,128)(2,1)S(1)} %get-tuple-element.130.refs_1_.refs_0_, f32[512,768]{1,0:T(8,128)S(1)} %ffn_backward.2.refs_1_, bf16[1,512,768]{2,1,0:T(8,128)(2,1)S(1)} %get-tuple-element.136.refs_2_, ...), custom_call_target="tpu_custom_call" | custom-call | bytes 1024 | tf_op jit(solution)/shard_map/ffn_backward/pallas_call | solution.py:463
  115.4 3.6 %attend_backward.4 = (f32[512,768]{1,0:T(8,128)S(1)}, f32[8,128]{1,0:T(8,128)S(1)}) custom-call(bf16[512,768]{1,0:T(8,128)(2,1)S(1)} %get-tuple-element.140.refs_0_.refs_1_, f32[512,768]{1,0:T(8,128)S(1)} %get-tuple-element.141.refs_1_, bf16[576,512]{1,0:T(8,128)(2,1)S(1)} %copy-done.9, bf16[192,512]{1,0:T(8,128)(2,1)S(1)} %copy-done.13, ...), custom_call_target="tpu_custom_call" | custom-call | bytes 1024 | tf_op jit(solution)/shard_map/attend_backward/pallas_call | solution.py:503
  123.6 3.6 %attend_backward.5 = (f32[512,768]{1,0:T(8,128)S(1)}, f32[8,128]{1,0:T(8,128)S(1)}) custom-call(bf16[4,80,384]{2,1,0:T(8,128)(2,1)S(1)} %get-tuple-element.149.refs_0_.refs_1_, bf16[512,768]{1,0:T(8,128)(2,1)S(1)} %get-tuple-element.140.refs_0_.refs_1_, f32[512,768]{1,0:T(8,128)S(1)} %get-tuple-element.150.refs_2_, bf16[576,512]{1,0:T(8,128)(2,1)S(1)} %copy-done.8, ...), custom_call_target="tpu_custom_call" | custom-call | bytes 1024 | tf_op jit(solution)/shard_map/attend_backward/pallas_call | solution.py:503
  130.5 2.6 %collective-permute-start.30 = (bf16[80,768]{1,0:T(8,128)(2,1)S(1)}, bf16[80,768]{1,0:T(8,128)(2,1)S(1)}, u32[]{:S(2)}, u32[]{:S(2)}) collective-permute-start(bf16[80,768]{1,0:T(8,128)(2,1)S(1)} %get-tuple-element.170), channel_id=1, source_target_pairs={{0,16},{1,17},{2,18},{3,19},{4,20},{5,21},{6,22},{7,23},{8,24},{9,... | collective-permute-start | bytes 368648 | tf_op jit(solution)/shard_map/ppermute | solution.py:716
  133.3 3.6 %attend_backward.6 = (f32[512,768]{1,0:T(8,128)S(1)}, f32[8,128]{1,0:T(8,128)}) custom-call(bf16[80,768]{1,0:T(8,128)(2,1)S(1)} %get-tuple-element.158.refs_0_.refs_1_, bf16[512,768]{1,0:T(8,128)(2,1)S(1)} %get-tuple-element.140.refs_0_.refs_1_, f32[512,768]{1,0:T(8,128)S(1)} %get-tuple-element.159.refs_2_, bf16[576,512]{1,0:T(8,128)(2,1)S(1)} %copy-done.11, ...), custom_call_target="tpu_custom_call" | custom-call | bytes 1024 | tf_op jit(solution)/shard_map/attend_backward/pallas_call | solution.py:503
  137.0 4.2 %attend_backward.7 = (f32[512,768]{1,0:T(8,128)}, f32[8,128]{1,0:T(8,128)S(1)}) custom-call(bf16[80,768]{1,0:T(8,128)(2,1)S(1)} %get-tuple-element.158.refs_0_.refs_1_, bf16[512,768]{1,0:T(8,128)(2,1)S(1)} %get-tuple-element.140.refs_0_.refs_1_, f32[512,768]{1,0:T(8,128)S(1)} %get-tuple-element.163.refs_2_, bf16[576,512]{1,0:T(8,128)(2,1)S(1)} %copy-done.10, ...), custom_call_target="tpu_custom_call" | custom-call | bytes 1024 | tf_op jit(solution)/shard_map/attend_backward/pallas_call | solution.py:503
  (103 shorter events, 38.1 us)
Async XLA Ops:
  4.4 7.9 %collective-permute-start.1 = (bf16[768,768]{1,0:T(8,128)(2,1)S(1)}, bf16[768,768]{1,0:T(8,128)(2,1)S(1)}, u32[]{:S(2)}, u32[]{:S(2)}) collective-permute-start(bf16[768,768]{1,0:T(8,128)(2,1)S(1)} %get-tuple-element.95.refs_1_.refs_6_.refs_5_), channel_id=1, source_target_pairs={{0,1},{1,0},{2,3},{3,2},{4,5},{5,4},{6,7},{7,6},{8,9},{9,8},{10,11... | collective-permute-start | bytes 3538952 | tf_op jit(solution)/shard_map/ppermute | solution.py:716
  4.5 7.8 %collective-permute-start.2 = (bf16[5,48,384]{2,1,0:T(8,128)(2,1)S(1)}, bf16[5,48,384]{2,1,0:T(8,128)(2,1)S(1)}, u32[]{:S(2)}, u32[]{:S(2)}) collective-permute-start(bf16[5,48,384]{2,1,0:T(8,128)(2,1)S(1)} %get-tuple-element.99.refs_5_), channel_id=1, source_target_pairs={{0,2},{1,3},{2,0},{3,1},{4,6},{5,7},{6,4},{7,5},{8,10},{9,11},{10,... | collective-permute-start | bytes 552968 | tf_op jit(solution)/shard_map/ppermute | solution.py:716
  12.9 22.2 %collective-permute-start.3 = (bf16[768,768]{1,0:T(8,128)(2,1)S(1)}, bf16[768,768]{1,0:T(8,128)(2,1)S(1)}, u32[]{:S(2)}, u32[]{:S(2)}) collective-permute-start(bf16[768,768]{1,0:T(8,128)(2,1)S(1)} %get-tuple-element.103), channel_id=1, source_target_pairs={{0,1},{1,0},{2,3},{3,2},{4,5},{5,4},{6,7},{7,6},{8,9},{9,8},{10,11... | collective-permute-start | bytes 3538952 | tf_op jit(solution)/shard_map/ppermute | solution.py:716
  13.0 22.1 %collective-permute-start.4 = (bf16[768,768]{1,0:T(8,128)(2,1)S(1)}, bf16[768,768]{1,0:T(8,128)(2,1)S(1)}, u32[]{:S(2)}, u32[]{:S(2)}) collective-permute-start(bf16[768,768]{1,0:T(8,128)(2,1)S(1)} %get-tuple-element.104), channel_id=1, source_target_pairs={{0,1},{1,0},{2,3},{3,2},{4,5},{5,4},{6,7},{7,6},{8,9},{9,8},{10,11... | collective-permute-start | bytes 3538952 | tf_op jit(solution)/shard_map/ppermute | solution.py:716
  13.5 21.6 %collective-permute-start.7 = (bf16[576,768]{1,0:T(8,128)(2,1)S(1)}, bf16[576,768]{1,0:T(8,128)(2,1)S(1)}, u32[]{:S(2)}, u32[]{:S(2)}) collective-permute-start(bf16[576,768]{1,0:T(8,128)(2,1)S(1)} %get-tuple-element.106), channel_id=1, source_target_pairs={{0,2},{1,3},{2,0},{3,1},{4,6},{5,7},{6,4},{7,5},{8,10},{9,11},{10,... | collective-permute-start | bytes 2654216 | tf_op jit(solution)/shard_map/ppermute | solution.py:716
  15.2 19.1 %collective-permute-start.6 = (bf16[10,48,384]{2,1,0:T(8,128)(2,1)S(1)}, bf16[10,48,384]{2,1,0:T(8,128)(2,1)S(1)}, u32[]{:S(2)}, u32[]{:S(2)}) collective-permute-start(bf16[10,48,384]{2,1,0:T(8,128)(2,1)S(1)} %get-tuple-element.100.refs_0_.refs_7_), channel_id=1, source_target_pairs={{0,16},{1,17},{2,18},{3,19},{4,20},{5,21},{6,22},{7,23},{8,24},{9,... | collective-permute-start | bytes 1105928 | tf_op jit(solution)/shard_map/ppermute | solution.py:716
  17.8 16.5 %collective-permute-start.5 = (bf16[10,48,384]{2,1,0:T(8,128)(2,1)S(1)}, bf16[10,48,384]{2,1,0:T(8,128)(2,1)S(1)}, u32[]{:S(2)}, u32[]{:S(2)}) collective-permute-start(bf16[10,48,384]{2,1,0:T(8,128)(2,1)S(1)} %get-tuple-element.100.refs_0_.refs_7_), channel_id=1, source_target_pairs={{0,4},{1,5},{2,6},{3,7},{4,0},{5,1},{6,2},{7,3},{8,12},{9,13},{10,... | collective-permute-start | bytes 1105928 | tf_op jit(solution)/shard_map/ppermute | solution.py:716
  35.7 20.9 %collective-permute-start.13 = (bf16[576,768]{1,0:T(8,128)(2,1)S(1)}, bf16[576,768]{1,0:T(8,128)(2,1)S(1)}, u32[]{:S(2)}, u32[]{:S(2)}) collective-permute-start(bf16[576,768]{1,0:T(8,128)(2,1)S(1)} %get-tuple-element.112), channel_id=1, source_target_pairs={{0,2},{1,3},{2,0},{3,1},{4,6},{5,7},{6,4},{7,5},{8,10},{9,11},{10,... | collective-permute-start | bytes 2654216 | tf_op jit(solution)/shard_map/ppermute | solution.py:716
  37.6 11.5 %collective-permute-start.11 = (bf16[10,48,384]{2,1,0:T(8,128)(2,1)S(1)}, bf16[10,48,384]{2,1,0:T(8,128)(2,1)S(1)}, u32[]{:S(2)}, u32[]{:S(2)}) collective-permute-start(bf16[10,48,384]{2,1,0:T(8,128)(2,1)S(1)} %get-tuple-element.110), channel_id=1, source_target_pairs={{0,4},{1,5},{2,6},{3,7},{4,0},{5,1},{6,2},{7,3},{8,12},{9,13},{10,... | collective-permute-start | bytes 1105928 | tf_op jit(solution)/shard_map/ppermute | solution.py:716
  39.1 17.1 %collective-permute-start.10 = (bf16[20,48,384]{2,1,0:T(8,128)(2,1)S(1)}, bf16[20,48,384]{2,1,0:T(8,128)(2,1)S(1)}, u32[]{:S(2)}, u32[]{:S(2)}) collective-permute-start(bf16[20,48,384]{2,1,0:T(8,128)(2,1)S(1)} %get-tuple-element.107.refs_2_), channel_id=1, source_target_pairs={{0,8},{1,9},{2,10},{3,11},{4,12},{5,13},{6,14},{7,15},{8,0},{9,1},... | collective-permute-start | bytes 2211848 | tf_op jit(solution)/shard_map/ppermute | solution.py:716
  40.6 15.5 %collective-permute-start.8 = (bf16[20,48,384]{2,1,0:T(8,128)(2,1)S(1)}, bf16[20,48,384]{2,1,0:T(8,128)(2,1)S(1)}, u32[]{:S(2)}, u32[]{:S(2)}) collective-permute-start(bf16[20,48,384]{2,1,0:T(8,128)(2,1)S(1)} %get-tuple-element.107.refs_2_), channel_id=1, source_target_pairs={{0,1},{1,0},{2,3},{3,2},{4,5},{5,4},{6,7},{7,6},{8,9},{9,8},{10,11... | collective-permute-start | bytes 2211848 | tf_op jit(solution)/shard_map/ppermute | solution.py:716
  40.7 14.8 %collective-permute-start.12 = (bf16[256,768]{1,0:T(8,128)(2,1)S(1)}, bf16[256,768]{1,0:T(8,128)(2,1)S(1)}, u32[]{:S(2)}, u32[]{:S(2)}) collective-permute-start(bf16[256,768]{1,0:T(8,128)(2,1)S(1)} %get-tuple-element.111), channel_id=1, source_target_pairs={{0,4},{1,5},{2,6},{3,7},{4,0},{5,1},{6,2},{7,3},{8,12},{9,13},{10,... | collective-permute-start | bytes 1179656 | tf_op jit(solution)/shard_map/ppermute | solution.py:716
  57.9 20.6 %collective-permute-start.18 = (bf16[512,768]{1,0:T(8,128)(2,1)S(1)}, bf16[512,768]{1,0:T(8,128)(2,1)S(1)}, u32[]{:S(2)}, u32[]{:S(2)}) collective-permute-start(bf16[512,768]{1,0:T(8,128)(2,1)S(1)} %get-tuple-element.119), channel_id=1, source_target_pairs={{0,2},{1,3},{2,0},{3,1},{4,6},{5,7},{6,4},{7,5},{8,10},{9,11},{10,... | collective-permute-start | bytes 2359304 | tf_op jit(solution)/shard_map/ppermute | solution.py:716
  59.6 16.4 %collective-permute-start.15 = (bf16[20,48,384]{2,1,0:T(8,128)(2,1)S(1)}, bf16[20,48,384]{2,1,0:T(8,128)(2,1)S(1)}, u32[]{:S(2)}, u32[]{:S(2)}) collective-permute-start(bf16[20,48,384]{2,1,0:T(8,128)(2,1)S(1)} %get-tuple-element.116.refs_4_), channel_id=1, source_target_pairs={{0,1},{1,0},{2,3},{3,2},{4,5},{5,4},{6,7},{7,6},{8,9},{9,8},{10,11... | collective-permute-start | bytes 2211848 | tf_op jit(solution)/shard_map/ppermute | solution.py:716
  59.6 18.9 %collective-permute-start.19 = (bf16[20,48,384]{2,1,0:T(8,128)(2,1)S(1)}, bf16[20,48,384]{2,1,0:T(8,128)(2,1)S(1)}, u32[]{:S(2)}, u32[]{:S(2)}) collective-permute-start(bf16[20,48,384]{2,1,0:T(8,128)(2,1)S(1)} %get-tuple-element.116.refs_4_), channel_id=1, source_target_pairs={{0,4},{1,5},{2,6},{3,7},{4,0},{5,1},{6,2},{7,3},{8,12},{9,13},{10,... | collective-permute-start | bytes 2211848 | tf_op jit(solution)/shard_map/ppermute | solution.py:716
  61.1 16.2 %collective-permute-start.20 = (bf16[384,768]{1,0:T(8,128)(2,1)S(1)}, bf16[384,768]{1,0:T(8,128)(2,1)S(1)}, u32[]{:S(2)}, u32[]{:S(2)}) collective-permute-start(bf16[384,768]{1,0:T(8,128)(2,1)S(1)} %get-tuple-element.120.refs_6_), channel_id=1, source_target_pairs={{0,8},{1,9},{2,10},{3,11},{4,12},{5,13},{6,14},{7,15},{8,0},{9,1},... | collective-permute-start | bytes 1769480 | tf_op jit(solution)/shard_map/ppermute | solution.py:716
  62.7 14.6 %collective-permute-start.17 = (bf16[256,768]{1,0:T(8,128)(2,1)S(1)}, bf16[256,768]{1,0:T(8,128)(2,1)S(1)}, u32[]{:S(2)}, u32[]{:S(2)}) collective-permute-start(bf16[256,768]{1,0:T(8,128)(2,1)S(1)} %get-tuple-element.118.refs_3_.refs_6_), channel_id=1, source_target_pairs={{0,1},{1,0},{2,3},{3,2},{4,5},{5,4},{6,7},{7,6},{8,9},{9,8},{10,11... | collective-permute-start | bytes 1179656 | tf_op jit(solution)/shard_map/ppermute | solution.py:716
  106.5 13.3 %collective-permute-start.25 = (bf16[2,4,80,384]{3,2,1,0:T(8,128)(2,1)S(1)}, bf16[2,4,80,384]{3,2,1,0:T(8,128)(2,1)S(1)}, u32[]{:S(2)}, u32[]{:S(2)}) collective-permute-start(bf16[2,4,80,384]{3,2,1,0:T(8,128)(2,1)S(1)} %get-tuple-element.146), channel_id=1, source_target_pairs={{0,2},{1,3},{2,0},{3,1},{4,6},{5,7},{6,4},{7,5},{8,10},{9,11},{10,... | collective-permute-start | bytes 1474568 | tf_op jit(solution)/shard_map/ppermute | solution.py:716
  107.2 13.0 %collective-permute-start.26 = (bf16[2,4,80,384]{3,2,1,0:T(8,128)(2,1)S(1)}, bf16[2,4,80,384]{3,2,1,0:T(8,128)(2,1)S(1)}, u32[]{:S(2)}, u32[]{:S(2)}) collective-permute-start(bf16[2,4,80,384]{3,2,1,0:T(8,128)(2,1)S(1)} %get-tuple-element.148), channel_id=1, source_target_pairs={{0,4},{1,5},{2,6},{3,7},{4,0},{5,1},{6,2},{7,3},{8,12},{9,13},{10,... | collective-permute-start | bytes 1474568 | tf_op jit(solution)/shard_map/ppermute | solution.py:716
  120.6 6.9 %collective-permute-start.27 = (bf16[4,80,384]{2,1,0:T(8,128)(2,1)S(1)}, bf16[4,80,384]{2,1,0:T(8,128)(2,1)S(1)}, u32[]{:S(2)}, u32[]{:S(2)}) collective-permute-start(bf16[4,80,384]{2,1,0:T(8,128)(2,1)S(1)} %get-tuple-element.155), channel_id=1, source_target_pairs={{0,4},{1,5},{2,6},{3,7},{4,0},{5,1},{6,2},{7,3},{8,12},{9,13},{10,... | collective-permute-start | bytes 737288 | tf_op jit(solution)/shard_map/ppermute | solution.py:716
  122.1 6.6 %collective-permute-start.28 = (bf16[4,80,384]{2,1,0:T(8,128)(2,1)S(1)}, bf16[4,80,384]{2,1,0:T(8,128)(2,1)S(1)}, u32[]{:S(2)}, u32[]{:S(2)}) collective-permute-start(bf16[4,80,384]{2,1,0:T(8,128)(2,1)S(1)} %get-tuple-element.157), channel_id=1, source_target_pairs={{0,2},{1,3},{2,0},{3,1},{4,6},{5,7},{6,4},{7,5},{8,10},{9,11},{10,... | collective-permute-start | bytes 737288 | tf_op jit(solution)/shard_map/ppermute | solution.py:716
  128.9 12.3 %collective-permute-start.29 = (bf16[80,768]{1,0:T(8,128)(2,1)S(1)}, bf16[80,768]{1,0:T(8,128)(2,1)S(1)}, u32[]{:S(2)}, u32[]{:S(2)}) collective-permute-start(bf16[80,768]{1,0:T(8,128)(2,1)S(1)} %get-tuple-element.169), channel_id=1, source_target_pairs={{0,8},{1,9},{2,10},{3,11},{4,12},{5,13},{6,14},{7,15},{8,0},{9,1},... | collective-permute-start | bytes 368648 | tf_op jit(solution)/shard_map/ppermute | solution.py:716
  130.5 10.7 %collective-permute-start.30 = (bf16[80,768]{1,0:T(8,128)(2,1)S(1)}, bf16[80,768]{1,0:T(8,128)(2,1)S(1)}, u32[]{:S(2)}, u32[]{:S(2)}) collective-permute-start(bf16[80,768]{1,0:T(8,128)(2,1)S(1)} %get-tuple-element.170), channel_id=1, source_target_pairs={{0,16},{1,17},{2,18},{3,19},{4,20},{5,21},{6,22},{7,23},{8,24},{9,... | collective-permute-start | bytes 368648 | tf_op jit(solution)/shard_map/ppermute | solution.py:716
  133.1 8.1 %collective-permute-start.31 = (bf16[80,768]{1,0:T(8,128)(2,1)S(1)}, bf16[80,768]{1,0:T(8,128)(2,1)S(1)}, u32[]{:S(2)}, u32[]{:S(2)}) collective-permute-start(bf16[80,768]{1,0:T(8,128)(2,1)S(1)} %get-tuple-element.171), channel_id=1, source_target_pairs={{0,24},{1,25},{2,26},{3,27},{4,28},{5,29},{6,30},{7,31},{8,16},{9,... | collective-permute-start | bytes 368648 | tf_op jit(solution)/shard_map/ppermute | solution.py:716
  (25 other events, 132.9 us)

commit v4 on v3

--- a/solution.py
+++ b/solution.py
@@ -286,7 +286,8 @@
 
 def merging(n_adapters, meta, lengths, sums, lines, out_grad, matrices, *refs):
     layer_out, part_out, fquery_out, middle_out, keep_out, send_out = refs[:6]
-    grads, sum_lines, states, probes, blends, values, fqueries = refs[6:]
+    grads, sum_lines, states, probes, blends, values, fqueries, joined, sem = refs[6:]
+    leave = pltpu.make_async_copy(joined, layer_out, sem)
     seq, width = sums.shape
     scale = width**-0.5
     down, up, query, key, value = (matrices.at[i] for i in range(5))
@@ -333,7 +334,8 @@
         blended = blended.astype(BF16)
         blends[rows] = blended
         normed3, inv_std3 = normalize(second + dot(blended, value[...]))
-        layer_out[rows] = normed3 * gain3 + shift3
+        joined[...] = normed3 * gain3 + shift3
+        leave.start()
 
         token = rows.start + lax.broadcasted_iota(jnp.int32, (rows.size, 1), 0)
         keep = jnp.where(token < count, 1.0, 0.0)
@@ -388,6 +390,8 @@
             block = [grads[i, pl.ds(first, rows)] for i in range(3)] + [tail]
             out[x_rel, y_rel, z_rel] = jnp.concatenate(block, axis=0).astype(BF16)
 
+    leave.wait()
+
 
 def call_merging(n_adapters, meta, lengths, sums, lines, out_grad, matrices):
     seq, width = sums.shape
@@ -395,12 +399,13 @@
     return pl.pallas_call(
         functools.partial(merging, n_adapters),
         in_specs=[SMEM, SMEM] + [VMEM] * 4,
-        out_specs=[VMEM] * 6,
+        out_specs=[ANY] + [VMEM] * 5,
         out_shape=[sds((seq, width), F32)] * 2
         + [sds((seq, width), BF16)] * 2
         + [sds((2, 2, 4, block, width), BF16)] * 2,
         scratch_shapes=[pltpu.VMEM((3, width, width), F32), pltpu.VMEM((8, width), F32)]
-        + [pltpu.VMEM((seq, width), BF16)] * 5,
+        + [pltpu.VMEM((seq, width), BF16)] * 5
+        + [pltpu.VMEM((seq, width), F32), pltpu.SemaphoreType.DMA],
         compiler_params=params(MERGE_MIB),
         cost_estimate=cost(18),
         name="merging",
@@ -472,9 +477,8 @@
     )(grad_low, before, *slopes, *in_quarters, *out_quarters, *for_norm)
 
 
-def attend_backward(
-    columns, unroll, grad_low, before, turned_ref, att_ref, prob_ref, weight, input_grad, token, grad_turned, grad_att
-):
+def attend_backward(columns, unroll, leaving, grad_low, before, turned_ref, att_ref, prob_ref, weight, *refs):
+    input_grad, token, grad_turned, grad_att = refs[:4]
     width = 3 * HEAD_DIM
     root = HEAD_DIM**-0.5
     grad_att[...] = dot_last(weight[columns:], grad_low[...]).astype(BF16)
@@ -493,21 +497,36 @@
         grad_turned[places[1]] = (dot_last(queries, grad_scores) * root).astype(BF16)
         grad_turned[places[2]] = dot_last(grad, prob).astype(BF16)
 
-    input_grad[...] = before[...] + dot(grad_turned[...].T, weight[:columns])
     token[...] = jnp.zeros_like(token)
-
-
-def call_attend_backward(deps, columns, unroll, grad_low, before, saved, quarter):
+    grads = grad_turned[...].T
+    if not leaving:
+        input_grad[...] = before[...] + dot(grads, weight[:columns])
+        return
+    total, sems = refs[4:]
+    parts = [slice(i, i + CHUNK) for i in range(0, before.shape[0], CHUNK)]
+    copies = [
+        pltpu.make_async_copy(total.at[part], input_grad.at[part], sems.at[i])
+        for i, part in enumerate(parts)
+    ]
+    for part, copy in zip(parts, copies):
+        total[part] = before[part] + dot(grads[part], weight[:columns])
+        copy.start()
+    for copy in copies:
+        copy.wait()
+
+
+def call_attend_backward(deps, columns, unroll, leaving, grad_low, before, saved, quarter):
     seq, width = before.shape
     inner = columns // 3
     return kernel(
-        functools.partial(attend_backward, columns, unroll),
+        functools.partial(attend_backward, columns, unroll, leaving),
         deps,
         ATTEND_MIB,
         in_specs=[VMEM] * 6,
-        out_specs=[VMEM] * 2,
+        out_specs=[ANY if leaving else VMEM, VMEM],
         out_shape=[sds((seq, width), F32), sds((8, LANES), F32)],
-        scratch_shapes=[pltpu.VMEM((columns, seq), BF16), pltpu.VMEM((inner, seq), BF16)],
+        scratch_shapes=[pltpu.VMEM((columns, seq), BF16), pltpu.VMEM((inner, seq), BF16)]
+        + [pltpu.VMEM((seq, width), F32), pltpu.SemaphoreType.DMA((seq // CHUNK,))] * leaving,
         cost_estimate=cost(8),
         name="attend_backward",
     )(grad_low, before, *saved, quarter)
@@ -758,7 +777,7 @@
         )
     (low,) = rest
     for quarter, kept in zip(attn, saved):
-        total, _ = call_attend_backward([], columns, False, low, total, kept, quarter)
+        total, _ = call_attend_backward([], columns, False, False, low, total, kept, quarter)
     mass = totals[2, :n_adapters] / totals[2, n_adapters]
     return (layer_out, total, squares[0], squares[1], squares[2], totals[0], totals[1], mass)
 
@@ -904,8 +923,9 @@
     def attention(deps, *quarters):
         for i in quarters:
             done["sum"], token = call_attend_backward(
-                deps, columns, i > 1, done["low"], done["sum"], saved[i], attn_quarters[i]
+                deps, columns, i > 1, i == 3, done["low"], done["sum"], saved[i], attn_quarters[i]
             )
+            deps = [token]
         return token
 
     def near(deps):

time: 142 us -> 141 us (level)
  Pallas kernels: 77.5 us -> 75.6 us
  transfers between devices with their start and end apart: 32 -> 32, of which waited for: 15 -> 16; matrix products, arithmetic and copies ran while one was open for 0% -> 0% of each run, Pallas kernels for 39% -> 39%
where the time goes in v4:
time: 141 us; the launch traced here: 140 us
  Pallas kernels  75.6 us (54%)
  waiting for transfers between devices  32 us (23%)
  starting transfers between devices  31.3 us (22%)
    ppermute x32, waiting for transfers between devices, flip(): return lax.ppermute(array, AXES, [(i, i ^ bits) for i in range(self.count)])  32 us
    ppermute x32, starting transfers between devices, flip(): return lax.ppermute(array, AXES, [(i, i ^ bits) for i in range(self.count)])  31.3 us
    pallas_call x2, Pallas kernels, call_attend_forward(): kernel(functools.partial(attend_forward, columns, last), deps, ATTEND_MIB...  18.6 us
    pallas_call x4, Pallas kernels, call_attend_backward(): kernel(functools.partial(attend_backward, columns, unroll, leaving), deps...  14.3 us
    pallas_call x1, Pallas kernels, call_merging(): pl.pallas_call(functools.partial(merging, n_adapters), in_specs=[SMEM, SM...  14 us
    pallas_call x3, Pallas kernels, call_ffn_forward(): kernel(functools.partial(ffn_forward, quarters, len(out_quarters) // quar...  8.3 us
    pallas_call x2, Pallas kernels, call_ffn_backward(): kernel(functools.partial(ffn_backward, last, len(out_quarters) // 2, len(...  6.54 us
  transfers between devices with their start and end apart: 32, of which 16 were waited for; matrix products, arithmetic and copies ran while one was open for 0% of the time, Pallas kernels for 39%

profile of v4, /device:TPU:0, one launch (start us, length us, event | category | flops | bytes accessed | tf_op | source)
XLA Modules:
  0.0 140.4 jit_solution(14026797486849900981)
XLA Ops:
  4.5 2.9 %collective-permute-start.2 = (bf16[5,48,384]{2,1,0:T(8,128)(2,1)S(1)}, bf16[5,48,384]{2,1,0:T(8,128)(2,1)S(1)}, u32[]{:S(2)}, u32[]{:S(2)}) collective-permute-start(bf16[5,48,384]{2,1,0:T(8,128)(2,1)S(1)} %get-tuple-element.100.refs_5_), channel_id=1, source_target_pairs={{0,2},{1,3},{2,0},{3,1},{4,6},{5,7},{6,4},{7,5},{8,10},{9,11},{10,... | collective-permute-start | bytes 552968 | tf_op jit(solution)/shard_map/ppermute | solution.py:735
  7.4 2.0 %prepare_shares.1 = (bf16[576,768]{1,0:T(8,128)(2,1)S(1)}, bf16[576,768]{1,0:T(8,128)(2,1)S(1)}, bf16[512,768]{1,0:T(8,128)(2,1)S(1)}, bf16[768,768]{1,0:T(8,128)(2,1)S(1)}, bf16[768,768]{1,0:T(8,128)(2,1)S(1)}) custom-call(s32[6]{0:T(128)S(1)} %stack.27.meta.refs_0_.refs_1_.refs_3_.refs_2_, bf16[768,768]{1,0:T(8,128)(2,1)S(1)} %get-tuple-element.96.refs_1_.refs_6_.refs_5_, ...), custom_call_target="tpu_custom_call" | custom-call | bytes 1024 | tf_op jit(solution)/shard_map/prepare_shares/pallas_call | solution.py:610
  9.4 2.9 %collective-permute-done.2.refs_6_ = bf16[5,48,384]{2,1,0:T(8,128)(2,1)S(1)} collective-permute-done((bf16[5,48,384]{2,1,0:T(8,128)(2,1)S(1)}, bf16[5,48,384]{2,1,0:T(8,128)(2,1)S(1)}, u32[]{:S(2)}, u32[]{:S(2)}) %collective-permute-start.2) | collective-permute-done | bytes 184352 | tf_op jit(solution)/shard_map/ppermute | solution.py:735
  13.5 1.7 %collective-permute-start.7 = (bf16[576,768]{1,0:T(8,128)(2,1)S(1)}, bf16[576,768]{1,0:T(8,128)(2,1)S(1)}, u32[]{:S(2)}, u32[]{:S(2)}) collective-permute-start(bf16[576,768]{1,0:T(8,128)(2,1)S(1)} %get-tuple-element.107), channel_id=1, source_target_pairs={{0,2},{1,3},{2,0},{3,1},{4,6},{5,7},{6,4},{7,5},{8,10},{9,11},{10,... | collective-permute-start | bytes 2654216 | tf_op jit(solution)/shard_map/ppermute | solution.py:735
  15.2 2.6 %collective-permute-start.6 = (bf16[10,48,384]{2,1,0:T(8,128)(2,1)S(1)}, bf16[10,48,384]{2,1,0:T(8,128)(2,1)S(1)}, u32[]{:S(2)}, u32[]{:S(2)}) collective-permute-start(bf16[10,48,384]{2,1,0:T(8,128)(2,1)S(1)} %get-tuple-element.101.refs_0_.refs_7_), channel_id=1, source_target_pairs={{0,16},{1,17},{2,18},{3,19},{4,20},{5,21},{6,22},{7,23},{8,24},{9,... | collective-permute-start | bytes 1105928 | tf_op jit(solution)/shard_map/ppermute | solution.py:735
  19.3 8.9 %attend_forward.2 = (bf16[576,512]{1,0:T(8,128)(2,1)}, bf16[192,512]{1,0:T(8,128)(2,1)}, bf16[3,512,512]{2,1,0:T(8,128)(2,1)}, bf16[576,512]{1,0:T(8,128)(2,1)},...) custom-call(bf16[10,48,384]{2,1,0:T(8,128)(2,1)S(1)} %get-tuple-element.101.refs_0_.refs_7_, ...), custom_call_target="tpu_custom_call" | custom-call | bytes 1024 | tf_op jit(solution)/shard_map/attend_forward/pallas_call | solution.py:193
  28.2 6.1 %collective-permute-done.6.refs_8_ = bf16[10,48,384]{2,1,0:T(8,128)(2,1)S(1)} collective-permute-done((bf16[10,48,384]{2,1,0:T(8,128)(2,1)S(1)}, bf16[10,48,384]{2,1,0:T(8,128)(2,1)S(1)}, u32[]{:S(2)}, u32[]{:S(2)}) %collective-permute-start.6) | collective-permute-done | bytes 368672 | tf_op jit(solution)/shard_map/ppermute | solution.py:735
  35.7 1.8 %collective-permute-start.13 = (bf16[576,768]{1,0:T(8,128)(2,1)S(1)}, bf16[576,768]{1,0:T(8,128)(2,1)S(1)}, u32[]{:S(2)}, u32[]{:S(2)}) collective-permute-start(bf16[576,768]{1,0:T(8,128)(2,1)S(1)} %get-tuple-element.113), channel_id=1, source_target_pairs={{0,2},{1,3},{2,0},{3,1},{4,6},{5,7},{6,4},{7,5},{8,10},{9,11},{10,... | collective-permute-start | bytes 2654216 | tf_op jit(solution)/shard_map/ppermute | solution.py:735
  41.2 7.9 %collective-permute-done.11.refs_5_ = bf16[10,48,384]{2,1,0:T(8,128)(2,1)S(1)} collective-permute-done((bf16[10,48,384]{2,1,0:T(8,128)(2,1)S(1)}, bf16[10,48,384]{2,1,0:T(8,128)(2,1)S(1)}, u32[]{:S(2)}, u32[]{:S(2)}) %collective-permute-start.11) | collective-permute-done | bytes 368672 | tf_op jit(solution)/shard_map/ppermute | solution.py:735
  50.8 4.7 %collective-permute-done.12.refs_9_.refs_10_ = bf16[256,768]{1,0:T(8,128)(2,1)S(1)} collective-permute-done((bf16[256,768]{1,0:T(8,128)(2,1)S(1)}, bf16[256,768]{1,0:T(8,128)(2,1)S(1)}, u32[]{:S(2)}, u32[]{:S(2)}) %collective-permute-start.12) | collective-permute-done | bytes 393248 | tf_op jit(solution)/shard_map/ppermute | solution.py:735
  62.7 9.7 %attend_forward.3 = (bf16[576,512]{1,0:T(8,128)(2,1)}, bf16[192,512]{1,0:T(8,128)(2,1)}, bf16[3,512,512]{2,1,0:T(8,128)(2,1)}, bf16[576,512]{1,0:T(8,128)(2,1)},...) custom-call(s32[6]{0:T(128)S(1)} %stack.27.meta.refs_0_.refs_1_.refs, ...), custom_call_target="tpu_custom_call" | custom-call | bytes 1024 | tf_op jit(solution)/shard_map/attend_forward/pallas_call | solution.py:193
  72.5 3.5 %ffn_forward.3 = (bf16[2,512,768]{2,1,0:T(8,128)(2,1)S(1)}, f32[512,768]{1,0:T(8,128)S(1)}) custom-call(f32[512,768]{1,0:T(8,128)S(1)} %get-tuple-element.115.refs_0_.refs_1_, f32[512,768]{1,0:T(8,128)S(1)} %get-tuple-element.115.refs_0_.refs_1_, bf16[768,768]{1,0:T(8,128)(2,1)S(1)} %copy-done, ...), custom_call_target="tpu_custom_call" | custom-call | bytes 1024 | tf_op jit(solution)/shard_map/ffn_forward/pallas_call | solution.py:231
  79.8 2.4 %ffn_forward.4 = (bf16[1,512,768]{2,1,0:T(8,128)(2,1)S(1)}, f32[512,768]{1,0:T(8,128)S(1)}) custom-call(f32[512,768]{1,0:T(8,128)S(1)} %get-tuple-element.115.refs_0_.refs_1_, f32[512,768]{1,0:T(8,128)S(1)} %get-tuple-element.116.refs_0_.refs_1_, bf16[768,768]{1,0:T(8,128)(2,1)S(1)} %get-tuple-element.122.refs_2_.refs_4_, ...), custom_call_target="tpu_custom_call" | custom-call | bytes 1024 | tf_op jit(solution)/shard_map/ffn_forward/pallas_call | solution.py:231
  83.2 2.4 %ffn_forward.5 = (bf16[1,512,768]{2,1,0:T(8,128)(2,1)S(1)}, f32[512,768]{1,0:T(8,128)S(1)}) custom-call(f32[512,768]{1,0:T(8,128)S(1)} %get-tuple-element.115.refs_0_.refs_1_, f32[512,768]{1,0:T(8,128)S(1)} %get-tuple-element.124.refs_1_, bf16[768,768]{1,0:T(8,128)(2,1)S(1)} %collective-permute-done.21.refs_2_.refs_5_, ...), custom_call_target="tpu_custom_call" | custom-call | bytes 1024 | tf_op jit(solution)/shard_map/ffn_forward/pallas_call | solution.py:231
  86.8 14.0 %merging.1 = (f32[512,768]{1,0:T(8,128)}, f32[512,768]{1,0:T(8,128)S(1)}, bf16[512,768]{1,0:T(8,128)(2,1)S(1)}, bf16[512,768]{1,0:T(8,128)(2,1)S(1)}, bf16[2,2,4...) custom-call(s32[6]{0:T(128)S(1)} %stack.27.meta.refs_0_.refs_1_.refs_3_.refs_2_, ...), custom_call_target="tpu_custom_call" | custom-call | bytes 1024 | tf_op jit(solution)/shard_map/merging/pallas_call | solution.py:399
  101.0 2.0 %merging_input.1 = (f32[512,768]{1,0:T(8,128)S(1)}, bf16[512,768]{1,0:T(8,128)(2,1)S(1)}) custom-call(f32[512,768]{1,0:T(8,128)S(1)} %get-tuple-element.125.refs_0_.sums, f32[8,768]{1,0:T(8,128)S(1)} %get-tuple-element.102.refs_5_.refs_4_.lines.refs_1_.refs_12_, f32[512,768]{1,0:T(8,128)S(1)} %get-tuple-element.128.refs_2_, ...), custom_call_target="tpu_custom_call" | custom-call | bytes 1024 | tf_op jit(solution)/shard_map/merging_input/pallas_call | solution.py:428
  103.0 1.8 %collective-permute-done.24.refs_2_ = bf16[2,2,4,80,768]{4,3,2,1,0:T(8,128)(2,1)S(1)} collective-permute-done((bf16[2,2,4,80,768]{4,3,2,1,0:T(8,128)(2,1)S(1)}, bf16[2,2,4,80,768]{4,3,2,1,0:T(8,128)(2,1)S(1)}, u32[]{:S(2)}, u32[]{:S(2)}) %collective-permute-start.24) | collective-permute-done | bytes 1966112 | tf_op jit(solution)/shard_map/ppermute | solution.py:735
  107.7 3.1 %ffn_backward.2.refs_1_ = f32[512,768]{1,0:T(8,128)S(1)} custom-call(bf16[2,4,80,384]{3,2,1,0:T(8,128)(2,1)S(1)} %get-tuple-element.135.refs_0_.refs_1_, bf16[512,768]{1,0:T(8,128)(2,1)S(1)} %get-tuple-element.131.refs_1_.refs_0_, f32[512,768]{1,0:T(8,128)S(1)} %get-tuple-element.132.refs_0_.refs_2_, bf16[2,512,768]{2,1,0:T(8,128)(2,1)S(1)} %get-tuple-element.136.refs_3_, ...), custom_call_target="tpu_custom_call" | custom-call | bytes 1024 | tf_op jit(solution)/shard_map/ffn_backward/pallas_call | solution.py:468
  110.9 3.4 %ffn_backward.3 = (f32[512,768]{1,0:T(8,128)S(1)}, bf16[512,768]{1,0:T(8,128)(2,1)S(1)}) custom-call(bf16[512,768]{1,0:T(8,128)(2,1)S(1)} %get-tuple-element.131.refs_1_.refs_0_, f32[512,768]{1,0:T(8,128)S(1)} %ffn_backward.2.refs_1_, bf16[1,512,768]{2,1,0:T(8,128)(2,1)S(1)} %get-tuple-element.137.refs_2_, ...), custom_call_target="tpu_custom_call" | custom-call | bytes 1024 | tf_op jit(solution)/shard_map/ffn_backward/pallas_call | solution.py:468
  114.3 3.6 %attend_backward.4 = (f32[512,768]{1,0:T(8,128)S(1)}, f32[8,128]{1,0:T(8,128)S(1)}) custom-call(bf16[512,768]{1,0:T(8,128)(2,1)S(1)} %get-tuple-element.141.refs_0_.refs_1_, f32[512,768]{1,0:T(8,128)S(1)} %get-tuple-element.142.refs_1_, bf16[576,512]{1,0:T(8,128)(2,1)S(1)} %copy-done.9, bf16[192,512]{1,0:T(8,128)(2,1)S(1)} %copy-done.13, ...), custom_call_target="tpu_custom_call" | custom-call | bytes 1024 | tf_op jit(solution)/shard_map/attend_backward/pallas_call | solution.py:521
  122.5 3.6 %attend_backward.5 = (f32[512,768]{1,0:T(8,128)S(1)}, f32[8,128]{1,0:T(8,128)S(1)}) custom-call(bf16[4,80,384]{2,1,0:T(8,128)(2,1)S(1)} %get-tuple-element.150.refs_0_.refs_1_, bf16[512,768]{1,0:T(8,128)(2,1)S(1)} %get-tuple-element.141.refs_0_.refs_1_, f32[512,768]{1,0:T(8,128)S(1)} %get-tuple-element.151.refs_2_, bf16[576,512]{1,0:T(8,128)(2,1)S(1)} %copy-done.8, ...), custom_call_target="tpu_custom_call" | custom-call | bytes 1024 | tf_op jit(solution)/shard_map/attend_backward/pallas_call | solution.py:521
  129.4 2.6 %collective-permute-start.30 = (bf16[80,768]{1,0:T(8,128)(2,1)S(1)}, bf16[80,768]{1,0:T(8,128)(2,1)S(1)}, u32[]{:S(2)}, u32[]{:S(2)}) collective-permute-start(bf16[80,768]{1,0:T(8,128)(2,1)S(1)} %get-tuple-element.172), channel_id=1, source_target_pairs={{0,16},{1,17},{2,18},{3,19},{4,20},{5,21},{6,22},{7,23},{8,24},{9,... | collective-permute-start | bytes 368648 | tf_op jit(solution)/shard_map/ppermute | solution.py:735
  132.3 3.1 %attend_backward.6 = (f32[512,768]{1,0:T(8,128)S(1)}, f32[8,128]{1,0:T(8,128)S(1)}) custom-call(bf16[80,768]{1,0:T(8,128)(2,1)S(1)} %get-tuple-element.159.refs_0_.refs_1_, bf16[512,768]{1,0:T(8,128)(2,1)S(1)} %get-tuple-element.141.refs_0_.refs_1_, f32[512,768]{1,0:T(8,128)S(1)} %get-tuple-element.160.refs_2_, bf16[576,512]{1,0:T(8,128)(2,1)S(1)} %copy-done.11, ...), custom_call_target="tpu_custom_call" | custom-call | bytes 1024 | tf_op jit(solution)/shard_map/attend_backward/pallas_call | solution.py:521
  135.4 4.0 %attend_backward.7 = (f32[512,768]{1,0:T(8,128)}, f32[8,128]{1,0:T(8,128)S(1)}) custom-call(f32[8,128]{1,0:T(8,128)S(1)} %get-tuple-element.164.refs_0_, bf16[512,768]{1,0:T(8,128)(2,1)S(1)} %get-tuple-element.141.refs_0_.refs_1_, f32[512,768]{1,0:T(8,128)S(1)} %get-tuple-element.165.refs_2_, bf16[576,512]{1,0:T(8,128)(2,1)S(1)} %copy-done.10, ...), custom_call_target="tpu_custom_call" | custom-call | bytes 1024 | tf_op jit(solution)/shard_map/attend_backward/pallas_call | solution.py:521
  (103 shorter events, 38.5 us)
Async XLA Ops:
  4.4 7.9 %collective-permute-start.1 = (bf16[768,768]{1,0:T(8,128)(2,1)S(1)}, bf16[768,768]{1,0:T(8,128)(2,1)S(1)}, u32[]{:S(2)}, u32[]{:S(2)}) collective-permute-start(bf16[768,768]{1,0:T(8,128)(2,1)S(1)} %get-tuple-element.96.refs_1_.refs_6_.refs_5_), channel_id=1, source_target_pairs={{0,1},{1,0},{2,3},{3,2},{4,5},{5,4},{6,7},{7,6},{8,9},{9,8},{10,11... | collective-permute-start | bytes 3538952 | tf_op jit(solution)/shard_map/ppermute | solution.py:735
  4.5 7.8 %collective-permute-start.2 = (bf16[5,48,384]{2,1,0:T(8,128)(2,1)S(1)}, bf16[5,48,384]{2,1,0:T(8,128)(2,1)S(1)}, u32[]{:S(2)}, u32[]{:S(2)}) collective-permute-start(bf16[5,48,384]{2,1,0:T(8,128)(2,1)S(1)} %get-tuple-element.100.refs_5_), channel_id=1, source_target_pairs={{0,2},{1,3},{2,0},{3,1},{4,6},{5,7},{6,4},{7,5},{8,10},{9,11},{10,... | collective-permute-start | bytes 552968 | tf_op jit(solution)/shard_map/ppermute | solution.py:735
  12.9 22.2 %collective-permute-start.3 = (bf16[768,768]{1,0:T(8,128)(2,1)S(1)}, bf16[768,768]{1,0:T(8,128)(2,1)S(1)}, u32[]{:S(2)}, u32[]{:S(2)}) collective-permute-start(bf16[768,768]{1,0:T(8,128)(2,1)S(1)} %get-tuple-element.104), channel_id=1, source_target_pairs={{0,1},{1,0},{2,3},{3,2},{4,5},{5,4},{6,7},{7,6},{8,9},{9,8},{10,11... | collective-permute-start | bytes 3538952 | tf_op jit(solution)/shard_map/ppermute | solution.py:735
  13.0 22.1 %collective-permute-start.4 = (bf16[768,768]{1,0:T(8,128)(2,1)S(1)}, bf16[768,768]{1,0:T(8,128)(2,1)S(1)}, u32[]{:S(2)}, u32[]{:S(2)}) collective-permute-start(bf16[768,768]{1,0:T(8,128)(2,1)S(1)} %get-tuple-element.105), channel_id=1, source_target_pairs={{0,1},{1,0},{2,3},{3,2},{4,5},{5,4},{6,7},{7,6},{8,9},{9,8},{10,11... | collective-permute-start | bytes 3538952 | tf_op jit(solution)/shard_map/ppermute | solution.py:735
  13.5 21.6 %collective-permute-start.7 = (bf16[576,768]{1,0:T(8,128)(2,1)S(1)}, bf16[576,768]{1,0:T(8,128)(2,1)S(1)}, u32[]{:S(2)}, u32[]{:S(2)}) collective-permute-start(bf16[576,768]{1,0:T(8,128)(2,1)S(1)} %get-tuple-element.107), channel_id=1, source_target_pairs={{0,2},{1,3},{2,0},{3,1},{4,6},{5,7},{6,4},{7,5},{8,10},{9,11},{10,... | collective-permute-start | bytes 2654216 | tf_op jit(solution)/shard_map/ppermute | solution.py:735
  15.2 19.1 %collective-permute-start.6 = (bf16[10,48,384]{2,1,0:T(8,128)(2,1)S(1)}, bf16[10,48,384]{2,1,0:T(8,128)(2,1)S(1)}, u32[]{:S(2)}, u32[]{:S(2)}) collective-permute-start(bf16[10,48,384]{2,1,0:T(8,128)(2,1)S(1)} %get-tuple-element.101.refs_0_.refs_7_), channel_id=1, source_target_pairs={{0,16},{1,17},{2,18},{3,19},{4,20},{5,21},{6,22},{7,23},{8,24},{9,... | collective-permute-start | bytes 1105928 | tf_op jit(solution)/shard_map/ppermute | solution.py:735
  17.8 16.5 %collective-permute-start.5 = (bf16[10,48,384]{2,1,0:T(8,128)(2,1)S(1)}, bf16[10,48,384]{2,1,0:T(8,128)(2,1)S(1)}, u32[]{:S(2)}, u32[]{:S(2)}) collective-permute-start(bf16[10,48,384]{2,1,0:T(8,128)(2,1)S(1)} %get-tuple-element.101.refs_0_.refs_7_), channel_id=1, source_target_pairs={{0,4},{1,5},{2,6},{3,7},{4,0},{5,1},{6,2},{7,3},{8,12},{9,13},{10,... | collective-permute-start | bytes 1105928 | tf_op jit(solution)/shard_map/ppermute | solution.py:735
  35.7 20.9 %collective-permute-start.13 = (bf16[576,768]{1,0:T(8,128)(2,1)S(1)}, bf16[576,768]{1,0:T(8,128)(2,1)S(1)}, u32[]{:S(2)}, u32[]{:S(2)}) collective-permute-start(bf16[576,768]{1,0:T(8,128)(2,1)S(1)} %get-tuple-element.113), channel_id=1, source_target_pairs={{0,2},{1,3},{2,0},{3,1},{4,6},{5,7},{6,4},{7,5},{8,10},{9,11},{10,... | collective-permute-start | bytes 2654216 | tf_op jit(solution)/shard_map/ppermute | solution.py:735
  37.6 11.5 %collective-permute-start.11 = (bf16[10,48,384]{2,1,0:T(8,128)(2,1)S(1)}, bf16[10,48,384]{2,1,0:T(8,128)(2,1)S(1)}, u32[]{:S(2)}, u32[]{:S(2)}) collective-permute-start(bf16[10,48,384]{2,1,0:T(8,128)(2,1)S(1)} %get-tuple-element.111), channel_id=1, source_target_pairs={{0,4},{1,5},{2,6},{3,7},{4,0},{5,1},{6,2},{7,3},{8,12},{9,13},{10,... | collective-permute-start | bytes 1105928 | tf_op jit(solution)/shard_map/ppermute | solution.py:735
  39.1 17.1 %collective-permute-start.10 = (bf16[20,48,384]{2,1,0:T(8,128)(2,1)S(1)}, bf16[20,48,384]{2,1,0:T(8,128)(2,1)S(1)}, u32[]{:S(2)}, u32[]{:S(2)}) collective-permute-start(bf16[20,48,384]{2,1,0:T(8,128)(2,1)S(1)} %get-tuple-element.108.refs_2_), channel_id=1, source_target_pairs={{0,8},{1,9},{2,10},{3,11},{4,12},{5,13},{6,14},{7,15},{8,0},{9,1},... | collective-permute-start | bytes 2211848 | tf_op jit(solution)/shard_map/ppermute | solution.py:735
  40.6 15.5 %collective-permute-start.8 = (bf16[20,48,384]{2,1,0:T(8,128)(2,1)S(1)}, bf16[20,48,384]{2,1,0:T(8,128)(2,1)S(1)}, u32[]{:S(2)}, u32[]{:S(2)}) collective-permute-start(bf16[20,48,384]{2,1,0:T(8,128)(2,1)S(1)} %get-tuple-element.108.refs_2_), channel_id=1, source_target_pairs={{0,1},{1,0},{2,3},{3,2},{4,5},{5,4},{6,7},{7,6},{8,9},{9,8},{10,11... | collective-permute-start | bytes 2211848 | tf_op jit(solution)/shard_map/ppermute | solution.py:735
  40.7 14.8 %collective-permute-start.12 = (bf16[256,768]{1,0:T(8,128)(2,1)S(1)}, bf16[256,768]{1,0:T(8,128)(2,1)S(1)}, u32[]{:S(2)}, u32[]{:S(2)}) collective-permute-start(bf16[256,768]{1,0:T(8,128)(2,1)S(1)} %get-tuple-element.112), channel_id=1, source_target_pairs={{0,4},{1,5},{2,6},{3,7},{4,0},{5,1},{6,2},{7,3},{8,12},{9,13},{10,... | collective-permute-start | bytes 1179656 | tf_op jit(solution)/shard_map/ppermute | solution.py:735
  57.9 20.6 %collective-permute-start.18 = (bf16[512,768]{1,0:T(8,128)(2,1)S(1)}, bf16[512,768]{1,0:T(8,128)(2,1)S(1)}, u32[]{:S(2)}, u32[]{:S(2)}) collective-permute-start(bf16[512,768]{1,0:T(8,128)(2,1)S(1)} %get-tuple-element.120), channel_id=1, source_target_pairs={{0,2},{1,3},{2,0},{3,1},{4,6},{5,7},{6,4},{7,5},{8,10},{9,11},{10,... | collective-permute-start | bytes 2359304 | tf_op jit(solution)/shard_map/ppermute | solution.py:735
  59.6 16.4 %collective-permute-start.15 = (bf16[20,48,384]{2,1,0:T(8,128)(2,1)S(1)}, bf16[20,48,384]{2,1,0:T(8,128)(2,1)S(1)}, u32[]{:S(2)}, u32[]{:S(2)}) collective-permute-start(bf16[20,48,384]{2,1,0:T(8,128)(2,1)S(1)} %get-tuple-element.117.refs_4_), channel_id=1, source_target_pairs={{0,1},{1,0},{2,3},{3,2},{4,5},{5,4},{6,7},{7,6},{8,9},{9,8},{10,11... | collective-permute-start | bytes 2211848 | tf_op jit(solution)/shard_map/ppermute | solution.py:735
  59.6 18.9 %collective-permute-start.19 = (bf16[20,48,384]{2,1,0:T(8,128)(2,1)S(1)}, bf16[20,48,384]{2,1,0:T(8,128)(2,1)S(1)}, u32[]{:S(2)}, u32[]{:S(2)}) collective-permute-start(bf16[20,48,384]{2,1,0:T(8,128)(2,1)S(1)} %get-tuple-element.117.refs_4_), channel_id=1, source_target_pairs={{0,4},{1,5},{2,6},{3,7},{4,0},{5,1},{6,2},{7,3},{8,12},{9,13},{10,... | collective-permute-start | bytes 2211848 | tf_op jit(solution)/shard_map/ppermute | solution.py:735
  61.1 16.2 %collective-permute-start.20 = (bf16[384,768]{1,0:T(8,128)(2,1)S(1)}, bf16[384,768]{1,0:T(8,128)(2,1)S(1)}, u32[]{:S(2)}, u32[]{:S(2)}) collective-permute-start(bf16[384,768]{1,0:T(8,128)(2,1)S(1)} %get-tuple-element.121.refs_6_), channel_id=1, source_target_pairs={{0,8},{1,9},{2,10},{3,11},{4,12},{5,13},{6,14},{7,15},{8,0},{9,1},... | collective-permute-start | bytes 1769480 | tf_op jit(solution)/shard_map/ppermute | solution.py:735
  62.7 14.6 %collective-permute-start.17 = (bf16[256,768]{1,0:T(8,128)(2,1)S(1)}, bf16[256,768]{1,0:T(8,128)(2,1)S(1)}, u32[]{:S(2)}, u32[]{:S(2)}) collective-permute-start(bf16[256,768]{1,0:T(8,128)(2,1)S(1)} %get-tuple-element.119.refs_3_.refs_6_), channel_id=1, source_target_pairs={{0,1},{1,0},{2,3},{3,2},{4,5},{5,4},{6,7},{7,6},{8,9},{9,8},{10,11... | collective-permute-start | bytes 1179656 | tf_op jit(solution)/shard_map/ppermute | solution.py:735
  105.5 13.3 %collective-permute-start.25 = (bf16[2,4,80,384]{3,2,1,0:T(8,128)(2,1)S(1)}, bf16[2,4,80,384]{3,2,1,0:T(8,128)(2,1)S(1)}, u32[]{:S(2)}, u32[]{:S(2)}) collective-permute-start(bf16[2,4,80,384]{3,2,1,0:T(8,128)(2,1)S(1)} %get-tuple-element.147), channel_id=1, source_target_pairs={{0,2},{1,3},{2,0},{3,1},{4,6},{5,7},{6,4},{7,5},{8,10},{9,11},{10,... | collective-permute-start | bytes 1474568 | tf_op jit(solution)/shard_map/ppermute | solution.py:735
  106.2 13.0 %collective-permute-start.26 = (bf16[2,4,80,384]{3,2,1,0:T(8,128)(2,1)S(1)}, bf16[2,4,80,384]{3,2,1,0:T(8,128)(2,1)S(1)}, u32[]{:S(2)}, u32[]{:S(2)}) collective-permute-start(bf16[2,4,80,384]{3,2,1,0:T(8,128)(2,1)S(1)} %get-tuple-element.149), channel_id=1, source_target_pairs={{0,4},{1,5},{2,6},{3,7},{4,0},{5,1},{6,2},{7,3},{8,12},{9,13},{10,... | collective-permute-start | bytes 1474568 | tf_op jit(solution)/shard_map/ppermute | solution.py:735
  119.5 6.9 %collective-permute-start.27 = (bf16[4,80,384]{2,1,0:T(8,128)(2,1)S(1)}, bf16[4,80,384]{2,1,0:T(8,128)(2,1)S(1)}, u32[]{:S(2)}, u32[]{:S(2)}) collective-permute-start(bf16[4,80,384]{2,1,0:T(8,128)(2,1)S(1)} %get-tuple-element.156), channel_id=1, source_target_pairs={{0,4},{1,5},{2,6},{3,7},{4,0},{5,1},{6,2},{7,3},{8,12},{9,13},{10,... | collective-permute-start | bytes 737288 | tf_op jit(solution)/shard_map/ppermute | solution.py:735
  121.1 6.6 %collective-permute-start.28 = (bf16[4,80,384]{2,1,0:T(8,128)(2,1)S(1)}, bf16[4,80,384]{2,1,0:T(8,128)(2,1)S(1)}, u32[]{:S(2)}, u32[]{:S(2)}) collective-permute-start(bf16[4,80,384]{2,1,0:T(8,128)(2,1)S(1)} %get-tuple-element.158), channel_id=1, source_target_pairs={{0,2},{1,3},{2,0},{3,1},{4,6},{5,7},{6,4},{7,5},{8,10},{9,11},{10,... | collective-permute-start | bytes 737288 | tf_op jit(solution)/shard_map/ppermute | solution.py:735
  127.8 11.6 %collective-permute-start.29 = (bf16[80,768]{1,0:T(8,128)(2,1)S(1)}, bf16[80,768]{1,0:T(8,128)(2,1)S(1)}, u32[]{:S(2)}, u32[]{:S(2)}) collective-permute-start(bf16[80,768]{1,0:T(8,128)(2,1)S(1)} %get-tuple-element.171), channel_id=1, source_target_pairs={{0,8},{1,9},{2,10},{3,11},{4,12},{5,13},{6,14},{7,15},{8,0},{9,1},... | collective-permute-start | bytes 368648 | tf_op jit(solution)/shard_map/ppermute | solution.py:735
  129.4 10.2 %collective-permute-start.30 = (bf16[80,768]{1,0:T(8,128)(2,1)S(1)}, bf16[80,768]{1,0:T(8,128)(2,1)S(1)}, u32[]{:S(2)}, u32[]{:S(2)}) collective-permute-start(bf16[80,768]{1,0:T(8,128)(2,1)S(1)} %get-tuple-element.172), channel_id=1, source_target_pairs={{0,16},{1,17},{2,18},{3,19},{4,20},{5,21},{6,22},{7,23},{8,24},{9,... | collective-permute-start | bytes 368648 | tf_op jit(solution)/shard_map/ppermute | solution.py:735
  132.0 7.6 %collective-permute-start.31 = (bf16[80,768]{1,0:T(8,128)(2,1)S(1)}, bf16[80,768]{1,0:T(8,128)(2,1)S(1)}, u32[]{:S(2)}, u32[]{:S(2)}) collective-permute-start(bf16[80,768]{1,0:T(8,128)(2,1)S(1)} %get-tuple-element.173), channel_id=1, source_target_pairs={{0,24},{1,25},{2,26},{3,27},{4,28},{5,29},{6,30},{7,31},{8,16},{9,... | collective-permute-start | bytes 368648 | tf_op jit(solution)/shard_map/ppermute | solution.py:735
  (25 other events, 131.5 us)

commit v5 on v4

--- a/solution.py
+++ b/solution.py
@@ -715,7 +715,7 @@
     parts = small_call(
         sum_second, "sum_second", [sds((block, width), BF16)] * 4, dep, pk, pg, qk, qg
     )
-    got = [hops.flip(part, z * ALONG_Z) for z, part in enumerate(parts) if z]
+    got = [hops.flip(parts[z], z * ALONG_Z) for z in (2, 3, 1)]
     dep = works[3]([parts[0]])
     rows = (block - 8) // 3
     outs = [sds((rows, width), F32)] * 3 + [sds((width,), F32)] * 2 + [sds((n_adapters,), F32)]

time: 141 us -> 140 us (level)
  transfers between devices with their start and end apart: 32 -> 32, of which waited for: 16 -> 15; matrix products, arithmetic and copies ran while one was open for 0% -> 0% of each run, Pallas kernels for 39% -> 39%
where the time goes in v5:
time: 140 us
  Pallas kernels  75.6 us (54%)
  waiting for transfers between devices  31.8 us (23%)
  starting transfers between devices  31.1 us (22%)
    ppermute x32, waiting for transfers between devices, flip(): return lax.ppermute(array, AXES, [(i, i ^ bits) for i in range(self.count)])  31.8 us
    ppermute x32, starting transfers between devices, flip(): return lax.ppermute(array, AXES, [(i, i ^ bits) for i in range(self.count)])  31.1 us
    pallas_call x2, Pallas kernels, call_attend_forward(): kernel(functools.partial(attend_forward, columns, last), deps, ATTEND_MIB...  18.6 us
    pallas_call x4, Pallas kernels, call_attend_backward(): kernel(functools.partial(attend_backward, columns, unroll, leaving), deps...  14.3 us
    pallas_call x1, Pallas kernels, call_merging(): pl.pallas_call(functools.partial(merging, n_adapters), in_specs=[SMEM, SM...  14 us
    pallas_call x3, Pallas kernels, call_ffn_forward(): kernel(functools.partial(ffn_forward, quarters, len(out_quarters) // quar...  8.3 us
    pallas_call x2, Pallas kernels, call_ffn_backward(): kernel(functools.partial(ffn_backward, last, len(out_quarters) // 2, len(...  6.54 us
  transfers between devices with their start and end apart: 32, of which 15 were waited for; matrix products, arithmetic and copies ran while one was open for 0% of the time, Pallas kernels for 39%

profile of v5, /device:TPU:0, one launch (start us, length us, event | category | flops | bytes accessed | tf_op | source)
XLA Modules:
  0.0 140.0 jit_solution(15266471821347774771)
XLA Ops:
  4.5 2.9 %collective-permute-start.2 = (bf16[5,48,384]{2,1,0:T(8,128)(2,1)S(1)}, bf16[5,48,384]{2,1,0:T(8,128)(2,1)S(1)}, u32[]{:S(2)}, u32[]{:S(2)}) collective-permute-start(bf16[5,48,384]{2,1,0:T(8,128)(2,1)S(1)} %get-tuple-element.100.refs_5_), channel_id=1, source_target_pairs={{0,2},{1,3},{2,0},{3,1},{4,6},{5,7},{6,4},{7,5},{8,10},{9,11},{10,... | collective-permute-start | bytes 552968 | tf_op jit(solution)/shard_map/ppermute | solution.py:735
  7.4 2.0 %prepare_shares.1 = (bf16[576,768]{1,0:T(8,128)(2,1)S(1)}, bf16[576,768]{1,0:T(8,128)(2,1)S(1)}, bf16[512,768]{1,0:T(8,128)(2,1)S(1)}, bf16[768,768]{1,0:T(8,128)(2,1)S(1)}, bf16[768,768]{1,0:T(8,128)(2,1)S(1)}) custom-call(s32[6]{0:T(128)S(1)} %stack.27.meta.refs_0_.refs_1_.refs_3_.refs_2_, bf16[768,768]{1,0:T(8,128)(2,1)S(1)} %get-tuple-element.96.refs_1_.refs_6_.refs_5_, ...), custom_call_target="tpu_custom_call" | custom-call | bytes 1024 | tf_op jit(solution)/shard_map/prepare_shares/pallas_call | solution.py:610
  9.4 2.9 %collective-permute-done.2.refs_6_ = bf16[5,48,384]{2,1,0:T(8,128)(2,1)S(1)} collective-permute-done((bf16[5,48,384]{2,1,0:T(8,128)(2,1)S(1)}, bf16[5,48,384]{2,1,0:T(8,128)(2,1)S(1)}, u32[]{:S(2)}, u32[]{:S(2)}) %collective-permute-start.2) | collective-permute-done | bytes 184352 | tf_op jit(solution)/shard_map/ppermute | solution.py:735
  13.5 1.7 %collective-permute-start.7 = (bf16[576,768]{1,0:T(8,128)(2,1)S(1)}, bf16[576,768]{1,0:T(8,128)(2,1)S(1)}, u32[]{:S(2)}, u32[]{:S(2)}) collective-permute-start(bf16[576,768]{1,0:T(8,128)(2,1)S(1)} %get-tuple-element.107), channel_id=1, source_target_pairs={{0,2},{1,3},{2,0},{3,1},{4,6},{5,7},{6,4},{7,5},{8,10},{9,11},{10,... | collective-permute-start | bytes 2654216 | tf_op jit(solution)/shard_map/ppermute | solution.py:735
  15.2 2.6 %collective-permute-start.6 = (bf16[10,48,384]{2,1,0:T(8,128)(2,1)S(1)}, bf16[10,48,384]{2,1,0:T(8,128)(2,1)S(1)}, u32[]{:S(2)}, u32[]{:S(2)}) collective-permute-start(bf16[10,48,384]{2,1,0:T(8,128)(2,1)S(1)} %get-tuple-element.101.refs_0_.refs_7_), channel_id=1, source_target_pairs={{0,16},{1,17},{2,18},{3,19},{4,20},{5,21},{6,22},{7,23},{8,24},{9,... | collective-permute-start | bytes 1105928 | tf_op jit(solution)/shard_map/ppermute | solution.py:735
  19.3 8.9 %attend_forward.2 = (bf16[576,512]{1,0:T(8,128)(2,1)}, bf16[192,512]{1,0:T(8,128)(2,1)}, bf16[3,512,512]{2,1,0:T(8,128)(2,1)}, bf16[576,512]{1,0:T(8,128)(2,1)},...) custom-call(bf16[10,48,384]{2,1,0:T(8,128)(2,1)S(1)} %get-tuple-element.101.refs_0_.refs_7_, ...), custom_call_target="tpu_custom_call" | custom-call | bytes 1024 | tf_op jit(solution)/shard_map/attend_forward/pallas_call | solution.py:193
  28.2 6.1 %collective-permute-done.6.refs_8_ = bf16[10,48,384]{2,1,0:T(8,128)(2,1)S(1)} collective-permute-done((bf16[10,48,384]{2,1,0:T(8,128)(2,1)S(1)}, bf16[10,48,384]{2,1,0:T(8,128)(2,1)S(1)}, u32[]{:S(2)}, u32[]{:S(2)}) %collective-permute-start.6) | collective-permute-done | bytes 368672 | tf_op jit(solution)/shard_map/ppermute | solution.py:735
  35.7 1.8 %collective-permute-start.13 = (bf16[576,768]{1,0:T(8,128)(2,1)S(1)}, bf16[576,768]{1,0:T(8,128)(2,1)S(1)}, u32[]{:S(2)}, u32[]{:S(2)}) collective-permute-start(bf16[576,768]{1,0:T(8,128)(2,1)S(1)} %get-tuple-element.113), channel_id=1, source_target_pairs={{0,2},{1,3},{2,0},{3,1},{4,6},{5,7},{6,4},{7,5},{8,10},{9,11},{10,... | collective-permute-start | bytes 2654216 | tf_op jit(solution)/shard_map/ppermute | solution.py:735
  41.2 7.9 %collective-permute-done.11.refs_5_ = bf16[10,48,384]{2,1,0:T(8,128)(2,1)S(1)} collective-permute-done((bf16[10,48,384]{2,1,0:T(8,128)(2,1)S(1)}, bf16[10,48,384]{2,1,0:T(8,128)(2,1)S(1)}, u32[]{:S(2)}, u32[]{:S(2)}) %collective-permute-start.11) | collective-permute-done | bytes 368672 | tf_op jit(solution)/shard_map/ppermute | solution.py:735
  50.8 4.7 %collective-permute-done.12.refs_9_.refs_10_ = bf16[256,768]{1,0:T(8,128)(2,1)S(1)} collective-permute-done((bf16[256,768]{1,0:T(8,128)(2,1)S(1)}, bf16[256,768]{1,0:T(8,128)(2,1)S(1)}, u32[]{:S(2)}, u32[]{:S(2)}) %collective-permute-start.12) | collective-permute-done | bytes 393248 | tf_op jit(solution)/shard_map/ppermute | solution.py:735
  62.7 9.7 %attend_forward.3 = (bf16[576,512]{1,0:T(8,128)(2,1)}, bf16[192,512]{1,0:T(8,128)(2,1)}, bf16[3,512,512]{2,1,0:T(8,128)(2,1)}, bf16[576,512]{1,0:T(8,128)(2,1)},...) custom-call(s32[6]{0:T(128)S(1)} %stack.27.meta.refs_0_.refs_1_.refs, ...), custom_call_target="tpu_custom_call" | custom-call | bytes 1024 | tf_op jit(solution)/shard_map/attend_forward/pallas_call | solution.py:193
  72.5 3.5 %ffn_forward.3 = (bf16[2,512,768]{2,1,0:T(8,128)(2,1)S(1)}, f32[512,768]{1,0:T(8,128)S(1)}) custom-call(f32[512,768]{1,0:T(8,128)S(1)} %get-tuple-element.115.refs_0_.refs_1_, f32[512,768]{1,0:T(8,128)S(1)} %get-tuple-element.115.refs_0_.refs_1_, bf16[768,768]{1,0:T(8,128)(2,1)S(1)} %copy-done, ...), custom_call_target="tpu_custom_call" | custom-call | bytes 1024 | tf_op jit(solution)/shard_map/ffn_forward/pallas_call | solution.py:231
  79.8 2.4 %ffn_forward.4 = (bf16[1,512,768]{2,1,0:T(8,128)(2,1)S(1)}, f32[512,768]{1,0:T(8,128)S(1)}) custom-call(f32[512,768]{1,0:T(8,128)S(1)} %get-tuple-element.115.refs_0_.refs_1_, f32[512,768]{1,0:T(8,128)S(1)} %get-tuple-element.116.refs_0_.refs_1_, bf16[768,768]{1,0:T(8,128)(2,1)S(1)} %get-tuple-element.122.refs_2_.refs_4_, ...), custom_call_target="tpu_custom_call" | custom-call | bytes 1024 | tf_op jit(solution)/shard_map/ffn_forward/pallas_call | solution.py:231
  83.2 2.4 %ffn_forward.5 = (bf16[1,512,768]{2,1,0:T(8,128)(2,1)S(1)}, f32[512,768]{1,0:T(8,128)S(1)}) custom-call(f32[512,768]{1,0:T(8,128)S(1)} %get-tuple-element.115.refs_0_.refs_1_, f32[512,768]{1,0:T(8,128)S(1)} %get-tuple-element.124.refs_1_, bf16[768,768]{1,0:T(8,128)(2,1)S(1)} %collective-permute-done.21.refs_2_.refs_5_, ...), custom_call_target="tpu_custom_call" | custom-call | bytes 1024 | tf_op jit(solution)/shard_map/ffn_forward/pallas_call | solution.py:231
  86.8 14.0 %merging.1 = (f32[512,768]{1,0:T(8,128)}, f32[512,768]{1,0:T(8,128)S(1)}, bf16[512,768]{1,0:T(8,128)(2,1)S(1)}, bf16[512,768]{1,0:T(8,128)(2,1)S(1)}, bf16[2,2,4...) custom-call(s32[6]{0:T(128)S(1)} %stack.27.meta.refs_0_.refs_1_.refs_3_.refs_2_, ...), custom_call_target="tpu_custom_call" | custom-call | bytes 1024 | tf_op jit(solution)/shard_map/merging/pallas_call | solution.py:399
  101.0 2.0 %merging_input.1 = (f32[512,768]{1,0:T(8,128)S(1)}, bf16[512,768]{1,0:T(8,128)(2,1)S(1)}) custom-call(f32[512,768]{1,0:T(8,128)S(1)} %get-tuple-element.125.refs_0_.sums, f32[8,768]{1,0:T(8,128)S(1)} %get-tuple-element.102.refs_5_.refs_4_.lines.refs_1_.refs_12_, f32[512,768]{1,0:T(8,128)S(1)} %get-tuple-element.128.refs_2_, ...), custom_call_target="tpu_custom_call" | custom-call | bytes 1024 | tf_op jit(solution)/shard_map/merging_input/pallas_call | solution.py:428
  103.0 1.8 %collective-permute-done.24.refs_2_ = bf16[2,2,4,80,768]{4,3,2,1,0:T(8,128)(2,1)S(1)} collective-permute-done((bf16[2,2,4,80,768]{4,3,2,1,0:T(8,128)(2,1)S(1)}, bf16[2,2,4,80,768]{4,3,2,1,0:T(8,128)(2,1)S(1)}, u32[]{:S(2)}, u32[]{:S(2)}) %collective-permute-start.24) | collective-permute-done | bytes 1966112 | tf_op jit(solution)/shard_map/ppermute | solution.py:735
  107.7 3.1 %ffn_backward.2.refs_1_ = f32[512,768]{1,0:T(8,128)S(1)} custom-call(bf16[2,4,80,384]{3,2,1,0:T(8,128)(2,1)S(1)} %get-tuple-element.135.refs_0_.refs_1_, bf16[512,768]{1,0:T(8,128)(2,1)S(1)} %get-tuple-element.131.refs_1_.refs_0_, f32[512,768]{1,0:T(8,128)S(1)} %get-tuple-element.132.refs_0_.refs_2_, bf16[2,512,768]{2,1,0:T(8,128)(2,1)S(1)} %get-tuple-element.136.refs_3_, ...), custom_call_target="tpu_custom_call" | custom-call | bytes 1024 | tf_op jit(solution)/shard_map/ffn_backward/pallas_call | solution.py:468
  110.9 3.4 %ffn_backward.3 = (f32[512,768]{1,0:T(8,128)S(1)}, bf16[512,768]{1,0:T(8,128)(2,1)S(1)}) custom-call(bf16[512,768]{1,0:T(8,128)(2,1)S(1)} %get-tuple-element.131.refs_1_.refs_0_, f32[512,768]{1,0:T(8,128)S(1)} %ffn_backward.2.refs_1_, bf16[1,512,768]{2,1,0:T(8,128)(2,1)S(1)} %get-tuple-element.137.refs_2_, ...), custom_call_target="tpu_custom_call" | custom-call | bytes 1024 | tf_op jit(solution)/shard_map/ffn_backward/pallas_call | solution.py:468
  114.3 3.6 %attend_backward.4 = (f32[512,768]{1,0:T(8,128)S(1)}, f32[8,128]{1,0:T(8,128)S(1)}) custom-call(bf16[512,768]{1,0:T(8,128)(2,1)S(1)} %get-tuple-element.141.refs_0_.refs_1_, f32[512,768]{1,0:T(8,128)S(1)} %get-tuple-element.142.refs_1_, bf16[576,512]{1,0:T(8,128)(2,1)S(1)} %copy-done.9, bf16[192,512]{1,0:T(8,128)(2,1)S(1)} %copy-done.13, ...), custom_call_target="tpu_custom_call" | custom-call | bytes 1024 | tf_op jit(solution)/shard_map/attend_backward/pallas_call | solution.py:521
  122.5 3.6 %attend_backward.5 = (f32[512,768]{1,0:T(8,128)S(1)}, f32[8,128]{1,0:T(8,128)S(1)}) custom-call(bf16[4,80,384]{2,1,0:T(8,128)(2,1)S(1)} %get-tuple-element.150.refs_0_.refs_1_, bf16[512,768]{1,0:T(8,128)(2,1)S(1)} %get-tuple-element.141.refs_0_.refs_1_, f32[512,768]{1,0:T(8,128)S(1)} %get-tuple-element.151.refs_2_, bf16[576,512]{1,0:T(8,128)(2,1)S(1)} %copy-done.8, ...), custom_call_target="tpu_custom_call" | custom-call | bytes 1024 | tf_op jit(solution)/shard_map/attend_backward/pallas_call | solution.py:521
  127.8 2.7 %collective-permute-start.29 = (bf16[80,768]{1,0:T(8,128)(2,1)S(1)}, bf16[80,768]{1,0:T(8,128)(2,1)S(1)}, u32[]{:S(2)}, u32[]{:S(2)}) collective-permute-start(bf16[80,768]{1,0:T(8,128)(2,1)S(1)} %get-tuple-element.171), channel_id=1, source_target_pairs={{0,16},{1,17},{2,18},{3,19},{4,20},{5,21},{6,22},{7,23},{8,24},{9,... | collective-permute-start | bytes 368648 | tf_op jit(solution)/shard_map/ppermute | solution.py:735
  132.1 3.1 %attend_backward.6 = (f32[512,768]{1,0:T(8,128)S(1)}, f32[8,128]{1,0:T(8,128)S(1)}) custom-call(bf16[80,768]{1,0:T(8,128)(2,1)S(1)} %get-tuple-element.159.refs_0_.refs_1_, bf16[512,768]{1,0:T(8,128)(2,1)S(1)} %get-tuple-element.141.refs_0_.refs_1_, f32[512,768]{1,0:T(8,128)S(1)} %get-tuple-element.160.refs_2_, bf16[576,512]{1,0:T(8,128)(2,1)S(1)} %copy-done.11, ...), custom_call_target="tpu_custom_call" | custom-call | bytes 1024 | tf_op jit(solution)/shard_map/attend_backward/pallas_call | solution.py:521
  135.2 4.0 %attend_backward.7 = (f32[512,768]{1,0:T(8,128)}, f32[8,128]{1,0:T(8,128)S(1)}) custom-call(f32[8,128]{1,0:T(8,128)S(1)} %get-tuple-element.164.refs_0_, bf16[512,768]{1,0:T(8,128)(2,1)S(1)} %get-tuple-element.141.refs_0_.refs_1_, f32[512,768]{1,0:T(8,128)S(1)} %get-tuple-element.165.refs_2_, bf16[576,512]{1,0:T(8,128)(2,1)S(1)} %copy-done.10, ...), custom_call_target="tpu_custom_call" | custom-call | bytes 1024 | tf_op jit(solution)/shard_map/attend_backward/pallas_call | solution.py:521
  (103 shorter events, 37.9 us)
Async XLA Ops:
  4.4 7.9 %collective-permute-start.1 = (bf16[768,768]{1,0:T(8,128)(2,1)S(1)}, bf16[768,768]{1,0:T(8,128)(2,1)S(1)}, u32[]{:S(2)}, u32[]{:S(2)}) collective-permute-start(bf16[768,768]{1,0:T(8,128)(2,1)S(1)} %get-tuple-element.96.refs_1_.refs_6_.refs_5_), channel_id=1, source_target_pairs={{0,1},{1,0},{2,3},{3,2},{4,5},{5,4},{6,7},{7,6},{8,9},{9,8},{10,11... | collective-permute-start | bytes 3538952 | tf_op jit(solution)/shard_map/ppermute | solution.py:735
  4.5 7.8 %collective-permute-start.2 = (bf16[5,48,384]{2,1,0:T(8,128)(2,1)S(1)}, bf16[5,48,384]{2,1,0:T(8,128)(2,1)S(1)}, u32[]{:S(2)}, u32[]{:S(2)}) collective-permute-start(bf16[5,48,384]{2,1,0:T(8,128)(2,1)S(1)} %get-tuple-element.100.refs_5_), channel_id=1, source_target_pairs={{0,2},{1,3},{2,0},{3,1},{4,6},{5,7},{6,4},{7,5},{8,10},{9,11},{10,... | collective-permute-start | bytes 552968 | tf_op jit(solution)/shard_map/ppermute | solution.py:735
  12.9 22.2 %collective-permute-start.3 = (bf16[768,768]{1,0:T(8,128)(2,1)S(1)}, bf16[768,768]{1,0:T(8,128)(2,1)S(1)}, u32[]{:S(2)}, u32[]{:S(2)}) collective-permute-start(bf16[768,768]{1,0:T(8,128)(2,1)S(1)} %get-tuple-element.104), channel_id=1, source_target_pairs={{0,1},{1,0},{2,3},{3,2},{4,5},{5,4},{6,7},{7,6},{8,9},{9,8},{10,11... | collective-permute-start | bytes 3538952 | tf_op jit(solution)/shard_map/ppermute | solution.py:735
  13.0 22.1 %collective-permute-start.4 = (bf16[768,768]{1,0:T(8,128)(2,1)S(1)}, bf16[768,768]{1,0:T(8,128)(2,1)S(1)}, u32[]{:S(2)}, u32[]{:S(2)}) collective-permute-start(bf16[768,768]{1,0:T(8,128)(2,1)S(1)} %get-tuple-element.105), channel_id=1, source_target_pairs={{0,1},{1,0},{2,3},{3,2},{4,5},{5,4},{6,7},{7,6},{8,9},{9,8},{10,11... | collective-permute-start | bytes 3538952 | tf_op jit(solution)/shard_map/ppermute | solution.py:735
  13.5 21.6 %collective-permute-start.7 = (bf16[576,768]{1,0:T(8,128)(2,1)S(1)}, bf16[576,768]{1,0:T(8,128)(2,1)S(1)}, u32[]{:S(2)}, u32[]{:S(2)}) collective-permute-start(bf16[576,768]{1,0:T(8,128)(2,1)S(1)} %get-tuple-element.107), channel_id=1, source_target_pairs={{0,2},{1,3},{2,0},{3,1},{4,6},{5,7},{6,4},{7,5},{8,10},{9,11},{10,... | collective-permute-start | bytes 2654216 | tf_op jit(solution)/shard_map/ppermute | solution.py:735
  15.2 19.1 %collective-permute-start.6 = (bf16[10,48,384]{2,1,0:T(8,128)(2,1)S(1)}, bf16[10,48,384]{2,1,0:T(8,128)(2,1)S(1)}, u32[]{:S(2)}, u32[]{:S(2)}) collective-permute-start(bf16[10,48,384]{2,1,0:T(8,128)(2,1)S(1)} %get-tuple-element.101.refs_0_.refs_7_), channel_id=1, source_target_pairs={{0,16},{1,17},{2,18},{3,19},{4,20},{5,21},{6,22},{7,23},{8,24},{9,... | collective-permute-start | bytes 1105928 | tf_op jit(solution)/shard_map/ppermute | solution.py:735
  17.8 16.5 %collective-permute-start.5 = (bf16[10,48,384]{2,1,0:T(8,128)(2,1)S(1)}, bf16[10,48,384]{2,1,0:T(8,128)(2,1)S(1)}, u32[]{:S(2)}, u32[]{:S(2)}) collective-permute-start(bf16[10,48,384]{2,1,0:T(8,128)(2,1)S(1)} %get-tuple-element.101.refs_0_.refs_7_), channel_id=1, source_target_pairs={{0,4},{1,5},{2,6},{3,7},{4,0},{5,1},{6,2},{7,3},{8,12},{9,13},{10,... | collective-permute-start | bytes 1105928 | tf_op jit(solution)/shard_map/ppermute | solution.py:735
  35.7 20.9 %collective-permute-start.13 = (bf16[576,768]{1,0:T(8,128)(2,1)S(1)}, bf16[576,768]{1,0:T(8,128)(2,1)S(1)}, u32[]{:S(2)}, u32[]{:S(2)}) collective-permute-start(bf16[576,768]{1,0:T(8,128)(2,1)S(1)} %get-tuple-element.113), channel_id=1, source_target_pairs={{0,2},{1,3},{2,0},{3,1},{4,6},{5,7},{6,4},{7,5},{8,10},{9,11},{10,... | collective-permute-start | bytes 2654216 | tf_op jit(solution)/shard_map/ppermute | solution.py:735
  37.6 11.5 %collective-permute-start.11 = (bf16[10,48,384]{2,1,0:T(8,128)(2,1)S(1)}, bf16[10,48,384]{2,1,0:T(8,128)(2,1)S(1)}, u32[]{:S(2)}, u32[]{:S(2)}) collective-permute-start(bf16[10,48,384]{2,1,0:T(8,128)(2,1)S(1)} %get-tuple-element.111), channel_id=1, source_target_pairs={{0,4},{1,5},{2,6},{3,7},{4,0},{5,1},{6,2},{7,3},{8,12},{9,13},{10,... | collective-permute-start | bytes 1105928 | tf_op jit(solution)/shard_map/ppermute | solution.py:735
  39.1 17.1 %collective-permute-start.10 = (bf16[20,48,384]{2,1,0:T(8,128)(2,1)S(1)}, bf16[20,48,384]{2,1,0:T(8,128)(2,1)S(1)}, u32[]{:S(2)}, u32[]{:S(2)}) collective-permute-start(bf16[20,48,384]{2,1,0:T(8,128)(2,1)S(1)} %get-tuple-element.108.refs_2_), channel_id=1, source_target_pairs={{0,8},{1,9},{2,10},{3,11},{4,12},{5,13},{6,14},{7,15},{8,0},{9,1},... | collective-permute-start | bytes 2211848 | tf_op jit(solution)/shard_map/ppermute | solution.py:735
  40.6 15.5 %collective-permute-start.8 = (bf16[20,48,384]{2,1,0:T(8,128)(2,1)S(1)}, bf16[20,48,384]{2,1,0:T(8,128)(2,1)S(1)}, u32[]{:S(2)}, u32[]{:S(2)}) collective-permute-start(bf16[20,48,384]{2,1,0:T(8,128)(2,1)S(1)} %get-tuple-element.108.refs_2_), channel_id=1, source_target_pairs={{0,1},{1,0},{2,3},{3,2},{4,5},{5,4},{6,7},{7,6},{8,9},{9,8},{10,11... | collective-permute-start | bytes 2211848 | tf_op jit(solution)/shard_map/ppermute | solution.py:735
  40.7 14.8 %collective-permute-start.12 = (bf16[256,768]{1,0:T(8,128)(2,1)S(1)}, bf16[256,768]{1,0:T(8,128)(2,1)S(1)}, u32[]{:S(2)}, u32[]{:S(2)}) collective-permute-start(bf16[256,768]{1,0:T(8,128)(2,1)S(1)} %get-tuple-element.112), channel_id=1, source_target_pairs={{0,4},{1,5},{2,6},{3,7},{4,0},{5,1},{6,2},{7,3},{8,12},{9,13},{10,... | collective-permute-start | bytes 1179656 | tf_op jit(solution)/shard_map/ppermute | solution.py:735
  57.9 20.6 %collective-permute-start.18 = (bf16[512,768]{1,0:T(8,128)(2,1)S(1)}, bf16[512,768]{1,0:T(8,128)(2,1)S(1)}, u32[]{:S(2)}, u32[]{:S(2)}) collective-permute-start(bf16[512,768]{1,0:T(8,128)(2,1)S(1)} %get-tuple-element.120), channel_id=1, source_target_pairs={{0,2},{1,3},{2,0},{3,1},{4,6},{5,7},{6,4},{7,5},{8,10},{9,11},{10,... | collective-permute-start | bytes 2359304 | tf_op jit(solution)/shard_map/ppermute | solution.py:735
  59.6 16.4 %collective-permute-start.15 = (bf16[20,48,384]{2,1,0:T(8,128)(2,1)S(1)}, bf16[20,48,384]{2,1,0:T(8,128)(2,1)S(1)}, u32[]{:S(2)}, u32[]{:S(2)}) collective-permute-start(bf16[20,48,384]{2,1,0:T(8,128)(2,1)S(1)} %get-tuple-element.117.refs_4_), channel_id=1, source_target_pairs={{0,1},{1,0},{2,3},{3,2},{4,5},{5,4},{6,7},{7,6},{8,9},{9,8},{10,11... | collective-permute-start | bytes 2211848 | tf_op jit(solution)/shard_map/ppermute | solution.py:735
  59.6 18.9 %collective-permute-start.19 = (bf16[20,48,384]{2,1,0:T(8,128)(2,1)S(1)}, bf16[20,48,384]{2,1,0:T(8,128)(2,1)S(1)}, u32[]{:S(2)}, u32[]{:S(2)}) collective-permute-start(bf16[20,48,384]{2,1,0:T(8,128)(2,1)S(1)} %get-tuple-element.117.refs_4_), channel_id=1, source_target_pairs={{0,4},{1,5},{2,6},{3,7},{4,0},{5,1},{6,2},{7,3},{8,12},{9,13},{10,... | collective-permute-start | bytes 2211848 | tf_op jit(solution)/shard_map/ppermute | solution.py:735
  61.1 16.2 %collective-permute-start.20 = (bf16[384,768]{1,0:T(8,128)(2,1)S(1)}, bf16[384,768]{1,0:T(8,128)(2,1)S(1)}, u32[]{:S(2)}, u32[]{:S(2)}) collective-permute-start(bf16[384,768]{1,0:T(8,128)(2,1)S(1)} %get-tuple-element.121.refs_6_), channel_id=1, source_target_pairs={{0,8},{1,9},{2,10},{3,11},{4,12},{5,13},{6,14},{7,15},{8,0},{9,1},... | collective-permute-start | bytes 1769480 | tf_op jit(solution)/shard_map/ppermute | solution.py:735
  62.7 14.6 %collective-permute-start.17 = (bf16[256,768]{1,0:T(8,128)(2,1)S(1)}, bf16[256,768]{1,0:T(8,128)(2,1)S(1)}, u32[]{:S(2)}, u32[]{:S(2)}) collective-permute-start(bf16[256,768]{1,0:T(8,128)(2,1)S(1)} %get-tuple-element.119.refs_3_.refs_6_), channel_id=1, source_target_pairs={{0,1},{1,0},{2,3},{3,2},{4,5},{5,4},{6,7},{7,6},{8,9},{9,8},{10,11... | collective-permute-start | bytes 1179656 | tf_op jit(solution)/shard_map/ppermute | solution.py:735
  105.5 13.3 %collective-permute-start.25 = (bf16[2,4,80,384]{3,2,1,0:T(8,128)(2,1)S(1)}, bf16[2,4,80,384]{3,2,1,0:T(8,128)(2,1)S(1)}, u32[]{:S(2)}, u32[]{:S(2)}) collective-permute-start(bf16[2,4,80,384]{3,2,1,0:T(8,128)(2,1)S(1)} %get-tuple-element.147), channel_id=1, source_target_pairs={{0,2},{1,3},{2,0},{3,1},{4,6},{5,7},{6,4},{7,5},{8,10},{9,11},{10,... | collective-permute-start | bytes 1474568 | tf_op jit(solution)/shard_map/ppermute | solution.py:735
  106.2 13.0 %collective-permute-start.26 = (bf16[2,4,80,384]{3,2,1,0:T(8,128)(2,1)S(1)}, bf16[2,4,80,384]{3,2,1,0:T(8,128)(2,1)S(1)}, u32[]{:S(2)}, u32[]{:S(2)}) collective-permute-start(bf16[2,4,80,384]{3,2,1,0:T(8,128)(2,1)S(1)} %get-tuple-element.149), channel_id=1, source_target_pairs={{0,4},{1,5},{2,6},{3,7},{4,0},{5,1},{6,2},{7,3},{8,12},{9,13},{10,... | collective-permute-start | bytes 1474568 | tf_op jit(solution)/shard_map/ppermute | solution.py:735
  119.5 6.9 %collective-permute-start.27 = (bf16[4,80,384]{2,1,0:T(8,128)(2,1)S(1)}, bf16[4,80,384]{2,1,0:T(8,128)(2,1)S(1)}, u32[]{:S(2)}, u32[]{:S(2)}) collective-permute-start(bf16[4,80,384]{2,1,0:T(8,128)(2,1)S(1)} %get-tuple-element.156), channel_id=1, source_target_pairs={{0,4},{1,5},{2,6},{3,7},{4,0},{5,1},{6,2},{7,3},{8,12},{9,13},{10,... | collective-permute-start | bytes 737288 | tf_op jit(solution)/shard_map/ppermute | solution.py:735
  121.1 6.6 %collective-permute-start.28 = (bf16[4,80,384]{2,1,0:T(8,128)(2,1)S(1)}, bf16[4,80,384]{2,1,0:T(8,128)(2,1)S(1)}, u32[]{:S(2)}, u32[]{:S(2)}) collective-permute-start(bf16[4,80,384]{2,1,0:T(8,128)(2,1)S(1)} %get-tuple-element.158), channel_id=1, source_target_pairs={{0,2},{1,3},{2,0},{3,1},{4,6},{5,7},{6,4},{7,5},{8,10},{9,11},{10,... | collective-permute-start | bytes 737288 | tf_op jit(solution)/shard_map/ppermute | solution.py:735
  127.8 11.4 %collective-permute-start.29 = (bf16[80,768]{1,0:T(8,128)(2,1)S(1)}, bf16[80,768]{1,0:T(8,128)(2,1)S(1)}, u32[]{:S(2)}, u32[]{:S(2)}) collective-permute-start(bf16[80,768]{1,0:T(8,128)(2,1)S(1)} %get-tuple-element.171), channel_id=1, source_target_pairs={{0,16},{1,17},{2,18},{3,19},{4,20},{5,21},{6,22},{7,23},{8,24},{9,... | collective-permute-start | bytes 368648 | tf_op jit(solution)/shard_map/ppermute | solution.py:735
  130.5 8.7 %collective-permute-start.30 = (bf16[80,768]{1,0:T(8,128)(2,1)S(1)}, bf16[80,768]{1,0:T(8,128)(2,1)S(1)}, u32[]{:S(2)}, u32[]{:S(2)}) collective-permute-start(bf16[80,768]{1,0:T(8,128)(2,1)S(1)} %get-tuple-element.172), channel_id=1, source_target_pairs={{0,24},{1,25},{2,26},{3,27},{4,28},{5,29},{6,30},{7,31},{8,16},{9,... | collective-permute-start | bytes 368648 | tf_op jit(solution)/shard_map/ppermute | solution.py:735
  131.8 7.4 %collective-permute-start.31 = (bf16[80,768]{1,0:T(8,128)(2,1)S(1)}, bf16[80,768]{1,0:T(8,128)(2,1)S(1)}, u32[]{:S(2)}, u32[]{:S(2)}) collective-permute-start(bf16[80,768]{1,0:T(8,128)(2,1)S(1)} %get-tuple-element.173), channel_id=1, source_target_pairs={{0,8},{1,9},{2,10},{3,11},{4,12},{5,13},{6,14},{7,15},{8,0},{9,1},... | collective-permute-start | bytes 368648 | tf_op jit(solution)/shard_map/ppermute | solution.py:735
  (25 other events, 130.9 us)

commit v6 on v5

--- a/solution.py
+++ b/solution.py
@@ -9,7 +9,7 @@
 
 HEAD_DIM = 64
 AXES = ("dp", "tensor")
-ATTEND_MIB, FFN_MIB, MERGE_MIB = 16, 16, 24
+ATTEND_MIB, FFN_MIB, MERGE_MIB = 13, 13, 24
 LANES = 128
 COST = 0.0
 CHUNK = 256

time: 140 us -> 140 us (level)
  no operation moved by 1% of the time
where the time goes in v6:
time: 140 us
  Pallas kernels  75.8 us (54%)
  waiting for transfers between devices  31.6 us (23%)
  starting transfers between devices  31.1 us (22%)
    ppermute x32, waiting for transfers between devices, flip(): return lax.ppermute(array, AXES, [(i, i ^ bits) for i in range(self.count)])  31.6 us
    ppermute x32, starting transfers between devices, flip(): return lax.ppermute(array, AXES, [(i, i ^ bits) for i in range(self.count)])  31.1 us
    pallas_call x2, Pallas kernels, call_attend_forward(): kernel(functools.partial(attend_forward, columns, last), deps, ATTEND_MIB...  18.7 us
    pallas_call x4, Pallas kernels, call_attend_backward(): kernel(functools.partial(attend_backward, columns, unroll, leaving), deps...  14.4 us
    pallas_call x1, Pallas kernels, call_merging(): pl.pallas_call(functools.partial(merging, n_adapters), in_specs=[SMEM, SM...  14 us
    pallas_call x3, Pallas kernels, call_ffn_forward(): kernel(functools.partial(ffn_forward, quarters, len(out_quarters) // quar...  8.25 us
    pallas_call x2, Pallas kernels, call_ffn_backward(): kernel(functools.partial(ffn_backward, last, len(out_quarters) // 2, len(...  6.6 us
  transfers between devices with their start and end apart: 32, of which 15 were waited for; matrix products, arithmetic and copies ran while one was open for 0% of the time, Pallas kernels for 39%

profile of v6, /device:TPU:0, one launch (start us, length us, event | category | flops | bytes accessed | tf_op | source)
XLA Modules:
  0.0 140.0 jit_solution(14525511116985257893)
XLA Ops:
  4.5 2.9 %collective-permute-start.2 = (bf16[5,48,384]{2,1,0:T(8,128)(2,1)S(1)}, bf16[5,48,384]{2,1,0:T(8,128)(2,1)S(1)}, u32[]{:S(2)}, u32[]{:S(2)}) collective-permute-start(bf16[5,48,384]{2,1,0:T(8,128)(2,1)S(1)} %get-tuple-element.100.refs_5_), channel_id=1, source_target_pairs={{0,2},{1,3},{2,0},{3,1},{4,6},{5,7},{6,4},{7,5},{8,10},{9,11},{10,... | collective-permute-start | bytes 552968 | tf_op jit(solution)/shard_map/ppermute | solution.py:735
  7.4 2.0 %prepare_shares.1 = (bf16[576,768]{1,0:T(8,128)(2,1)S(1)}, bf16[576,768]{1,0:T(8,128)(2,1)S(1)}, bf16[512,768]{1,0:T(8,128)(2,1)S(1)}, bf16[768,768]{1,0:T(8,128)(2,1)S(1)}, bf16[768,768]{1,0:T(8,128)(2,1)S(1)}) custom-call(s32[6]{0:T(128)S(1)} %stack.27.meta.refs_0_.refs_1_.refs_3_.refs_2_, bf16[768,768]{1,0:T(8,128)(2,1)S(1)} %get-tuple-element.96.refs_1_.refs_6_.refs_5_, ...), custom_call_target="tpu_custom_call" | custom-call | bytes 1024 | tf_op jit(solution)/shard_map/prepare_shares/pallas_call | solution.py:610
  9.4 2.9 %collective-permute-done.2.refs_6_ = bf16[5,48,384]{2,1,0:T(8,128)(2,1)S(1)} collective-permute-done((bf16[5,48,384]{2,1,0:T(8,128)(2,1)S(1)}, bf16[5,48,384]{2,1,0:T(8,128)(2,1)S(1)}, u32[]{:S(2)}, u32[]{:S(2)}) %collective-permute-start.2) | collective-permute-done | bytes 184352 | tf_op jit(solution)/shard_map/ppermute | solution.py:735
  13.5 1.7 %collective-permute-start.7 = (bf16[576,768]{1,0:T(8,128)(2,1)S(1)}, bf16[576,768]{1,0:T(8,128)(2,1)S(1)}, u32[]{:S(2)}, u32[]{:S(2)}) collective-permute-start(bf16[576,768]{1,0:T(8,128)(2,1)S(1)} %get-tuple-element.107), channel_id=1, source_target_pairs={{0,2},{1,3},{2,0},{3,1},{4,6},{5,7},{6,4},{7,5},{8,10},{9,11},{10,... | collective-permute-start | bytes 2654216 | tf_op jit(solution)/shard_map/ppermute | solution.py:735
  15.2 2.6 %collective-permute-start.6 = (bf16[10,48,384]{2,1,0:T(8,128)(2,1)S(1)}, bf16[10,48,384]{2,1,0:T(8,128)(2,1)S(1)}, u32[]{:S(2)}, u32[]{:S(2)}) collective-permute-start(bf16[10,48,384]{2,1,0:T(8,128)(2,1)S(1)} %get-tuple-element.101.refs_0_.refs_7_), channel_id=1, source_target_pairs={{0,16},{1,17},{2,18},{3,19},{4,20},{5,21},{6,22},{7,23},{8,24},{9,... | collective-permute-start | bytes 1105928 | tf_op jit(solution)/shard_map/ppermute | solution.py:735
  19.3 8.9 %attend_forward.2 = (bf16[576,512]{1,0:T(8,128)(2,1)}, bf16[192,512]{1,0:T(8,128)(2,1)}, bf16[3,512,512]{2,1,0:T(8,128)(2,1)}, bf16[576,512]{1,0:T(8,128)(2,1)},...) custom-call(bf16[10,48,384]{2,1,0:T(8,128)(2,1)S(1)} %get-tuple-element.101.refs_0_.refs_7_, ...), custom_call_target="tpu_custom_call" | custom-call | bytes 1024 | tf_op jit(solution)/shard_map/attend_forward/pallas_call | solution.py:193
  28.2 6.1 %collective-permute-done.6.refs_8_ = bf16[10,48,384]{2,1,0:T(8,128)(2,1)S(1)} collective-permute-done((bf16[10,48,384]{2,1,0:T(8,128)(2,1)S(1)}, bf16[10,48,384]{2,1,0:T(8,128)(2,1)S(1)}, u32[]{:S(2)}, u32[]{:S(2)}) %collective-permute-start.6) | collective-permute-done | bytes 368672 | tf_op jit(solution)/shard_map/ppermute | solution.py:735
  35.7 1.8 %collective-permute-start.13 = (bf16[576,768]{1,0:T(8,128)(2,1)S(1)}, bf16[576,768]{1,0:T(8,128)(2,1)S(1)}, u32[]{:S(2)}, u32[]{:S(2)}) collective-permute-start(bf16[576,768]{1,0:T(8,128)(2,1)S(1)} %get-tuple-element.113), channel_id=1, source_target_pairs={{0,2},{1,3},{2,0},{3,1},{4,6},{5,7},{6,4},{7,5},{8,10},{9,11},{10,... | collective-permute-start | bytes 2654216 | tf_op jit(solution)/shard_map/ppermute | solution.py:735
  41.2 7.9 %collective-permute-done.11.refs_5_ = bf16[10,48,384]{2,1,0:T(8,128)(2,1)S(1)} collective-permute-done((bf16[10,48,384]{2,1,0:T(8,128)(2,1)S(1)}, bf16[10,48,384]{2,1,0:T(8,128)(2,1)S(1)}, u32[]{:S(2)}, u32[]{:S(2)}) %collective-permute-start.11) | collective-permute-done | bytes 368672 | tf_op jit(solution)/shard_map/ppermute | solution.py:735
  50.8 4.7 %collective-permute-done.12.refs_9_.refs_10_ = bf16[256,768]{1,0:T(8,128)(2,1)S(1)} collective-permute-done((bf16[256,768]{1,0:T(8,128)(2,1)S(1)}, bf16[256,768]{1,0:T(8,128)(2,1)S(1)}, u32[]{:S(2)}, u32[]{:S(2)}) %collective-permute-start.12) | collective-permute-done | bytes 393248 | tf_op jit(solution)/shard_map/ppermute | solution.py:735
  57.9 1.7 %collective-permute-start.18 = (bf16[512,768]{1,0:T(8,128)(2,1)S(1)}, bf16[512,768]{1,0:T(8,128)(2,1)S(1)}, u32[]{:S(2)}, u32[]{:S(2)}) collective-permute-start(bf16[512,768]{1,0:T(8,128)(2,1)S(1)} %get-tuple-element.120), channel_id=1, source_target_pairs={{0,2},{1,3},{2,0},{3,1},{4,6},{5,7},{6,4},{7,5},{8,10},{9,11},{10,... | collective-permute-start | bytes 2359304 | tf_op jit(solution)/shard_map/ppermute | solution.py:735
  62.7 9.7 %attend_forward.3 = (bf16[576,512]{1,0:T(8,128)(2,1)}, bf16[192,512]{1,0:T(8,128)(2,1)}, bf16[3,512,512]{2,1,0:T(8,128)(2,1)}, bf16[576,512]{1,0:T(8,128)(2,1)},...) custom-call(s32[6]{0:T(128)S(1)} %stack.27.meta.refs_0_.refs_1_.refs, ...), custom_call_target="tpu_custom_call" | custom-call | bytes 1024 | tf_op jit(solution)/shard_map/attend_forward/pallas_call | solution.py:193
  72.5 3.4 %ffn_forward.3 = (bf16[2,512,768]{2,1,0:T(8,128)(2,1)S(1)}, f32[512,768]{1,0:T(8,128)S(1)}) custom-call(f32[512,768]{1,0:T(8,128)S(1)} %get-tuple-element.115.refs_0_.refs_1_, f32[512,768]{1,0:T(8,128)S(1)} %get-tuple-element.115.refs_0_.refs_1_, bf16[768,768]{1,0:T(8,128)(2,1)S(1)} %copy-done, ...), custom_call_target="tpu_custom_call" | custom-call | bytes 1024 | tf_op jit(solution)/shard_map/ffn_forward/pallas_call | solution.py:231
  79.8 2.4 %ffn_forward.4 = (bf16[1,512,768]{2,1,0:T(8,128)(2,1)S(1)}, f32[512,768]{1,0:T(8,128)S(1)}) custom-call(f32[512,768]{1,0:T(8,128)S(1)} %get-tuple-element.115.refs_0_.refs_1_, f32[512,768]{1,0:T(8,128)S(1)} %get-tuple-element.116.refs_0_.refs_1_, bf16[768,768]{1,0:T(8,128)(2,1)S(1)} %get-tuple-element.122.refs_2_.refs_4_, ...), custom_call_target="tpu_custom_call" | custom-call | bytes 1024 | tf_op jit(solution)/shard_map/ffn_forward/pallas_call | solution.py:231
  83.2 2.4 %ffn_forward.5 = (bf16[1,512,768]{2,1,0:T(8,128)(2,1)S(1)}, f32[512,768]{1,0:T(8,128)S(1)}) custom-call(f32[512,768]{1,0:T(8,128)S(1)} %get-tuple-element.115.refs_0_.refs_1_, f32[512,768]{1,0:T(8,128)S(1)} %get-tuple-element.124.refs_1_, bf16[768,768]{1,0:T(8,128)(2,1)S(1)} %collective-permute-done.21.refs_2_.refs_5_, ...), custom_call_target="tpu_custom_call" | custom-call | bytes 1024 | tf_op jit(solution)/shard_map/ffn_forward/pallas_call | solution.py:231
  86.7 14.0 %merging.1 = (f32[512,768]{1,0:T(8,128)}, f32[512,768]{1,0:T(8,128)S(1)}, bf16[512,768]{1,0:T(8,128)(2,1)S(1)}, bf16[512,768]{1,0:T(8,128)(2,1)S(1)}, bf16[2,2,4...) custom-call(s32[6]{0:T(128)S(1)} %stack.27.meta.refs_0_.refs_1_.refs_3_.refs_2_, ...), custom_call_target="tpu_custom_call" | custom-call | bytes 1024 | tf_op jit(solution)/shard_map/merging/pallas_call | solution.py:399
  101.0 2.1 %merging_input.1 = (f32[512,768]{1,0:T(8,128)S(1)}, bf16[512,768]{1,0:T(8,128)(2,1)S(1)}) custom-call(f32[512,768]{1,0:T(8,128)S(1)} %get-tuple-element.125.refs_0_.sums, f32[8,768]{1,0:T(8,128)S(1)} %get-tuple-element.102.refs_5_.refs_4_.lines.refs_1_.refs_12_, f32[512,768]{1,0:T(8,128)S(1)} %get-tuple-element.128.refs_2_, ...), custom_call_target="tpu_custom_call" | custom-call | bytes 1024 | tf_op jit(solution)/shard_map/merging_input/pallas_call | solution.py:428
  107.7 3.1 %ffn_backward.2.refs_1_ = f32[512,768]{1,0:T(8,128)S(1)} custom-call(bf16[2,4,80,384]{3,2,1,0:T(8,128)(2,1)S(1)} %get-tuple-element.135.refs_0_.refs_1_, bf16[512,768]{1,0:T(8,128)(2,1)S(1)} %get-tuple-element.131.refs_1_.refs_0_, f32[512,768]{1,0:T(8,128)S(1)} %get-tuple-element.132.refs_0_.refs_2_, bf16[2,512,768]{2,1,0:T(8,128)(2,1)S(1)} %get-tuple-element.136.refs_3_, ...), custom_call_target="tpu_custom_call" | custom-call | bytes 1024 | tf_op jit(solution)/shard_map/ffn_backward/pallas_call | solution.py:468
  110.9 3.5 %ffn_backward.3 = (f32[512,768]{1,0:T(8,128)S(1)}, bf16[512,768]{1,0:T(8,128)(2,1)S(1)}) custom-call(bf16[512,768]{1,0:T(8,128)(2,1)S(1)} %get-tuple-element.131.refs_1_.refs_0_, f32[512,768]{1,0:T(8,128)S(1)} %ffn_backward.2.refs_1_, bf16[1,512,768]{2,1,0:T(8,128)(2,1)S(1)} %get-tuple-element.137.refs_2_, ...), custom_call_target="tpu_custom_call" | custom-call | bytes 1024 | tf_op jit(solution)/shard_map/ffn_backward/pallas_call | solution.py:468
  114.4 3.7 %attend_backward.4 = (f32[512,768]{1,0:T(8,128)S(1)}, f32[8,128]{1,0:T(8,128)S(1)}) custom-call(bf16[512,768]{1,0:T(8,128)(2,1)S(1)} %get-tuple-element.141.refs_0_.refs_1_, f32[512,768]{1,0:T(8,128)S(1)} %get-tuple-element.142.refs_1_, bf16[576,512]{1,0:T(8,128)(2,1)S(1)} %copy-done.9, bf16[192,512]{1,0:T(8,128)(2,1)S(1)} %copy-done.13, ...), custom_call_target="tpu_custom_call" | custom-call | bytes 1024 | tf_op jit(solution)/shard_map/attend_backward/pallas_call | solution.py:521
  122.5 3.6 %attend_backward.5 = (f32[512,768]{1,0:T(8,128)S(1)}, f32[8,128]{1,0:T(8,128)S(1)}) custom-call(bf16[4,80,384]{2,1,0:T(8,128)(2,1)S(1)} %get-tuple-element.150.refs_0_.refs_1_, bf16[512,768]{1,0:T(8,128)(2,1)S(1)} %get-tuple-element.141.refs_0_.refs_1_, f32[512,768]{1,0:T(8,128)S(1)} %get-tuple-element.151.refs_2_, bf16[576,512]{1,0:T(8,128)(2,1)S(1)} %copy-done.8, ...), custom_call_target="tpu_custom_call" | custom-call | bytes 1024 | tf_op jit(solution)/shard_map/attend_backward/pallas_call | solution.py:521
  127.8 2.7 %collective-permute-start.29 = (bf16[80,768]{1,0:T(8,128)(2,1)S(1)}, bf16[80,768]{1,0:T(8,128)(2,1)S(1)}, u32[]{:S(2)}, u32[]{:S(2)}) collective-permute-start(bf16[80,768]{1,0:T(8,128)(2,1)S(1)} %get-tuple-element.171), channel_id=1, source_target_pairs={{0,16},{1,17},{2,18},{3,19},{4,20},{5,21},{6,22},{7,23},{8,24},{9,... | collective-permute-start | bytes 368648 | tf_op jit(solution)/shard_map/ppermute | solution.py:735
  132.1 3.1 %attend_backward.6 = (f32[512,768]{1,0:T(8,128)S(1)}, f32[8,128]{1,0:T(8,128)S(1)}) custom-call(bf16[80,768]{1,0:T(8,128)(2,1)S(1)} %get-tuple-element.159.refs_0_.refs_1_, bf16[512,768]{1,0:T(8,128)(2,1)S(1)} %get-tuple-element.141.refs_0_.refs_1_, f32[512,768]{1,0:T(8,128)S(1)} %get-tuple-element.160.refs_2_, bf16[576,512]{1,0:T(8,128)(2,1)S(1)} %copy-done.11, ...), custom_call_target="tpu_custom_call" | custom-call | bytes 1024 | tf_op jit(solution)/shard_map/attend_backward/pallas_call | solution.py:521
  135.2 4.0 %attend_backward.7 = (f32[512,768]{1,0:T(8,128)}, f32[8,128]{1,0:T(8,128)S(1)}) custom-call(f32[8,128]{1,0:T(8,128)S(1)} %get-tuple-element.164.refs_0_, bf16[512,768]{1,0:T(8,128)(2,1)S(1)} %get-tuple-element.141.refs_0_.refs_1_, f32[512,768]{1,0:T(8,128)S(1)} %get-tuple-element.165.refs_2_, bf16[576,512]{1,0:T(8,128)(2,1)S(1)} %copy-done.10, ...), custom_call_target="tpu_custom_call" | custom-call | bytes 1024 | tf_op jit(solution)/shard_map/attend_backward/pallas_call | solution.py:521
  (103 shorter events, 37.8 us)
Async XLA Ops:
  4.4 7.9 %collective-permute-start.1 = (bf16[768,768]{1,0:T(8,128)(2,1)S(1)}, bf16[768,768]{1,0:T(8,128)(2,1)S(1)}, u32[]{:S(2)}, u32[]{:S(2)}) collective-permute-start(bf16[768,768]{1,0:T(8,128)(2,1)S(1)} %get-tuple-element.96.refs_1_.refs_6_.refs_5_), channel_id=1, source_target_pairs={{0,1},{1,0},{2,3},{3,2},{4,5},{5,4},{6,7},{7,6},{8,9},{9,8},{10,11... | collective-permute-start | bytes 3538952 | tf_op jit(solution)/shard_map/ppermute | solution.py:735
  4.5 7.8 %collective-permute-start.2 = (bf16[5,48,384]{2,1,0:T(8,128)(2,1)S(1)}, bf16[5,48,384]{2,1,0:T(8,128)(2,1)S(1)}, u32[]{:S(2)}, u32[]{:S(2)}) collective-permute-start(bf16[5,48,384]{2,1,0:T(8,128)(2,1)S(1)} %get-tuple-element.100.refs_5_), channel_id=1, source_target_pairs={{0,2},{1,3},{2,0},{3,1},{4,6},{5,7},{6,4},{7,5},{8,10},{9,11},{10,... | collective-permute-start | bytes 552968 | tf_op jit(solution)/shard_map/ppermute | solution.py:735
  12.9 22.2 %collective-permute-start.3 = (bf16[768,768]{1,0:T(8,128)(2,1)S(1)}, bf16[768,768]{1,0:T(8,128)(2,1)S(1)}, u32[]{:S(2)}, u32[]{:S(2)}) collective-permute-start(bf16[768,768]{1,0:T(8,128)(2,1)S(1)} %get-tuple-element.104), channel_id=1, source_target_pairs={{0,1},{1,0},{2,3},{3,2},{4,5},{5,4},{6,7},{7,6},{8,9},{9,8},{10,11... | collective-permute-start | bytes 3538952 | tf_op jit(solution)/shard_map/ppermute | solution.py:735
  13.0 22.1 %collective-permute-start.4 = (bf16[768,768]{1,0:T(8,128)(2,1)S(1)}, bf16[768,768]{1,0:T(8,128)(2,1)S(1)}, u32[]{:S(2)}, u32[]{:S(2)}) collective-permute-start(bf16[768,768]{1,0:T(8,128)(2,1)S(1)} %get-tuple-element.105), channel_id=1, source_target_pairs={{0,1},{1,0},{2,3},{3,2},{4,5},{5,4},{6,7},{7,6},{8,9},{9,8},{10,11... | collective-permute-start | bytes 3538952 | tf_op jit(solution)/shard_map/ppermute | solution.py:735
  13.5 21.6 %collective-permute-start.7 = (bf16[576,768]{1,0:T(8,128)(2,1)S(1)}, bf16[576,768]{1,0:T(8,128)(2,1)S(1)}, u32[]{:S(2)}, u32[]{:S(2)}) collective-permute-start(bf16[576,768]{1,0:T(8,128)(2,1)S(1)} %get-tuple-element.107), channel_id=1, source_target_pairs={{0,2},{1,3},{2,0},{3,1},{4,6},{5,7},{6,4},{7,5},{8,10},{9,11},{10,... | collective-permute-start | bytes 2654216 | tf_op jit(solution)/shard_map/ppermute | solution.py:735
  15.2 19.1 %collective-permute-start.6 = (bf16[10,48,384]{2,1,0:T(8,128)(2,1)S(1)}, bf16[10,48,384]{2,1,0:T(8,128)(2,1)S(1)}, u32[]{:S(2)}, u32[]{:S(2)}) collective-permute-start(bf16[10,48,384]{2,1,0:T(8,128)(2,1)S(1)} %get-tuple-element.101.refs_0_.refs_7_), channel_id=1, source_target_pairs={{0,16},{1,17},{2,18},{3,19},{4,20},{5,21},{6,22},{7,23},{8,24},{9,... | collective-permute-start | bytes 1105928 | tf_op jit(solution)/shard_map/ppermute | solution.py:735
  17.8 16.5 %collective-permute-start.5 = (bf16[10,48,384]{2,1,0:T(8,128)(2,1)S(1)}, bf16[10,48,384]{2,1,0:T(8,128)(2,1)S(1)}, u32[]{:S(2)}, u32[]{:S(2)}) collective-permute-start(bf16[10,48,384]{2,1,0:T(8,128)(2,1)S(1)} %get-tuple-element.101.refs_0_.refs_7_), channel_id=1, source_target_pairs={{0,4},{1,5},{2,6},{3,7},{4,0},{5,1},{6,2},{7,3},{8,12},{9,13},{10,... | collective-permute-start | bytes 1105928 | tf_op jit(solution)/shard_map/ppermute | solution.py:735
  35.7 20.9 %collective-permute-start.13 = (bf16[576,768]{1,0:T(8,128)(2,1)S(1)}, bf16[576,768]{1,0:T(8,128)(2,1)S(1)}, u32[]{:S(2)}, u32[]{:S(2)}) collective-permute-start(bf16[576,768]{1,0:T(8,128)(2,1)S(1)} %get-tuple-element.113), channel_id=1, source_target_pairs={{0,2},{1,3},{2,0},{3,1},{4,6},{5,7},{6,4},{7,5},{8,10},{9,11},{10,... | collective-permute-start | bytes 2654216 | tf_op jit(solution)/shard_map/ppermute | solution.py:735
  37.6 11.5 %collective-permute-start.11 = (bf16[10,48,384]{2,1,0:T(8,128)(2,1)S(1)}, bf16[10,48,384]{2,1,0:T(8,128)(2,1)S(1)}, u32[]{:S(2)}, u32[]{:S(2)}) collective-permute-start(bf16[10,48,384]{2,1,0:T(8,128)(2,1)S(1)} %get-tuple-element.111), channel_id=1, source_target_pairs={{0,4},{1,5},{2,6},{3,7},{4,0},{5,1},{6,2},{7,3},{8,12},{9,13},{10,... | collective-permute-start | bytes 1105928 | tf_op jit(solution)/shard_map/ppermute | solution.py:735
  39.1 17.1 %collective-permute-start.10 = (bf16[20,48,384]{2,1,0:T(8,128)(2,1)S(1)}, bf16[20,48,384]{2,1,0:T(8,128)(2,1)S(1)}, u32[]{:S(2)}, u32[]{:S(2)}) collective-permute-start(bf16[20,48,384]{2,1,0:T(8,128)(2,1)S(1)} %get-tuple-element.108.refs_2_), channel_id=1, source_target_pairs={{0,8},{1,9},{2,10},{3,11},{4,12},{5,13},{6,14},{7,15},{8,0},{9,1},... | collective-permute-start | bytes 2211848 | tf_op jit(solution)/shard_map/ppermute | solution.py:735
  40.6 15.5 %collective-permute-start.8 = (bf16[20,48,384]{2,1,0:T(8,128)(2,1)S(1)}, bf16[20,48,384]{2,1,0:T(8,128)(2,1)S(1)}, u32[]{:S(2)}, u32[]{:S(2)}) collective-permute-start(bf16[20,48,384]{2,1,0:T(8,128)(2,1)S(1)} %get-tuple-element.108.refs_2_), channel_id=1, source_target_pairs={{0,1},{1,0},{2,3},{3,2},{4,5},{5,4},{6,7},{7,6},{8,9},{9,8},{10,11... | collective-permute-start | bytes 2211848 | tf_op jit(solution)/shard_map/ppermute | solution.py:735
  40.7 14.8 %collective-permute-start.12 = (bf16[256,768]{1,0:T(8,128)(2,1)S(1)}, bf16[256,768]{1,0:T(8,128)(2,1)S(1)}, u32[]{:S(2)}, u32[]{:S(2)}) collective-permute-start(bf16[256,768]{1,0:T(8,128)(2,1)S(1)} %get-tuple-element.112), channel_id=1, source_target_pairs={{0,4},{1,5},{2,6},{3,7},{4,0},{5,1},{6,2},{7,3},{8,12},{9,13},{10,... | collective-permute-start | bytes 1179656 | tf_op jit(solution)/shard_map/ppermute | solution.py:735
  57.9 20.6 %collective-permute-start.18 = (bf16[512,768]{1,0:T(8,128)(2,1)S(1)}, bf16[512,768]{1,0:T(8,128)(2,1)S(1)}, u32[]{:S(2)}, u32[]{:S(2)}) collective-permute-start(bf16[512,768]{1,0:T(8,128)(2,1)S(1)} %get-tuple-element.120), channel_id=1, source_target_pairs={{0,2},{1,3},{2,0},{3,1},{4,6},{5,7},{6,4},{7,5},{8,10},{9,11},{10,... | collective-permute-start | bytes 2359304 | tf_op jit(solution)/shard_map/ppermute | solution.py:735
  59.6 16.3 %collective-permute-start.15 = (bf16[20,48,384]{2,1,0:T(8,128)(2,1)S(1)}, bf16[20,48,384]{2,1,0:T(8,128)(2,1)S(1)}, u32[]{:S(2)}, u32[]{:S(2)}) collective-permute-start(bf16[20,48,384]{2,1,0:T(8,128)(2,1)S(1)} %get-tuple-element.117.refs_4_), channel_id=1, source_target_pairs={{0,1},{1,0},{2,3},{3,2},{4,5},{5,4},{6,7},{7,6},{8,9},{9,8},{10,11... | collective-permute-start | bytes 2211848 | tf_op jit(solution)/shard_map/ppermute | solution.py:735
  59.6 18.9 %collective-permute-start.19 = (bf16[20,48,384]{2,1,0:T(8,128)(2,1)S(1)}, bf16[20,48,384]{2,1,0:T(8,128)(2,1)S(1)}, u32[]{:S(2)}, u32[]{:S(2)}) collective-permute-start(bf16[20,48,384]{2,1,0:T(8,128)(2,1)S(1)} %get-tuple-element.117.refs_4_), channel_id=1, source_target_pairs={{0,4},{1,5},{2,6},{3,7},{4,0},{5,1},{6,2},{7,3},{8,12},{9,13},{10,... | collective-permute-start | bytes 2211848 | tf_op jit(solution)/shard_map/ppermute | solution.py:735
  61.1 16.2 %collective-permute-start.20 = (bf16[384,768]{1,0:T(8,128)(2,1)S(1)}, bf16[384,768]{1,0:T(8,128)(2,1)S(1)}, u32[]{:S(2)}, u32[]{:S(2)}) collective-permute-start(bf16[384,768]{1,0:T(8,128)(2,1)S(1)} %get-tuple-element.121.refs_6_), channel_id=1, source_target_pairs={{0,8},{1,9},{2,10},{3,11},{4,12},{5,13},{6,14},{7,15},{8,0},{9,1},... | collective-permute-start | bytes 1769480 | tf_op jit(solution)/shard_map/ppermute | solution.py:735
  62.7 14.6 %collective-permute-start.17 = (bf16[256,768]{1,0:T(8,128)(2,1)S(1)}, bf16[256,768]{1,0:T(8,128)(2,1)S(1)}, u32[]{:S(2)}, u32[]{:S(2)}) collective-permute-start(bf16[256,768]{1,0:T(8,128)(2,1)S(1)} %get-tuple-element.119.refs_3_.refs_6_), channel_id=1, source_target_pairs={{0,1},{1,0},{2,3},{3,2},{4,5},{5,4},{6,7},{7,6},{8,9},{9,8},{10,11... | collective-permute-start | bytes 1179656 | tf_op jit(solution)/shard_map/ppermute | solution.py:735
  105.5 13.3 %collective-permute-start.25 = (bf16[2,4,80,384]{3,2,1,0:T(8,128)(2,1)S(1)}, bf16[2,4,80,384]{3,2,1,0:T(8,128)(2,1)S(1)}, u32[]{:S(2)}, u32[]{:S(2)}) collective-permute-start(bf16[2,4,80,384]{3,2,1,0:T(8,128)(2,1)S(1)} %get-tuple-element.147), channel_id=1, source_target_pairs={{0,2},{1,3},{2,0},{3,1},{4,6},{5,7},{6,4},{7,5},{8,10},{9,11},{10,... | collective-permute-start | bytes 1474568 | tf_op jit(solution)/shard_map/ppermute | solution.py:735
  106.2 13.0 %collective-permute-start.26 = (bf16[2,4,80,384]{3,2,1,0:T(8,128)(2,1)S(1)}, bf16[2,4,80,384]{3,2,1,0:T(8,128)(2,1)S(1)}, u32[]{:S(2)}, u32[]{:S(2)}) collective-permute-start(bf16[2,4,80,384]{3,2,1,0:T(8,128)(2,1)S(1)} %get-tuple-element.149), channel_id=1, source_target_pairs={{0,4},{1,5},{2,6},{3,7},{4,0},{5,1},{6,2},{7,3},{8,12},{9,13},{10,... | collective-permute-start | bytes 1474568 | tf_op jit(solution)/shard_map/ppermute | solution.py:735
  119.5 6.9 %collective-permute-start.27 = (bf16[4,80,384]{2,1,0:T(8,128)(2,1)S(1)}, bf16[4,80,384]{2,1,0:T(8,128)(2,1)S(1)}, u32[]{:S(2)}, u32[]{:S(2)}) collective-permute-start(bf16[4,80,384]{2,1,0:T(8,128)(2,1)S(1)} %get-tuple-element.156), channel_id=1, source_target_pairs={{0,4},{1,5},{2,6},{3,7},{4,0},{5,1},{6,2},{7,3},{8,12},{9,13},{10,... | collective-permute-start | bytes 737288 | tf_op jit(solution)/shard_map/ppermute | solution.py:735
  121.1 6.6 %collective-permute-start.28 = (bf16[4,80,384]{2,1,0:T(8,128)(2,1)S(1)}, bf16[4,80,384]{2,1,0:T(8,128)(2,1)S(1)}, u32[]{:S(2)}, u32[]{:S(2)}) collective-permute-start(bf16[4,80,384]{2,1,0:T(8,128)(2,1)S(1)} %get-tuple-element.158), channel_id=1, source_target_pairs={{0,2},{1,3},{2,0},{3,1},{4,6},{5,7},{6,4},{7,5},{8,10},{9,11},{10,... | collective-permute-start | bytes 737288 | tf_op jit(solution)/shard_map/ppermute | solution.py:735
  127.8 11.4 %collective-permute-start.29 = (bf16[80,768]{1,0:T(8,128)(2,1)S(1)}, bf16[80,768]{1,0:T(8,128)(2,1)S(1)}, u32[]{:S(2)}, u32[]{:S(2)}) collective-permute-start(bf16[80,768]{1,0:T(8,128)(2,1)S(1)} %get-tuple-element.171), channel_id=1, source_target_pairs={{0,16},{1,17},{2,18},{3,19},{4,20},{5,21},{6,22},{7,23},{8,24},{9,... | collective-permute-start | bytes 368648 | tf_op jit(solution)/shard_map/ppermute | solution.py:735
  130.5 8.8 %collective-permute-start.30 = (bf16[80,768]{1,0:T(8,128)(2,1)S(1)}, bf16[80,768]{1,0:T(8,128)(2,1)S(1)}, u32[]{:S(2)}, u32[]{:S(2)}) collective-permute-start(bf16[80,768]{1,0:T(8,128)(2,1)S(1)} %get-tuple-element.172), channel_id=1, source_target_pairs={{0,24},{1,25},{2,26},{3,27},{4,28},{5,29},{6,30},{7,31},{8,16},{9,... | collective-permute-start | bytes 368648 | tf_op jit(solution)/shard_map/ppermute | solution.py:735
  131.8 7.4 %collective-permute-start.31 = (bf16[80,768]{1,0:T(8,128)(2,1)S(1)}, bf16[80,768]{1,0:T(8,128)(2,1)S(1)}, u32[]{:S(2)}, u32[]{:S(2)}) collective-permute-start(bf16[80,768]{1,0:T(8,128)(2,1)S(1)} %get-tuple-element.173), channel_id=1, source_target_pairs={{0,8},{1,9},{2,10},{3,11},{4,12},{5,13},{6,14},{7,15},{8,0},{9,1},... | collective-permute-start | bytes 368648 | tf_op jit(solution)/shard_map/ppermute | solution.py:735
  (25 other events, 130.8 us)

commit v7 on v5

--- a/solution.py
+++ b/solution.py
@@ -221,7 +221,7 @@
                 start += out.shape[0]
         sum_out[rows] = total
 
-    by_chunks(first.shape[0], chunk)
+    by_chunks(first.shape[0], chunk, CHUNK * 2 // quarters)
 
 
 def call_ffn_forward(deps, first, before, in_quarters, out_quarters):
@@ -923,7 +923,7 @@
     def attention(deps, *quarters):
         for i in quarters:
             done["sum"], token = call_attend_backward(
-                deps, columns, i > 1, i == 3, done["low"], done["sum"], saved[i], attn_quarters[i]
+                deps, columns, i > 2, i == 3, done["low"], done["sum"], saved[i], attn_quarters[i]
             )
             deps = [token]
         return token

time: 140 us -> 141 us (level)
  no operation moved by 1% of the time
where the time goes in v7:
time: 141 us; the launch traced here: 140 us
  Pallas kernels  75.7 us (54%)
  waiting for transfers between devices  32.2 us (23%)
  starting transfers between devices  30.7 us (22%)
    ppermute x32, waiting for transfers between devices, flip(): return lax.ppermute(array, AXES, [(i, i ^ bits) for i in range(self.count)])  32.2 us
    ppermute x32, starting transfers between devices, flip(): return lax.ppermute(array, AXES, [(i, i ^ bits) for i in range(self.count)])  30.7 us
    pallas_call x2, Pallas kernels, call_attend_forward(): kernel(functools.partial(attend_forward, columns, last), deps, ATTEND_MIB...  18.6 us
    pallas_call x4, Pallas kernels, call_attend_backward(): kernel(functools.partial(attend_backward, columns, unroll, leaving), deps...  14.9 us
    pallas_call x1, Pallas kernels, call_merging(): pl.pallas_call(functools.partial(merging, n_adapters), in_specs=[SMEM, SM...  14 us
    pallas_call x3, Pallas kernels, call_ffn_forward(): kernel(functools.partial(ffn_forward, quarters, len(out_quarters) // quar...  7.81 us
    pallas_call x2, Pallas kernels, call_ffn_backward(): kernel(functools.partial(ffn_backward, last, len(out_quarters) // 2, len(...  6.54 us
  transfers between devices with their start and end apart: 32, of which 15 were waited for; matrix products, arithmetic and copies ran while one was open for 0% of the time, Pallas kernels for 39%

profile of v7, /device:TPU:0, one launch (start us, length us, event | category | flops | bytes accessed | tf_op | source)
XLA Modules:
  0.0 140.2 jit_solution(12514908249774925484)
XLA Ops:
  4.5 2.9 %collective-permute-start.2 = (bf16[5,48,384]{2,1,0:T(8,128)(2,1)S(1)}, bf16[5,48,384]{2,1,0:T(8,128)(2,1)S(1)}, u32[]{:S(2)}, u32[]{:S(2)}) collective-permute-start(bf16[5,48,384]{2,1,0:T(8,128)(2,1)S(1)} %get-tuple-element.100.refs_5_), channel_id=1, source_target_pairs={{0,2},{1,3},{2,0},{3,1},{4,6},{5,7},{6,4},{7,5},{8,10},{9,11},{10,... | collective-permute-start | bytes 552968 | tf_op jit(solution)/shard_map/ppermute | solution.py:735
  7.4 2.0 %prepare_shares.1 = (bf16[576,768]{1,0:T(8,128)(2,1)S(1)}, bf16[576,768]{1,0:T(8,128)(2,1)S(1)}, bf16[512,768]{1,0:T(8,128)(2,1)S(1)}, bf16[768,768]{1,0:T(8,128)(2,1)S(1)}, bf16[768,768]{1,0:T(8,128)(2,1)S(1)}) custom-call(s32[6]{0:T(128)S(1)} %stack.27.meta.refs_0_.refs_1_.refs_3_.refs_2_, bf16[768,768]{1,0:T(8,128)(2,1)S(1)} %get-tuple-element.96.refs_1_.refs_6_.refs_5_, ...), custom_call_target="tpu_custom_call" | custom-call | bytes 1024 | tf_op jit(solution)/shard_map/prepare_shares/pallas_call | solution.py:610
  9.4 2.9 %collective-permute-done.2.refs_6_ = bf16[5,48,384]{2,1,0:T(8,128)(2,1)S(1)} collective-permute-done((bf16[5,48,384]{2,1,0:T(8,128)(2,1)S(1)}, bf16[5,48,384]{2,1,0:T(8,128)(2,1)S(1)}, u32[]{:S(2)}, u32[]{:S(2)}) %collective-permute-start.2) | collective-permute-done | bytes 184352 | tf_op jit(solution)/shard_map/ppermute | solution.py:735
  13.5 1.7 %collective-permute-start.7 = (bf16[576,768]{1,0:T(8,128)(2,1)S(1)}, bf16[576,768]{1,0:T(8,128)(2,1)S(1)}, u32[]{:S(2)}, u32[]{:S(2)}) collective-permute-start(bf16[576,768]{1,0:T(8,128)(2,1)S(1)} %get-tuple-element.107), channel_id=1, source_target_pairs={{0,2},{1,3},{2,0},{3,1},{4,6},{5,7},{6,4},{7,5},{8,10},{9,11},{10,... | collective-permute-start | bytes 2654216 | tf_op jit(solution)/shard_map/ppermute | solution.py:735
  15.2 2.6 %collective-permute-start.6 = (bf16[10,48,384]{2,1,0:T(8,128)(2,1)S(1)}, bf16[10,48,384]{2,1,0:T(8,128)(2,1)S(1)}, u32[]{:S(2)}, u32[]{:S(2)}) collective-permute-start(bf16[10,48,384]{2,1,0:T(8,128)(2,1)S(1)} %get-tuple-element.101.refs_0_.refs_7_), channel_id=1, source_target_pairs={{0,16},{1,17},{2,18},{3,19},{4,20},{5,21},{6,22},{7,23},{8,24},{9,... | collective-permute-start | bytes 1105928 | tf_op jit(solution)/shard_map/ppermute | solution.py:735
  19.3 8.9 %attend_forward.2 = (bf16[576,512]{1,0:T(8,128)(2,1)}, bf16[192,512]{1,0:T(8,128)(2,1)}, bf16[3,512,512]{2,1,0:T(8,128)(2,1)}, bf16[576,512]{1,0:T(8,128)(2,1)},...) custom-call(bf16[10,48,384]{2,1,0:T(8,128)(2,1)S(1)} %get-tuple-element.101.refs_0_.refs_7_, ...), custom_call_target="tpu_custom_call" | custom-call | bytes 1024 | tf_op jit(solution)/shard_map/attend_forward/pallas_call | solution.py:193
  28.2 6.1 %collective-permute-done.6.refs_8_ = bf16[10,48,384]{2,1,0:T(8,128)(2,1)S(1)} collective-permute-done((bf16[10,48,384]{2,1,0:T(8,128)(2,1)S(1)}, bf16[10,48,384]{2,1,0:T(8,128)(2,1)S(1)}, u32[]{:S(2)}, u32[]{:S(2)}) %collective-permute-start.6) | collective-permute-done | bytes 368672 | tf_op jit(solution)/shard_map/ppermute | solution.py:735
  35.7 1.8 %collective-permute-start.13 = (bf16[576,768]{1,0:T(8,128)(2,1)S(1)}, bf16[576,768]{1,0:T(8,128)(2,1)S(1)}, u32[]{:S(2)}, u32[]{:S(2)}) collective-permute-start(bf16[576,768]{1,0:T(8,128)(2,1)S(1)} %get-tuple-element.113), channel_id=1, source_target_pairs={{0,2},{1,3},{2,0},{3,1},{4,6},{5,7},{6,4},{7,5},{8,10},{9,11},{10,... | collective-permute-start | bytes 2654216 | tf_op jit(solution)/shard_map/ppermute | solution.py:735
  41.2 7.9 %collective-permute-done.11.refs_5_ = bf16[10,48,384]{2,1,0:T(8,128)(2,1)S(1)} collective-permute-done((bf16[10,48,384]{2,1,0:T(8,128)(2,1)S(1)}, bf16[10,48,384]{2,1,0:T(8,128)(2,1)S(1)}, u32[]{:S(2)}, u32[]{:S(2)}) %collective-permute-start.11) | collective-permute-done | bytes 368672 | tf_op jit(solution)/shard_map/ppermute | solution.py:735
  50.8 4.7 %collective-permute-done.12.refs_9_.refs_10_ = bf16[256,768]{1,0:T(8,128)(2,1)S(1)} collective-permute-done((bf16[256,768]{1,0:T(8,128)(2,1)S(1)}, bf16[256,768]{1,0:T(8,128)(2,1)S(1)}, u32[]{:S(2)}, u32[]{:S(2)}) %collective-permute-start.12) | collective-permute-done | bytes 393248 | tf_op jit(solution)/shard_map/ppermute | solution.py:735
  62.7 9.7 %attend_forward.3 = (bf16[576,512]{1,0:T(8,128)(2,1)}, bf16[192,512]{1,0:T(8,128)(2,1)}, bf16[3,512,512]{2,1,0:T(8,128)(2,1)}, bf16[576,512]{1,0:T(8,128)(2,1)},...) custom-call(s32[6]{0:T(128)S(1)} %stack.27.meta.refs_0_.refs_1_.refs, ...), custom_call_target="tpu_custom_call" | custom-call | bytes 1024 | tf_op jit(solution)/shard_map/attend_forward/pallas_call | solution.py:193
  72.5 3.5 %ffn_forward.3 = (bf16[2,512,768]{2,1,0:T(8,128)(2,1)S(1)}, f32[512,768]{1,0:T(8,128)S(1)}) custom-call(f32[512,768]{1,0:T(8,128)S(1)} %get-tuple-element.115.refs_0_.refs_1_, f32[512,768]{1,0:T(8,128)S(1)} %get-tuple-element.115.refs_0_.refs_1_, bf16[768,768]{1,0:T(8,128)(2,1)S(1)} %copy-done, ...), custom_call_target="tpu_custom_call" | custom-call | bytes 1024 | tf_op jit(solution)/shard_map/ffn_forward/pallas_call | solution.py:231
  79.8 2.2 %ffn_forward.4 = (bf16[1,512,768]{2,1,0:T(8,128)(2,1)S(1)}, f32[512,768]{1,0:T(8,128)S(1)}) custom-call(f32[512,768]{1,0:T(8,128)S(1)} %get-tuple-element.115.refs_0_.refs_1_, f32[512,768]{1,0:T(8,128)S(1)} %get-tuple-element.116.refs_0_.refs_1_, bf16[768,768]{1,0:T(8,128)(2,1)S(1)} %get-tuple-element.122.refs_2_.refs_4_, ...), custom_call_target="tpu_custom_call" | custom-call | bytes 1024 | tf_op jit(solution)/shard_map/ffn_forward/pallas_call | solution.py:231
  83.2 2.2 %ffn_forward.5 = (bf16[1,512,768]{2,1,0:T(8,128)(2,1)S(1)}, f32[512,768]{1,0:T(8,128)S(1)}) custom-call(f32[512,768]{1,0:T(8,128)S(1)} %get-tuple-element.115.refs_0_.refs_1_, f32[512,768]{1,0:T(8,128)S(1)} %get-tuple-element.124.refs_1_, bf16[768,768]{1,0:T(8,128)(2,1)S(1)} %collective-permute-done.21.refs_2_.refs_5_, ...), custom_call_target="tpu_custom_call" | custom-call | bytes 1024 | tf_op jit(solution)/shard_map/ffn_forward/pallas_call | solution.py:231
  86.5 14.0 %merging.1 = (f32[512,768]{1,0:T(8,128)}, f32[512,768]{1,0:T(8,128)S(1)}, bf16[512,768]{1,0:T(8,128)(2,1)S(1)}, bf16[512,768]{1,0:T(8,128)(2,1)S(1)}, bf16[2,2,4...) custom-call(s32[6]{0:T(128)S(1)} %stack.27.meta.refs_0_.refs_1_.refs_3_.refs_2_, ...), custom_call_target="tpu_custom_call" | custom-call | bytes 1024 | tf_op jit(solution)/shard_map/merging/pallas_call | solution.py:399
  100.7 2.0 %merging_input.1 = (f32[512,768]{1,0:T(8,128)S(1)}, bf16[512,768]{1,0:T(8,128)(2,1)S(1)}) custom-call(f32[512,768]{1,0:T(8,128)S(1)} %get-tuple-element.125.refs_0_.sums, f32[8,768]{1,0:T(8,128)S(1)} %get-tuple-element.102.refs_5_.refs_4_.lines.refs_1_.refs_12_, f32[512,768]{1,0:T(8,128)S(1)} %get-tuple-element.128.refs_2_, ...), custom_call_target="tpu_custom_call" | custom-call | bytes 1024 | tf_op jit(solution)/shard_map/merging_input/pallas_call | solution.py:428
  102.8 1.8 %collective-permute-done.24.refs_2_ = bf16[2,2,4,80,768]{4,3,2,1,0:T(8,128)(2,1)S(1)} collective-permute-done((bf16[2,2,4,80,768]{4,3,2,1,0:T(8,128)(2,1)S(1)}, bf16[2,2,4,80,768]{4,3,2,1,0:T(8,128)(2,1)S(1)}, u32[]{:S(2)}, u32[]{:S(2)}) %collective-permute-start.24) | collective-permute-done | bytes 1966112 | tf_op jit(solution)/shard_map/ppermute | solution.py:735
  107.5 3.1 %ffn_backward.2.refs_1_ = f32[512,768]{1,0:T(8,128)S(1)} custom-call(bf16[2,4,80,384]{3,2,1,0:T(8,128)(2,1)S(1)} %get-tuple-element.135.refs_0_.refs_1_, bf16[512,768]{1,0:T(8,128)(2,1)S(1)} %get-tuple-element.131.refs_1_.refs_0_, f32[512,768]{1,0:T(8,128)S(1)} %get-tuple-element.132.refs_0_.refs_2_, bf16[2,512,768]{2,1,0:T(8,128)(2,1)S(1)} %get-tuple-element.136.refs_3_, ...), custom_call_target="tpu_custom_call" | custom-call | bytes 1024 | tf_op jit(solution)/shard_map/ffn_backward/pallas_call | solution.py:468
  110.6 3.4 %ffn_backward.3 = (f32[512,768]{1,0:T(8,128)S(1)}, bf16[512,768]{1,0:T(8,128)(2,1)S(1)}) custom-call(bf16[512,768]{1,0:T(8,128)(2,1)S(1)} %get-tuple-element.131.refs_1_.refs_0_, f32[512,768]{1,0:T(8,128)S(1)} %ffn_backward.2.refs_1_, bf16[1,512,768]{2,1,0:T(8,128)(2,1)S(1)} %get-tuple-element.137.refs_2_, ...), custom_call_target="tpu_custom_call" | custom-call | bytes 1024 | tf_op jit(solution)/shard_map/ffn_backward/pallas_call | solution.py:468
  114.1 3.6 %attend_backward.4 = (f32[512,768]{1,0:T(8,128)S(1)}, f32[8,128]{1,0:T(8,128)S(1)}) custom-call(bf16[512,768]{1,0:T(8,128)(2,1)S(1)} %get-tuple-element.141.refs_0_.refs_1_, f32[512,768]{1,0:T(8,128)S(1)} %get-tuple-element.142.refs_1_, bf16[576,512]{1,0:T(8,128)(2,1)S(1)} %copy-done.9, bf16[192,512]{1,0:T(8,128)(2,1)S(1)} %copy-done.13, ...), custom_call_target="tpu_custom_call" | custom-call | bytes 1024 | tf_op jit(solution)/shard_map/attend_backward/pallas_call | solution.py:521
  122.3 3.6 %attend_backward.5 = (f32[512,768]{1,0:T(8,128)S(1)}, f32[8,128]{1,0:T(8,128)S(1)}) custom-call(bf16[4,80,384]{2,1,0:T(8,128)(2,1)S(1)} %get-tuple-element.150.refs_0_.refs_1_, bf16[512,768]{1,0:T(8,128)(2,1)S(1)} %get-tuple-element.141.refs_0_.refs_1_, f32[512,768]{1,0:T(8,128)S(1)} %get-tuple-element.151.refs_2_, bf16[576,512]{1,0:T(8,128)(2,1)S(1)} %copy-done.8, ...), custom_call_target="tpu_custom_call" | custom-call | bytes 1024 | tf_op jit(solution)/shard_map/attend_backward/pallas_call | solution.py:521
  127.8 2.7 %collective-permute-start.29 = (bf16[80,768]{1,0:T(8,128)(2,1)S(1)}, bf16[80,768]{1,0:T(8,128)(2,1)S(1)}, u32[]{:S(2)}, u32[]{:S(2)}) collective-permute-start(bf16[80,768]{1,0:T(8,128)(2,1)S(1)} %get-tuple-element.171), channel_id=1, source_target_pairs={{0,16},{1,17},{2,18},{3,19},{4,20},{5,21},{6,22},{7,23},{8,24},{9,... | collective-permute-start | bytes 368648 | tf_op jit(solution)/shard_map/ppermute | solution.py:735
  131.8 3.6 %attend_backward.6 = (f32[512,768]{1,0:T(8,128)S(1)}, f32[8,128]{1,0:T(8,128)S(1)}) custom-call(bf16[80,768]{1,0:T(8,128)(2,1)S(1)} %get-tuple-element.159.refs_0_.refs_1_, bf16[512,768]{1,0:T(8,128)(2,1)S(1)} %get-tuple-element.141.refs_0_.refs_1_, f32[512,768]{1,0:T(8,128)S(1)} %get-tuple-element.160.refs_2_, bf16[576,512]{1,0:T(8,128)(2,1)S(1)} %copy-done.11, ...), custom_call_target="tpu_custom_call" | custom-call | bytes 1024 | tf_op jit(solution)/shard_map/attend_backward/pallas_call | solution.py:521
  135.5 4.0 %attend_backward.7 = (f32[512,768]{1,0:T(8,128)}, f32[8,128]{1,0:T(8,128)S(1)}) custom-call(f32[8,128]{1,0:T(8,128)S(1)} %get-tuple-element.164.refs_0_, bf16[512,768]{1,0:T(8,128)(2,1)S(1)} %get-tuple-element.141.refs_0_.refs_1_, f32[512,768]{1,0:T(8,128)S(1)} %get-tuple-element.165.refs_2_, bf16[576,512]{1,0:T(8,128)(2,1)S(1)} %copy-done.10, ...), custom_call_target="tpu_custom_call" | custom-call | bytes 1024 | tf_op jit(solution)/shard_map/attend_backward/pallas_call | solution.py:521
  (103 shorter events, 38.2 us)
Async XLA Ops:
  4.4 7.9 %collective-permute-start.1 = (bf16[768,768]{1,0:T(8,128)(2,1)S(1)}, bf16[768,768]{1,0:T(8,128)(2,1)S(1)}, u32[]{:S(2)}, u32[]{:S(2)}) collective-permute-start(bf16[768,768]{1,0:T(8,128)(2,1)S(1)} %get-tuple-element.96.refs_1_.refs_6_.refs_5_), channel_id=1, source_target_pairs={{0,1},{1,0},{2,3},{3,2},{4,5},{5,4},{6,7},{7,6},{8,9},{9,8},{10,11... | collective-permute-start | bytes 3538952 | tf_op jit(solution)/shard_map/ppermute | solution.py:735
  4.5 7.8 %collective-permute-start.2 = (bf16[5,48,384]{2,1,0:T(8,128)(2,1)S(1)}, bf16[5,48,384]{2,1,0:T(8,128)(2,1)S(1)}, u32[]{:S(2)}, u32[]{:S(2)}) collective-permute-start(bf16[5,48,384]{2,1,0:T(8,128)(2,1)S(1)} %get-tuple-element.100.refs_5_), channel_id=1, source_target_pairs={{0,2},{1,3},{2,0},{3,1},{4,6},{5,7},{6,4},{7,5},{8,10},{9,11},{10,... | collective-permute-start | bytes 552968 | tf_op jit(solution)/shard_map/ppermute | solution.py:735
  12.9 22.2 %collective-permute-start.3 = (bf16[768,768]{1,0:T(8,128)(2,1)S(1)}, bf16[768,768]{1,0:T(8,128)(2,1)S(1)}, u32[]{:S(2)}, u32[]{:S(2)}) collective-permute-start(bf16[768,768]{1,0:T(8,128)(2,1)S(1)} %get-tuple-element.104), channel_id=1, source_target_pairs={{0,1},{1,0},{2,3},{3,2},{4,5},{5,4},{6,7},{7,6},{8,9},{9,8},{10,11... | collective-permute-start | bytes 3538952 | tf_op jit(solution)/shard_map/ppermute | solution.py:735
  13.0 22.1 %collective-permute-start.4 = (bf16[768,768]{1,0:T(8,128)(2,1)S(1)}, bf16[768,768]{1,0:T(8,128)(2,1)S(1)}, u32[]{:S(2)}, u32[]{:S(2)}) collective-permute-start(bf16[768,768]{1,0:T(8,128)(2,1)S(1)} %get-tuple-element.105), channel_id=1, source_target_pairs={{0,1},{1,0},{2,3},{3,2},{4,5},{5,4},{6,7},{7,6},{8,9},{9,8},{10,11... | collective-permute-start | bytes 3538952 | tf_op jit(solution)/shard_map/ppermute | solution.py:735
  13.5 21.6 %collective-permute-start.7 = (bf16[576,768]{1,0:T(8,128)(2,1)S(1)}, bf16[576,768]{1,0:T(8,128)(2,1)S(1)}, u32[]{:S(2)}, u32[]{:S(2)}) collective-permute-start(bf16[576,768]{1,0:T(8,128)(2,1)S(1)} %get-tuple-element.107), channel_id=1, source_target_pairs={{0,2},{1,3},{2,0},{3,1},{4,6},{5,7},{6,4},{7,5},{8,10},{9,11},{10,... | collective-permute-start | bytes 2654216 | tf_op jit(solution)/shard_map/ppermute | solution.py:735
  15.2 19.1 %collective-permute-start.6 = (bf16[10,48,384]{2,1,0:T(8,128)(2,1)S(1)}, bf16[10,48,384]{2,1,0:T(8,128)(2,1)S(1)}, u32[]{:S(2)}, u32[]{:S(2)}) collective-permute-start(bf16[10,48,384]{2,1,0:T(8,128)(2,1)S(1)} %get-tuple-element.101.refs_0_.refs_7_), channel_id=1, source_target_pairs={{0,16},{1,17},{2,18},{3,19},{4,20},{5,21},{6,22},{7,23},{8,24},{9,... | collective-permute-start | bytes 1105928 | tf_op jit(solution)/shard_map/ppermute | solution.py:735
  17.8 16.5 %collective-permute-start.5 = (bf16[10,48,384]{2,1,0:T(8,128)(2,1)S(1)}, bf16[10,48,384]{2,1,0:T(8,128)(2,1)S(1)}, u32[]{:S(2)}, u32[]{:S(2)}) collective-permute-start(bf16[10,48,384]{2,1,0:T(8,128)(2,1)S(1)} %get-tuple-element.101.refs_0_.refs_7_), channel_id=1, source_target_pairs={{0,4},{1,5},{2,6},{3,7},{4,0},{5,1},{6,2},{7,3},{8,12},{9,13},{10,... | collective-permute-start | bytes 1105928 | tf_op jit(solution)/shard_map/ppermute | solution.py:735
  35.7 20.9 %collective-permute-start.13 = (bf16[576,768]{1,0:T(8,128)(2,1)S(1)}, bf16[576,768]{1,0:T(8,128)(2,1)S(1)}, u32[]{:S(2)}, u32[]{:S(2)}) collective-permute-start(bf16[576,768]{1,0:T(8,128)(2,1)S(1)} %get-tuple-element.113), channel_id=1, source_target_pairs={{0,2},{1,3},{2,0},{3,1},{4,6},{5,7},{6,4},{7,5},{8,10},{9,11},{10,... | collective-permute-start | bytes 2654216 | tf_op jit(solution)/shard_map/ppermute | solution.py:735
  37.6 11.5 %collective-permute-start.11 = (bf16[10,48,384]{2,1,0:T(8,128)(2,1)S(1)}, bf16[10,48,384]{2,1,0:T(8,128)(2,1)S(1)}, u32[]{:S(2)}, u32[]{:S(2)}) collective-permute-start(bf16[10,48,384]{2,1,0:T(8,128)(2,1)S(1)} %get-tuple-element.111), channel_id=1, source_target_pairs={{0,4},{1,5},{2,6},{3,7},{4,0},{5,1},{6,2},{7,3},{8,12},{9,13},{10,... | collective-permute-start | bytes 1105928 | tf_op jit(solution)/shard_map/ppermute | solution.py:735
  39.1 17.1 %collective-permute-start.10 = (bf16[20,48,384]{2,1,0:T(8,128)(2,1)S(1)}, bf16[20,48,384]{2,1,0:T(8,128)(2,1)S(1)}, u32[]{:S(2)}, u32[]{:S(2)}) collective-permute-start(bf16[20,48,384]{2,1,0:T(8,128)(2,1)S(1)} %get-tuple-element.108.refs_2_), channel_id=1, source_target_pairs={{0,8},{1,9},{2,10},{3,11},{4,12},{5,13},{6,14},{7,15},{8,0},{9,1},... | collective-permute-start | bytes 2211848 | tf_op jit(solution)/shard_map/ppermute | solution.py:735
  40.6 15.5 %collective-permute-start.8 = (bf16[20,48,384]{2,1,0:T(8,128)(2,1)S(1)}, bf16[20,48,384]{2,1,0:T(8,128)(2,1)S(1)}, u32[]{:S(2)}, u32[]{:S(2)}) collective-permute-start(bf16[20,48,384]{2,1,0:T(8,128)(2,1)S(1)} %get-tuple-element.108.refs_2_), channel_id=1, source_target_pairs={{0,1},{1,0},{2,3},{3,2},{4,5},{5,4},{6,7},{7,6},{8,9},{9,8},{10,11... | collective-permute-start | bytes 2211848 | tf_op jit(solution)/shard_map/ppermute | solution.py:735
  40.7 14.8 %collective-permute-start.12 = (bf16[256,768]{1,0:T(8,128)(2,1)S(1)}, bf16[256,768]{1,0:T(8,128)(2,1)S(1)}, u32[]{:S(2)}, u32[]{:S(2)}) collective-permute-start(bf16[256,768]{1,0:T(8,128)(2,1)S(1)} %get-tuple-element.112), channel_id=1, source_target_pairs={{0,4},{1,5},{2,6},{3,7},{4,0},{5,1},{6,2},{7,3},{8,12},{9,13},{10,... | collective-permute-start | bytes 1179656 | tf_op jit(solution)/shard_map/ppermute | solution.py:735
  57.9 20.6 %collective-permute-start.18 = (bf16[512,768]{1,0:T(8,128)(2,1)S(1)}, bf16[512,768]{1,0:T(8,128)(2,1)S(1)}, u32[]{:S(2)}, u32[]{:S(2)}) collective-permute-start(bf16[512,768]{1,0:T(8,128)(2,1)S(1)} %get-tuple-element.120), channel_id=1, source_target_pairs={{0,2},{1,3},{2,0},{3,1},{4,6},{5,7},{6,4},{7,5},{8,10},{9,11},{10,... | collective-permute-start | bytes 2359304 | tf_op jit(solution)/shard_map/ppermute | solution.py:735
  59.6 16.4 %collective-permute-start.15 = (bf16[20,48,384]{2,1,0:T(8,128)(2,1)S(1)}, bf16[20,48,384]{2,1,0:T(8,128)(2,1)S(1)}, u32[]{:S(2)}, u32[]{:S(2)}) collective-permute-start(bf16[20,48,384]{2,1,0:T(8,128)(2,1)S(1)} %get-tuple-element.117.refs_4_), channel_id=1, source_target_pairs={{0,1},{1,0},{2,3},{3,2},{4,5},{5,4},{6,7},{7,6},{8,9},{9,8},{10,11... | collective-permute-start | bytes 2211848 | tf_op jit(solution)/shard_map/ppermute | solution.py:735
  59.6 18.9 %collective-permute-start.19 = (bf16[20,48,384]{2,1,0:T(8,128)(2,1)S(1)}, bf16[20,48,384]{2,1,0:T(8,128)(2,1)S(1)}, u32[]{:S(2)}, u32[]{:S(2)}) collective-permute-start(bf16[20,48,384]{2,1,0:T(8,128)(2,1)S(1)} %get-tuple-element.117.refs_4_), channel_id=1, source_target_pairs={{0,4},{1,5},{2,6},{3,7},{4,0},{5,1},{6,2},{7,3},{8,12},{9,13},{10,... | collective-permute-start | bytes 2211848 | tf_op jit(solution)/shard_map/ppermute | solution.py:735
  61.1 16.4 %collective-permute-start.20 = (bf16[384,768]{1,0:T(8,128)(2,1)S(1)}, bf16[384,768]{1,0:T(8,128)(2,1)S(1)}, u32[]{:S(2)}, u32[]{:S(2)}) collective-permute-start(bf16[384,768]{1,0:T(8,128)(2,1)S(1)} %get-tuple-element.121.refs_6_), channel_id=1, source_target_pairs={{0,8},{1,9},{2,10},{3,11},{4,12},{5,13},{6,14},{7,15},{8,0},{9,1},... | collective-permute-start | bytes 1769480 | tf_op jit(solution)/shard_map/ppermute | solution.py:735
  62.7 14.8 %collective-permute-start.17 = (bf16[256,768]{1,0:T(8,128)(2,1)S(1)}, bf16[256,768]{1,0:T(8,128)(2,1)S(1)}, u32[]{:S(2)}, u32[]{:S(2)}) collective-permute-start(bf16[256,768]{1,0:T(8,128)(2,1)S(1)} %get-tuple-element.119.refs_3_.refs_6_), channel_id=1, source_target_pairs={{0,1},{1,0},{2,3},{3,2},{4,5},{5,4},{6,7},{7,6},{8,9},{9,8},{10,11... | collective-permute-start | bytes 1179656 | tf_op jit(solution)/shard_map/ppermute | solution.py:735
  105.3 13.3 %collective-permute-start.25 = (bf16[2,4,80,384]{3,2,1,0:T(8,128)(2,1)S(1)}, bf16[2,4,80,384]{3,2,1,0:T(8,128)(2,1)S(1)}, u32[]{:S(2)}, u32[]{:S(2)}) collective-permute-start(bf16[2,4,80,384]{3,2,1,0:T(8,128)(2,1)S(1)} %get-tuple-element.147), channel_id=1, source_target_pairs={{0,2},{1,3},{2,0},{3,1},{4,6},{5,7},{6,4},{7,5},{8,10},{9,11},{10,... | collective-permute-start | bytes 1474568 | tf_op jit(solution)/shard_map/ppermute | solution.py:735
  105.9 13.1 %collective-permute-start.26 = (bf16[2,4,80,384]{3,2,1,0:T(8,128)(2,1)S(1)}, bf16[2,4,80,384]{3,2,1,0:T(8,128)(2,1)S(1)}, u32[]{:S(2)}, u32[]{:S(2)}) collective-permute-start(bf16[2,4,80,384]{3,2,1,0:T(8,128)(2,1)S(1)} %get-tuple-element.149), channel_id=1, source_target_pairs={{0,4},{1,5},{2,6},{3,7},{4,0},{5,1},{6,2},{7,3},{8,12},{9,13},{10,... | collective-permute-start | bytes 1474568 | tf_op jit(solution)/shard_map/ppermute | solution.py:735
  119.4 7.0 %collective-permute-start.27 = (bf16[4,80,384]{2,1,0:T(8,128)(2,1)S(1)}, bf16[4,80,384]{2,1,0:T(8,128)(2,1)S(1)}, u32[]{:S(2)}, u32[]{:S(2)}) collective-permute-start(bf16[4,80,384]{2,1,0:T(8,128)(2,1)S(1)} %get-tuple-element.156), channel_id=1, source_target_pairs={{0,4},{1,5},{2,6},{3,7},{4,0},{5,1},{6,2},{7,3},{8,12},{9,13},{10,... | collective-permute-start | bytes 737288 | tf_op jit(solution)/shard_map/ppermute | solution.py:735
  120.9 6.7 %collective-permute-start.28 = (bf16[4,80,384]{2,1,0:T(8,128)(2,1)S(1)}, bf16[4,80,384]{2,1,0:T(8,128)(2,1)S(1)}, u32[]{:S(2)}, u32[]{:S(2)}) collective-permute-start(bf16[4,80,384]{2,1,0:T(8,128)(2,1)S(1)} %get-tuple-element.158), channel_id=1, source_target_pairs={{0,2},{1,3},{2,0},{3,1},{4,6},{5,7},{6,4},{7,5},{8,10},{9,11},{10,... | collective-permute-start | bytes 737288 | tf_op jit(solution)/shard_map/ppermute | solution.py:735
  127.8 11.7 %collective-permute-start.29 = (bf16[80,768]{1,0:T(8,128)(2,1)S(1)}, bf16[80,768]{1,0:T(8,128)(2,1)S(1)}, u32[]{:S(2)}, u32[]{:S(2)}) collective-permute-start(bf16[80,768]{1,0:T(8,128)(2,1)S(1)} %get-tuple-element.171), channel_id=1, source_target_pairs={{0,16},{1,17},{2,18},{3,19},{4,20},{5,21},{6,22},{7,23},{8,24},{9,... | collective-permute-start | bytes 368648 | tf_op jit(solution)/shard_map/ppermute | solution.py:735
  130.5 9.0 %collective-permute-start.30 = (bf16[80,768]{1,0:T(8,128)(2,1)S(1)}, bf16[80,768]{1,0:T(8,128)(2,1)S(1)}, u32[]{:S(2)}, u32[]{:S(2)}) collective-permute-start(bf16[80,768]{1,0:T(8,128)(2,1)S(1)} %get-tuple-element.172), channel_id=1, source_target_pairs={{0,24},{1,25},{2,26},{3,27},{4,28},{5,29},{6,30},{7,31},{8,16},{9,... | collective-permute-start | bytes 368648 | tf_op jit(solution)/shard_map/ppermute | solution.py:735
  131.6 7.9 %collective-permute-start.31 = (bf16[80,768]{1,0:T(8,128)(2,1)S(1)}, bf16[80,768]{1,0:T(8,128)(2,1)S(1)}, u32[]{:S(2)}, u32[]{:S(2)}) collective-permute-start(bf16[80,768]{1,0:T(8,128)(2,1)S(1)} %get-tuple-element.173), channel_id=1, source_target_pairs={{0,8},{1,9},{2,10},{3,11},{4,12},{5,13},{6,14},{7,15},{8,0},{9,1},... | collective-permute-start | bytes 368648 | tf_op jit(solution)/shard_map/ppermute | solution.py:735
  (25 other events, 132.2 us)
